TPU v7x, 256 devices: a whole 4x4x8 slice. The times are simulated.
256 devices in a mesh: feat: 32 (over y, z), tok: 8 (over x, core).
Axes of the slice: x: 4, y: 4, z: 8, core: 2. Of those that a mesh axis runs over, the one named last changes fastest.
Arguments:
- layer_input: bfloat16 [128, 8192], P(None, 'tok'), may hold values from -6 to 6
- enc_weight: bfloat16 [8192, 32768], P('tok', 'feat'), may hold values from -0.0625 to 0.0625
- enc_bias: float32 [32768], P('feat'), may hold values from -3 to 3
- active: int32 [512, 32768], P('tok', 'feat'), may hold values 0 or 1
- dec_weight: bfloat16 [32768, 8192], P('feat', 'tok'), may hold values from -0.03125 to 0.03125
- dec_bias: float32 [8192], P('tok'), may hold values from -3 to 3
- sae_error: bfloat16 [128, 8192], P(None, 'tok'), may hold values from -3 to 3
- positions: int32 [8, 16], P('tok'), may hold values from 0 to 123, as said below
- attn_gain: float32 [8192], P('tok'), may hold values from 0.1 to 1.9
- query_weight: bfloat16 [8192, 8192], P('tok', 'feat')
- kv_weight: bfloat16 [8192, 2048], P('tok', 'feat')
- out_weight: bfloat16 [8192, 8192], P('feat', 'tok'), may hold values from -0.0625 to 0.0625
- mlp_gain: float32 [8192], P('tok'), may hold values from 0.1 to 1.9
- gate_weight: bfloat16 [8192, 16384], P('tok', 'feat'), may hold values from -0.0625 to 0.0625
- up_weight: bfloat16 [8192, 16384], P('tok', 'feat'), may hold values from -0.0625 to 0.0625
- down_weight: bfloat16 [16384, 8192], P('feat', 'tok'), may hold values from -0.046875 to 0.046875
- cotangent: bfloat16 [128, 8192], P(None, 'tok'), may hold values from -6 to 6
Outputs:
- attribution: float32 [128, 32768], P('tok', 'feat')
Inputs may be any that keep to these rules, and one draw needn't show every extreme that they name: `positions`: positions rise strictly along each prompt.
All inputs are finite; a program needn't handle non-finite values. No bound on the sum of `active` on one device may be relied on, other than what follows from the above.
Results may differ from a plain program's by a relative error of at most 0.022.
Values may be sent and summed in bfloat16 or wider, within the bound.
No kernel may reach another device: no remote copies, remote signals or barrier semaphores. Data moves between devices by JAX's collectives and lax.ppermute only.
A program may use at most 64 MiB of HBM per device.

v0:
```python
import jax
import jax.numpy as jnp
from jax import lax
from jax.sharding import PartitionSpec as P

D = 8192
HEADS = 64
KV = 8
HD = 128
POINTS = 4
SEQ = 16


epsilon = 1e-05
rope_base = 500000.0


def expand_points(values):
    last_width = values.shape[1]
    spread_out = jnp.broadcast_to(
        values.reshape(-1, 1, SEQ, last_width), (values.shape[0] // SEQ, POINTS, SEQ, last_width)
    )
    return spread_out.reshape(-1, last_width)


def rotate_half(vectors, cosine_table, sine_table):
    half_width = vectors.shape[-1] // 2
    first_half = vectors[..., :half_width]
    second_half = vectors[..., half_width:]
    return jnp.concatenate(
        [
            first_half * cosine_table - second_half * sine_table,
            second_half * cosine_table + first_half * sine_table,
        ],
        axis=-1,
    )


def attend(query_rows, keyval_rows, position_rows, head_start):
    seq_count = query_rows.shape[0] // SEQ
    head_count = query_rows.shape[1] // HD
    queries = query_rows.reshape(seq_count, SEQ, head_count, HD)
    keys_all = keyval_rows[:, : KV * HD].reshape(seq_count, SEQ, KV, HD)
    values_all = keyval_rows[:, KV * HD :].reshape(seq_count, SEQ, KV, HD)
    owners = (head_start + jnp.arange(head_count, dtype=jnp.int32)) // (HEADS // KV)
    selector = (owners[:, None] == jnp.arange(KV, dtype=jnp.int32)[None, :]).astype(jnp.float32)
    key_heads = jnp.einsum("nskd,hk->nshd", keys_all, selector, precision=lax.Precision.HIGHEST)
    value_heads = jnp.einsum("nskd,hk->nshd", values_all, selector, precision=lax.Precision.HIGHEST)
    frequency = rope_base ** (-jnp.arange(HD // 2, dtype=jnp.float32) * 2.0 / HD)
    angles = position_rows.astype(jnp.float32).reshape(seq_count, SEQ, 1, 1) * frequency
    cosine_table = jnp.cos(angles)
    sine_table = jnp.sin(angles)
    queries = rotate_half(queries, cosine_table, sine_table)
    key_heads = rotate_half(key_heads, cosine_table, sine_table)
    scores = jnp.einsum(
        "nqhd,nkhd->nhqk", queries, key_heads, precision=lax.Precision.HIGHEST
    ) * HD ** (-0.5)
    positions_grid = position_rows.reshape(seq_count, SEQ)
    visible = positions_grid[:, None, :, None] >= positions_grid[:, None, None, :]
    scores = jnp.where(visible, scores, -1e30)
    highest = jnp.max(scores, axis=-1, keepdims=True)
    weights = jnp.exp(scores - highest)
    weights = weights / jnp.sum(weights, axis=-1, keepdims=True)
    mixed_values = jnp.einsum(
        "nhqk,nkhd->nqhd", weights, value_heads, precision=lax.Precision.HIGHEST
    )
    return mixed_values.reshape(seq_count * SEQ, head_count * HD)


def contract(left_side, right_side, transposed):
    if transposed:
        return lax.dot_general(
            left_side, right_side, (((1,), (1,)), ((), ())), preferred_element_type=jnp.float32
        )
    return jnp.dot(left_side, right_side, preferred_element_type=jnp.float32)


def token_sums(left_side, right_sides, transposed):
    share_rows = left_side.shape[0] // lax.axis_size("tok")

    def product_term(first_row, row_count):
        products = [contract(left_side, right_side, transposed) for right_side in right_sides]
        if len(products) > 1:
            return jnp.concatenate(products, axis=1)
        return products[0]

    return lax.psum_scatter(
        product_term(jnp.int32(0), share_rows * lax.axis_size("tok")),
        "tok",
        scatter_dimension=0,
        tiled=True,
    )


def token_rows(piece):
    return lax.all_gather(piece, "tok", axis=0, tiled=True)


def model_term(gathered, right_sides, transposed):

    def product_term(first_row, row_count):
        running = None
        column = 0
        for right_side in right_sides:
            span_width = right_side.shape[1] if transposed else right_side.shape[0]
            product = contract(gathered[:, column : column + span_width], right_side, transposed)
            running = product if running is None else running + product
            column = column + span_width
        return running

    return product_term


def feature_sums(product_term, share_rows):
    return lax.psum_scatter(
        product_term(jnp.int32(0), share_rows * lax.axis_size("feat")),
        "feat",
        scatter_dimension=0,
        tiled=True,
    )


def feature_rows(piece):
    return lax.all_gather(piece, "feat", axis=0, tiled=True)


def row_total(values):
    return lax.psum(jnp.sum(values, axis=1, keepdims=True), "tok")


def model_space(piece, right_sides, share_rows):
    product_term = model_term(token_rows(piece), right_sides, False)
    return feature_sums(product_term, share_rows)


def replicated(piece):
    return feature_rows(piece)


def local(
    layer_input,
    enc_weight,
    enc_bias,
    active,
    dec_weight,
    dec_bias,
    sae_error,
    positions,
    attn_gain,
    query_weight,
    kv_weight,
    out_weight,
    mlp_gain,
    gate_weight,
    up_weight,
    down_weight,
    cotangent,
):
    feat_index = lax.axis_index("feat")
    own_rows = POINTS * (layer_input.shape[0] // lax.axis_size("tok"))
    whole_rows = own_rows * lax.axis_size("tok")
    share_rows = whole_rows // lax.axis_size("feat")
    feature_width = enc_weight.shape[1]
    hidden_width = gate_weight.shape[1]
    head_width = query_weight.shape[1]
    alphas = jnp.arange(1, POINTS + 1, dtype=jnp.float32) / POINTS
    encoded = token_sums(layer_input, (enc_weight,), False)
    pre_active = alphas[None, :, None, None] * encoded.reshape(-1, 1, SEQ, feature_width) + enc_bias
    features = active.reshape(-1, POINTS, SEQ, feature_width).astype(jnp.float32) * pre_active
    sent_features = features.reshape(own_rows, feature_width).astype(jnp.bfloat16)
    decoded = model_space(sent_features, (dec_weight,), share_rows)
    first_row = feat_index * share_rows
    error_rows = lax.dynamic_slice_in_dim(expand_points(sae_error), first_row, decoded.shape[0], 0)
    hidden_in = decoded + dec_bias + error_rows.astype(jnp.float32)
    scale_first = lax.rsqrt(row_total(hidden_in * hidden_in) / D + epsilon)
    normed_first = (hidden_in * scale_first * attn_gain).astype(jnp.bfloat16)
    projections = token_sums(replicated(normed_first), (query_weight, kv_weight), False)
    query_rows = projections[:, :head_width]
    kv_local = projections[:, head_width:].astype(jnp.bfloat16)
    keyval_rows = lax.all_gather(kv_local, "feat", axis=1, tiled=True).astype(jnp.float32)
    position_rows = jnp.broadcast_to(
        positions.reshape(-1, 1, SEQ), (positions.shape[0], POINTS, SEQ)
    ).reshape(-1)
    head_start = feat_index * (head_width // HD)
    attended, pullback = jax.vjp(
        lambda left_value, right_value: attend(left_value, right_value, position_rows, head_start),
        query_rows,
        keyval_rows,
    )
    projected = model_space(attended.astype(jnp.bfloat16), (out_weight,), share_rows)
    middle = hidden_in + projected
    scale_second = lax.rsqrt(row_total(middle * middle) / D + epsilon)
    normed_second = (middle * scale_second * mlp_gain).astype(jnp.bfloat16)
    gate_up = token_sums(replicated(normed_second), (gate_weight, up_weight), False)
    gate_value = gate_up[:, :hidden_width]
    up_value = gate_up[:, hidden_width:]
    back_hidden = token_sums(cotangent, (down_weight,), True)
    back_hidden = jnp.broadcast_to(
        back_hidden.reshape(-1, 1, SEQ, hidden_width),
        (back_hidden.shape[0] // SEQ, POINTS, SEQ, hidden_width),
    ).reshape(own_rows, hidden_width)
    sigmoid_gate = jax.nn.sigmoid(gate_value)
    grad_gate = back_hidden * up_value * sigmoid_gate * (1.0 + gate_value * (1.0 - sigmoid_gate))
    grad_up = back_hidden * gate_value * sigmoid_gate
    mlp_grads = jnp.concatenate([grad_gate, grad_up], axis=1).astype(jnp.bfloat16)
    back_second = feature_sums(
        model_term(token_rows(mlp_grads), (gate_weight, up_weight), True), share_rows
    )
    cot_rows = lax.dynamic_slice_in_dim(
        expand_points(cotangent), feat_index * share_rows, share_rows, 0
    ).astype(jnp.float32)
    weighted_second = back_second * mlp_gain
    grad_middle = (
        cot_rows
        + scale_second * weighted_second
        - middle * scale_second**3 * (row_total(weighted_second * middle) / D)
    )
    grad_attended = token_sums(feature_rows(grad_middle.astype(jnp.bfloat16)), (out_weight,), True)
    grad_query, grad_keyval = pullback(grad_attended)
    grad_kv_local = lax.psum_scatter(grad_keyval, "feat", scatter_dimension=1, tiled=True)
    attn_grads = jnp.concatenate([grad_query, grad_kv_local], axis=1).astype(jnp.bfloat16)
    back_first = feature_sums(
        model_term(token_rows(attn_grads), (query_weight, kv_weight), True), share_rows
    )
    weighted_first = back_first * attn_gain
    grad_hidden = (
        grad_middle
        + scale_first * weighted_first
        - hidden_in * scale_first**3 * (row_total(weighted_first * hidden_in) / D)
    )
    feature_grads = token_sums(feature_rows(grad_hidden.astype(jnp.bfloat16)), (dec_weight,), True)
    grads_grid = feature_grads.reshape(-1, POINTS, SEQ, feature_width)
    previous = jnp.concatenate([jnp.zeros_like(features[:, :1]), features[:, :-1]], axis=1)
    return jnp.sum(grads_grid * (features - previous), axis=1).reshape(-1, feature_width)


def solution(mesh):
    in_specs = (
        P(None, "tok"),
        P("tok", "feat"),
        P("feat"),
        P("tok", "feat"),
        P("feat", "tok"),
        P("tok"),
        P(None, "tok"),
        P("tok", None),
        P("tok"),
        P("tok", "feat"),
        P("tok", "feat"),
        P("feat", "tok"),
        P("tok"),
        P("tok", "feat"),
        P("tok", "feat"),
        P("feat", "tok"),
        P(None, "tok"),
    )
    out_specs = P("tok", "feat")
    return jax.shard_map(local, mesh=mesh, in_specs=in_specs, out_specs=out_specs, check_vma=False)
```

profile of v0, /device:TPU:1, one launch (start us, length us, event | category | flops | bytes accessed | tf_op | source)
XLA Modules:
  0.0 1828.6 jit_solution(11662826388875026040)
XLA Ops:
  6.5 3.1 fusion.71
  10.4 34.3 %reduce-scatter.18.cloned.1.call-done = f32[16,1024]{1,0:T(8,128)} async-done(((f32[128,1024]{1,0:T(8,128)}), f32[16,1024]{1,0:T(8,128)}) %reduce-scatter.18.cloned.1.call-update) | async-done | bytes 65552 | tf_op jit(solution)/shard_map/reduce_scatter | solution.py:87
  44.8 1.6 fusion.8
  46.4 27.9 %all-gather.7.cloned.1.call-done = bf16[512,1024]{1,0:T(8,128)(2,1)} async-done(((bf16[64,1024]{1,0:T(8,128)(2,1)}), bf16[512,1024]{1,0:T(8,128)(2,1)}) %all-gather.7.cloned.1.call-update) | async-done | bytes 1048592 | tf_op jit(solution)/shard_map/all_gather | solution.py:96
  74.3 3.8 fusion.72
  78.3 211.1 %reduce-scatter.20.cloned.1.call-done = f32[16,1024]{1,0:T(8,128)} async-done(((f32[512,1024]{1,0:T(8,128)}), f32[16,1024]{1,0:T(8,128)}) %reduce-scatter.20.cloned.1.call-update) | async-done | bytes 65552 | tf_op jit(solution)/shard_map/reduce_scatter | solution.py:115
  289.5 1.0 multiply_reduce_fusion.5
  290.5 17.7 psum.28
  309.5 67.9 %all-gather.9.cloned.1.call-done = bf16[512,1024]{1,0:T(8,128)(2,1)} async-done(((bf16[16,1024]{1,0:T(8,128)(2,1)}), bf16[512,1024]{1,0:T(8,128)(2,1)}) %all-gather.9.cloned.1.call-update) | async-done | bytes 1048592 | tf_op jit(solution)/shard_map/all_gather | solution.py:124
  377.4 1.8 fusion.73
  379.7 1.2 copy.75
  381.9 32.7 %reduce-scatter.34.cloned.1.call-done = f32[64,320]{1,0:T(8,128)} async-done(((f32[512,320]{1,0:T(8,128)}), f32[64,320]{1,0:T(8,128)}) %reduce-scatter.34.cloned.1.call-update) | async-done | bytes 81936
  415.4 38.6 %all_gather.29 = bf16[64,2048]{0,1:T(8,128)(2,1)S(1)} all-gather(bf16[64,64]{0,1:T(8,128)(2,1)S(1)} %copy.81), channel_id=1, replica_groups=mesh['feat'=32,'tok'=8] {'feat'}, dimensions={1}, use_global_device_ids=true | all-gather | bytes 270336 | tf_op jit(solution)/shard_map/all_gather | solution.py:180
  454.9 1.1 copy.53
  457.6 1.1 convolution_bitcast_fusion
  458.7 1.0 multiply_subtract_fusion.2
  461.4 1.2 convert_reduce_fusion
  462.7 1.7 copy.51
  464.4 0.9 copy.83
  466.2 1.1 fusion.1
  467.4 27.6 %all_gather.30 = bf16[512,256]{1,0:T(8,128)(2,1)S(1)} all-gather(bf16[64,256]{1,0:T(8,128)(2,1)S(1)} %bitcast.167), channel_id=1, replica_groups=mesh['feat'=32,'tok'=8] {'tok'}, dimensions={0}, use_global_device_ids=true | all-gather | bytes 294912 | tf_op jit(solution)/shard_map/all_gather | solution.py:96
  495.0 1.8 fusion.75
  496.8 207.5 %reduce-scatter.22.cloned.1.call-done = f32[16,1024]{1,0:T(8,128)} async-done(((f32[512,1024]{1,0:T(8,128)}), f32[16,1024]{1,0:T(8,128)}) %reduce-scatter.22.cloned.1.call-update) | async-done | bytes 65552 | tf_op jit(solution)/shard_map/reduce_scatter | solution.py:115
  704.3 2.1 multiply_reduce_fusion.4
  706.4 18.2 psum.29
  724.7 1.2 fusion.54
  726.4 1.5 multiply_convert_fusion
  728.0 2.5 fusion.76
  730.6 65.3 %all-gather.11.cloned.1.call-done = bf16[512,1024]{1,0:T(8,128)(2,1)} async-done(((bf16[16,1024]{1,0:T(8,128)(2,1)}), bf16[512,1024]{1,0:T(8,128)(2,1)}) %all-gather.11.cloned.1.call-update) | async-done | bytes 1048592 | tf_op jit(solution)/shard_map/all_gather | solution.py:124
  795.9 2.4 fusion.77
  799.1 1.5 pad_maximum_fusion
  800.6 2.9 copy.77
  803.6 27.6 %reduce-scatter.24.cloned.1.call-done = f32[16,512]{1,0:T(8,128)} async-done(((f32[128,512]{1,0:T(8,128)}), f32[16,512]{1,0:T(8,128)}) %reduce-scatter.24.cloned.1.call-update) | async-done | bytes 32784 | tf_op jit(solution)/shard_map/reduce_scatter | solution.py:87
  831.2 37.5 %reduce-scatter.36.cloned.1.call-done = f32[64,1024]{1,0:T(8,128)} async-done(((f32[512,1024]{1,0:T(8,128)}), f32[64,1024]{1,0:T(8,128)}) %reduce-scatter.36.cloned.1.call-update) | async-done | bytes 262160 | tf_op jit(solution)/shard_map/reduce_scatter | solution.py:87
  868.7 1.0 fusion.11
  870.5 27.8 %all-gather.13.cloned.1.call-done = bf16[512,1024]{1,0:T(8,128)(2,1)} async-done(((bf16[64,1024]{1,0:T(8,128)(2,1)}), bf16[512,1024]{1,0:T(8,128)(2,1)}) %all-gather.13.cloned.1.call-update) | async-done | bytes 1048592 | tf_op jit(solution)/shard_map/all_gather | solution.py:96
  898.3 2.3 fusion.3
  900.6 2.1 convolution_add_fusion.1
  902.7 210.9 %reduce-scatter.26.cloned.1.call-done = f32[16,1024]{1,0:T(8,128)} async-done(((f32[512,1024]{1,0:T(8,128)}), f32[16,1024]{1,0:T(8,128)}) %reduce-scatter.26.cloned.1.call-update) | async-done | bytes 65552 | tf_op jit(solution)/shard_map/reduce_scatter | solution.py:115
  1113.6 1.5 multiply_reduce_fusion.3
  1115.1 18.2 psum.30
  1134.0 1.1 broadcast_in_dim.75
  1135.1 1.6 fusion.68
  1136.8 68.0 %all-gather.15.cloned.1.call-done = bf16[512,1024]{1,0:T(8,128)(2,1)} async-done(((bf16[16,1024]{1,0:T(8,128)(2,1)}), bf16[512,1024]{1,0:T(8,128)(2,1)}) %all-gather.15.cloned.1.call-update) | async-done | bytes 1048592 | tf_op jit(solution)/shard_map/all_gather | solution.py:124
  1204.8 2.5 fusion.79
  1208.2 32.4 %reduce-scatter.28.cloned.1.call-done = f32[64,256]{1,0:T(8,128)} async-done(((f32[512,256]{1,0:T(8,128)}), f32[64,256]{1,0:T(8,128)}) %reduce-scatter.28.cloned.1.call-update) | async-done | bytes 65552 | tf_op jit(solution)/shard_map/reduce_scatter | solution.py:87
  1241.5 1.1 multiply_reduce_fusion.2
  1244.0 1.1 fusion.37
  1245.1 1.2 fusion.34
  1246.2 1.0 fusion.23
  1249.2 1.3 copy.79
  1250.6 1.0 add_convert_fusion
  1251.6 209.4 %reduce-scatter.38.cloned.1.call-done = f32[64,64]{1,0:T(8,128)} async-done(((f32[2048,64]{1,0:T(8,128)}), f32[64,64]{1,0:T(8,128)}) %reduce-scatter.38.cloned.1.call-update) | async-done | bytes 16400
  1461.9 19.0 %all_gather.34 = bf16[512,320]{1,0:T(8,128)(2,1)S(1)} all-gather(bf16[64,320]{1,0:T(8,128)(2,1)S(1)} %pad_maximum_fusion.5), channel_id=1, replica_groups=mesh['feat'=32,'tok'=8] {'tok'}, dimensions={0}, use_global_device_ids=true | all-gather | bytes 368640 | tf_op jit(solution)/shard_map/all_gather | solution.py:96
  1480.9 1.3 fusion.16
  1482.2 1.8 convolution_add_fusion
  1484.1 208.4 %reduce-scatter.30.cloned.1.call-done = f32[16,1024]{1,0:T(8,128)} async-done(((f32[512,1024]{1,0:T(8,128)}), f32[16,1024]{1,0:T(8,128)}) %reduce-scatter.30.cloned.1.call-update) | async-done | bytes 65552 | tf_op jit(solution)/shard_map/reduce_scatter | solution.py:115
  1692.5 1.0 multiply_reduce_fusion.1
  1693.5 17.7 psum.31
  1711.2 1.5 subtract_convert_fusion
  1712.8 67.9 %all-gather.17.cloned.1.call-done = bf16[512,1024]{1,0:T(8,128)(2,1)} async-done(((bf16[16,1024]{1,0:T(8,128)(2,1)}), bf16[512,1024]{1,0:T(8,128)(2,1)}) %all-gather.17.cloned.1.call-update) | async-done | bytes 1048592 | tf_op jit(solution)/shard_map/all_gather | solution.py:124
  1780.7 3.8 fusion.80
  1785.5 34.8 %reduce-scatter.32.cloned.1.call-done = f32[64,1024]{1,0:T(8,128)} async-done(((f32[512,1024]{1,0:T(8,128)}), f32[64,1024]{1,0:T(8,128)}) %reduce-scatter.32.cloned.1.call-update) | async-done | bytes 262160 | tf_op jit(solution)/shard_map/reduce_scatter | solution.py:87
  1820.4 1.7 multiply_reduce_fusion
  (158 shorter events, 19.6 us)
Async XLA Ops:
  6.5 67.8 %copy-start = (bf16[1024,1024]{1,0:T(8,128)(2,1)S(1)}, bf16[1024,1024]{1,0:T(8,128)(2,1)}, u32[]{:S(2)}) copy-start(bf16[1024,1024]{1,0:T(8,128)(2,1)} %param.21) | copy-start | bytes 6291460
  6.5 38.2 %copy-start.23 = (f32[1024]{0:T(1024)S(1)}, f32[1024]{0:T(1024)}, u32[]{:S(2)}) copy-start(f32[1024]{0:T(1024)} %param.19) | copy-start | bytes 12292
  6.5 38.2 %copy-start.2 = (s32[64,1024]{1,0:T(8,128)S(1)}, s32[64,1024]{1,0:T(8,128)}, u32[]{:S(2)}) copy-start(s32[64,1024]{1,0:T(8,128)} %param.20) | copy-start | bytes 786436
  6.5 38.2 %reduce-scatter.18.cloned.1.call-start = ((), (), s32[]{:S(2)}) async-start(), calls=%async_computation.11 | async-start | bytes 589824 | tf_op jit(solution)/shard_map/reduce_scatter | solution.py:87
  9.6 64.7 %all-gather.7.cloned.1.call-start = ((), (), s32[]{:S(2)}) async-start(), calls=%async_computation.12 | async-start | bytes 1179648 | tf_op jit(solution)/shard_map/all_gather | solution.py:96
  9.7 0.6 copy-start.29
  46.4 243.0 %reduce-scatter.20.cloned.1.call-start = ((), (), s32[]{:S(2)}) async-start(), calls=%async_computation.13 | async-start | bytes 2162688 | tf_op jit(solution)/shard_map/reduce_scatter | solution.py:115
  78.2 211.2 %copy-start.17 = (bf16[128,1024]{1,0:T(8,128)(2,1)S(1)}, bf16[128,1024]{1,0:T(8,128)(2,1)}, u32[]{:S(2)}) copy-start(bf16[128,1024]{1,0:T(8,128)(2,1)} %param.23) | copy-start | bytes 786436
  78.2 211.3 %copy-start.31 = (f32[1024]{0:T(1024)S(1)}, f32[1024]{0:T(1024)}, u32[]{:S(2)}) copy-start(f32[1024]{0:T(1024)} %param.22) | copy-start | bytes 12292
  78.2 230.5 %copy-start.25 = (f32[1024]{0:T(1024)S(1)}, f32[1024]{0:T(1024)}, u32[]{:S(2)}) copy-start(f32[1024]{0:T(1024)} %param.25) | copy-start | bytes 12292
  78.2 299.2 %copy-start.3 = (bf16[1024,256]{1,0:T(8,128)(2,1)S(1)}, bf16[1024,256]{1,0:T(8,128)(2,1)}, u32[]{:S(2)}) copy-start(bf16[1024,256]{1,0:T(8,128)(2,1)} %param.26) | copy-start | bytes 1572868
  78.2 301.0 %copy-start.14 = (bf16[1024,64]{0,1:T(8,128)(2,1)S(1)}, bf16[1024,64]{0,1:T(8,128)(2,1)}, u32[]{:S(2)}) copy-start(bf16[1024,64]{0,1:T(8,128)(2,1)} %param.27) | copy-start | bytes 393220
  78.2 299.2 %all-gather.9.cloned.1.call-start = ((), (), s32[]{:S(2)}) async-start(), calls=%async_computation.14 | async-start | bytes 1081344 | tf_op jit(solution)/shard_map/all_gather | solution.py:124
  290.5 88.7 %copy-start.5 = (f32[16,1024]{1,0:T(8,128)}, f32[16,1024]{1,0:T(8,128)S(1)}, u32[]{:S(2)}) copy-start(f32[16,1024]{1,0:T(8,128)S(1)} %get-tuple-element.14) | copy-start | bytes 196612
  308.7 70.5 %copy-start.32 = (f32[16]{0:T(128)}, f32[16]{0:T(128)S(1)}, u32[]{:S(2)}) copy-start(f32[16]{0:T(128)S(1)} %get-tuple-element.35) | copy-start | bytes 196
  309.4 105.2 %reduce-scatter.34.cloned.1.call-start = ((), (), s32[]{:S(2)}) async-start(), calls=%async_computation.25 | async-start | bytes 884736
  377.4 1.8 copy-start.1
  379.7 1.3 copy-start.35
  380.9 323.4 %reduce-scatter.22.cloned.1.call-start = ((), (), s32[]{:S(2)}) async-start(), calls=%async_computation.15 | async-start | bytes 2162688 | tf_op jit(solution)/shard_map/reduce_scatter | solution.py:115
  381.0 79.8 %copy-start.27 = (s32[2]{0:T(128)}, s32[2]{0:T(128)S(1)}, u32[]{:S(2)}) copy-start(s32[2]{0:T(128)S(1)} %and_select_fusion) | copy-start | bytes 28
  381.1 79.7 %copy-start.20 = (pred[4,16,16]{1,2,0:T(8,128)(4,1)}, pred[4,16,16]{1,2,0:T(8,128)(4,1)S(1)}, u32[]{:S(2)}) copy-start(pred[4,16,16]{1,2,0:T(8,128)(4,1)S(1)} %broadcast_compare_fusion.1) | copy-start | bytes 3076
  454.9 40.0 %copy-start.4 = (bf16[256,1024]{1,0:T(8,128)(2,1)S(1)}, bf16[256,1024]{1,0:T(8,128)(2,1)}, u32[]{:S(2)}) copy-start(bf16[256,1024]{1,0:T(8,128)(2,1)} %param.28) | copy-start | bytes 1572868
  460.0 0.6 copy-start.11
  460.0 7.4 copy-start.10
  460.8 0.6 copy-start.21
  461.4 1.2 copy-start.22
  466.2 1.2 copy-start.12
  495.0 209.4 %copy-start.6 = (f32[16,1024]{1,0:T(8,128)S(1)}, f32[16,1024]{1,0:T(8,128)}, u32[]{:S(2)}) copy-start(f32[16,1024]{1,0:T(8,128)} %copy-done.5) | copy-start | bytes 196612
  496.8 299.2 %all-gather.11.cloned.1.call-start = ((), (), s32[]{:S(2)}) async-start(), calls=%async_computation.17 | async-start | bytes 1081344 | tf_op jit(solution)/shard_map/all_gather | solution.py:124
  725.8 0.6 copy-start.34
  727.9 103.3 %reduce-scatter.24.cloned.1.call-start = ((), (), s32[]{:S(2)}) async-start(), calls=%async_computation.16 | async-start | bytes 294912 | tf_op jit(solution)/shard_map/reduce_scatter | solution.py:87
  730.5 138.2 %reduce-scatter.36.cloned.1.call-start = ((), (), s32[]{:S(2)}) async-start(), calls=%async_computation.26 | async-start | bytes 2359296 | tf_op jit(solution)/shard_map/reduce_scatter | solution.py:87
  795.9 2.5 copy-start.7
  795.9 2.5 copy-start.37
  803.6 94.7 %all-gather.13.cloned.1.call-start = ((), (), s32[]{:S(2)}) async-start(), calls=%async_computation.18 | async-start | bytes 1179648 | tf_op jit(solution)/shard_map/all_gather | solution.py:96
  870.5 243.1 %reduce-scatter.26.cloned.1.call-start = ((), (), s32[]{:S(2)}) async-start(), calls=%async_computation.19 | async-start | bytes 2162688 | tf_op jit(solution)/shard_map/reduce_scatter | solution.py:115
  898.3 2.3 copy-start.8
  898.3 2.3 copy-start.9
  902.7 302.1 %all-gather.15.cloned.1.call-start = ((), (), s32[]{:S(2)}) async-start(), calls=%async_computation.20 | async-start | bytes 1081344 | tf_op jit(solution)/shard_map/all_gather | solution.py:124
  1136.7 103.9 %reduce-scatter.28.cloned.1.call-start = ((), (), s32[]{:S(2)}) async-start(), calls=%async_computation.21 | async-start | bytes 589824 | tf_op jit(solution)/shard_map/reduce_scatter | solution.py:87
  1207.3 40.1 %copy-start.28 = (s32[2]{0:T(128)S(1)}, s32[2]{0:T(128)}, u32[]{:S(2)}) copy-start(s32[2]{0:T(128)} %copy-done.27) | copy-start | bytes 28
  1207.3 40.6 %copy-start.15 = (f32[4,16,64]{2,1,0:T(8,128)S(1)}, f32[4,16,64]{2,1,0:T(8,128)}, u32[]{:S(2)}) copy-start(f32[4,16,64]{2,1,0:T(8,128)} %get-tuple-element.32) | copy-start | bytes 49156
  1207.3 40.6 %copy-start.16 = (f32[4,16,64]{2,1,0:T(8,128)S(1)}, f32[4,16,64]{2,1,0:T(8,128)}, u32[]{:S(2)}) copy-start(f32[4,16,64]{2,1,0:T(8,128)} %get-tuple-element.33) | copy-start | bytes 49156
  1207.3 253.7 %reduce-scatter.38.cloned.1.call-start = ((), (), s32[]{:S(2)}) async-start(), calls=%async_computation.27 | async-start | bytes 1081344
  1249.1 1.5 copy-start.18
  1250.6 442.0 %reduce-scatter.30.cloned.1.call-start = ((), (), s32[]{:S(2)}) async-start(), calls=%async_computation.22 | async-start | bytes 2162688 | tf_op jit(solution)/shard_map/reduce_scatter | solution.py:115
  1484.0 208.5 %copy-start.26 = (f32[1024]{0:T(1024)S(1)}, f32[1024]{0:T(1024)}, u32[]{:S(2)}) copy-start(f32[1024]{0:T(1024)} %param.25) | copy-start | bytes 12292
  1484.0 227.2 %copy-start.19 = (f32[16,1024]{1,0:T(8,128)S(1)}, f32[16,1024]{1,0:T(8,128)}, u32[]{:S(2)}) copy-start(f32[16,1024]{1,0:T(8,128)} %get-tuple-element.10) | copy-start | bytes 196612
  1484.0 227.2 %copy-start.33 = (f32[16]{0:T(128)S(1)}, f32[16]{0:T(128)}, u32[]{:S(2)}) copy-start(f32[16]{0:T(128)} %copy-done.32) | copy-start | bytes 196
  1484.0 227.2 %copy-start.36 = (f32[16]{0:T(128)S(1)}, f32[16]{0:T(128)}, u32[]{:S(2)}) copy-start(f32[16]{0:T(128)} %get-tuple-element.34) | copy-start | bytes 196
  1484.0 296.7 %all-gather.17.cloned.1.call-start = ((), (), s32[]{:S(2)}) async-start(), calls=%async_computation.23 | async-start | bytes 1081344 | tf_op jit(solution)/shard_map/all_gather | solution.py:124
  1712.7 107.6 %reduce-scatter.32.cloned.1.call-start = ((), (), s32[]{:S(2)}) async-start(), calls=%async_computation.24 | async-start | bytes 2359296 | tf_op jit(solution)/shard_map/reduce_scatter | solution.py:87
  1784.6 0.8 copy-start.13
  1784.6 0.8 copy-start.24
  1784.6 0.8 copy-start.30
Sparse Core Ops, SparseCore 0:
  9.9 34.8 reduce-scatter.17
  46.8 27.5 all-gather.6
  78.7 210.6 reduce-scatter.19
  309.5 67.7 all-gather.8
  381.0 33.5 reduce-scatter.33
  496.9 207.4 reduce-scatter.21
  728.1 67.8 all-gather.10
  798.4 32.7 reduce-scatter.23
  833.9 34.7 reduce-scatter.35
  870.6 27.6 all-gather.12
  902.8 210.7 reduce-scatter.25
  1136.8 67.8 all-gather.14
  1207.4 33.1 reduce-scatter.27
  1250.7 210.2 reduce-scatter.37
  1484.2 208.3 reduce-scatter.29
  1712.9 67.8 all-gather.16
  1784.7 35.6 reduce-scatter.31
where the time goes:
time: 1830 us
  waiting for transfers between devices  1570 us (86%)
  blocking collectives  157 us (9%)
  matrix products  38.9 us (2%)
  other arithmetic  27.2 us (1%)
  local copies, waits for them, and re-layouts  18.9 us (1%)
    reduce_scatter x4, waiting for transfers between devices, feature_sums(): lax.psum_scatter(product_term(jnp.int32(0), share_rows * lax.axis_size('f...  838 us
    all_gather x4, waiting for transfers between devices, feature_rows(): return lax.all_gather(piece, 'feat', axis=0, tiled=True)  269 us
    unnamed x19, waiting for transfers between devices  242 us
    reduce_scatter x5, waiting for transfers between devices, token_sums(): lax.psum_scatter(product_term(jnp.int32(0), share_rows * lax.axis_size('t...  167 us
    psum x4, blocking collectives, row_total(): return lax.psum(jnp.sum(values, axis=1, keepdims=True), 'tok')  71.8 us
    all_gather x2, waiting for transfers between devices, token_rows(): return lax.all_gather(piece, 'tok', axis=0, tiled=True)  55.7 us
    all_gather x2, blocking collectives, token_rows(): return lax.all_gather(piece, 'tok', axis=0, tiled=True)  46.6 us
    all_gather x1, blocking collectives, local(): lax.all_gather(kv_local, 'feat', axis=1, tiled=True).astype(jnp.float32)  38.6 us
  transfers between devices with their start and end apart: 17, of which 17 were waited for; matrix products, arithmetic and copies ran while one was open for 1% of the time, Pallas kernels for 0%

commit v1 on v0

v1 whole, which is shorter than its diff:
```python
import jax
import jax.numpy as jnp
import numpy as np
from jax import lax
from jax.sharding import Mesh
from jax.sharding import PartitionSpec as P

D = 8192
HEADS = 64
KV = 8
HD = 128
POINTS = 4
SEQ = 16
NY, NZ, NX, NC = 4, 8, 4, 2
FEAT = ("y", "z")
TOK = ("x", "c")

epsilon = 1e-05
rope_base = 500000.0
F32 = jnp.float32
B16 = jnp.bfloat16


def dot(left_side, right_side):
    return jnp.dot(left_side, right_side, preferred_element_type=F32)


def dot_t(left_side, right_side):
    return lax.dot_general(
        left_side, right_side, (((1,), (1,)), ((), ())), preferred_element_type=F32
    )


def swap(blocks, axes):
    return lax.all_to_all(blocks, axes, 0, 0, tiled=True)


def spread(piece, axes, count):
    blocks = jnp.broadcast_to(piece[None], (count,) + piece.shape)
    return swap(lax.optimization_barrier(blocks), axes).reshape((-1,) + piece.shape[1:])


def added(blocks):
    return jnp.sum(blocks.astype(F32), axis=0)


def feat_sums(partial):
    rows, width = partial.shape
    blocks = swap(partial.astype(B16).reshape(NY, rows // NY, width), "y")
    blocks = added(blocks).astype(B16).reshape(NZ, rows // (NY * NZ), width)
    return added(swap(blocks, "z"))


def feat_rows(piece):
    return spread(spread(piece, "z", NZ), "y", NY)


def tok_sums(partial):
    rows, width = partial.shape
    return added(swap(partial.astype(B16).reshape(NX * NC, rows // (NX * NC), width), TOK))


def other_core(values):
    return lax.ppermute(values, "c", [(0, 1), (1, 0)])


def tok_sums_wide(partial, core):
    rows, width = partial.shape
    blocks = partial.reshape(NX, NC, rows // (NX * NC), width)
    own = lax.dynamic_index_in_dim(blocks, core, 1, keepdims=False)
    other = lax.dynamic_index_in_dim(blocks, 1 - core, 1, keepdims=False)
    own = own + other_core(other.astype(B16)).astype(F32)
    return added(swap(own.astype(B16), "x"))


def tok_rows(piece):
    return spread(piece, TOK, NX * NC)


def tok_rows_wide(piece, core):
    own = spread(piece, "x", NX).reshape((NX,) + piece.shape)
    other = other_core(own)
    first = jnp.where(core == 0, own, other)
    second = jnp.where(core == 0, other, own)
    return jnp.stack([first, second], axis=1).reshape((-1,) + piece.shape[1:])


def split_column(values):
    high = lax.reduce_precision(values, 8, 7)
    low = values - high
    lanes = lax.broadcasted_iota(jnp.int32, (values.shape[0], 128), 1)
    return jnp.where(lanes == 0, high, jnp.where(lanes == 1, low, 0.0)).astype(B16)


def joined_column(block):
    return block[:, 0:1].astype(F32) + block[:, 1:2].astype(F32)


def row_total(values):
    partial = jnp.sum(values, axis=1, keepdims=True)
    rows = partial.shape[0]
    block = jnp.broadcast_to(partial.reshape(1, 1, rows), (NX * NC, 1, rows))
    parts = swap(lax.optimization_barrier(block), TOK)
    return jnp.sum(parts, axis=0).reshape(rows, 1)


def rotate(vectors, cosine, sine):
    half = vectors.shape[-1] // 2
    first, second = vectors[:, :half], vectors[:, half:]
    return jnp.concatenate(
        [first * cosine - second * sine, second * cosine + first * sine], axis=-1
    )


def attend(query_rows, keyval_rows, cosine, sine, visible):
    high = lax.Precision.HIGHEST
    heads = query_rows.shape[1] // HD
    keys = rotate(keyval_rows[:, :HD], cosine, sine)
    values = keyval_rows[:, HD:]
    queries = jnp.concatenate(
        [rotate(query_rows[:, h * HD : (h + 1) * HD], cosine, sine) for h in range(heads)], axis=0
    )
    scores = lax.dot_general(
        queries, keys, (((1,), (1,)), ((), ())), precision=high, preferred_element_type=F32
    ) * HD ** (-0.5)
    scores = jnp.where(visible, scores, -1e30)
    weights = jnp.exp(scores - jnp.max(scores, axis=-1, keepdims=True))
    weights = weights / jnp.sum(weights, axis=-1, keepdims=True)
    mixed = jnp.dot(weights, values, precision=high, preferred_element_type=F32)
    rows = query_rows.shape[0]
    return jnp.concatenate([mixed[h * rows : (h + 1) * rows] for h in range(heads)], axis=1)


def own_keyval_weight(kv_weight):
    feat = lax.axis_index(FEAT)
    group = lax.rem(feat, 4)
    parts = []
    for shift in range(4):
        moves = []
        for source in range(NY * NZ):
            kind = (source // 16) * 2 + source % 2
            head = (source % 16) // 2
            moves.append((source, 4 * head + (kind + shift) % 4))
        parts.append(lax.ppermute(kv_weight, FEAT, moves))
    parts = jnp.stack(parts)
    blocks = [
        lax.dynamic_index_in_dim(parts, lax.rem(group - kind + 4, 4), 0, keepdims=False)
        for kind in range(4)
    ]
    return jnp.concatenate(blocks, axis=1)


def local(
    layer_input,
    enc_weight,
    enc_bias,
    active,
    dec_weight,
    dec_bias,
    sae_error,
    positions,
    attn_gain,
    query_weight,
    kv_weight,
    out_weight,
    mlp_gain,
    gate_weight,
    up_weight,
    down_weight,
    cotangent,
):
    feat = lax.axis_index(FEAT)
    core = lax.axis_index("c")
    width = enc_weight.shape[1]
    hidden = gate_weight.shape[1]
    head_width = query_weight.shape[1]
    own_rows = POINTS * SEQ

    first_sums = jnp.concatenate(
        [dot(layer_input, enc_weight), dot_t(cotangent, down_weight)], axis=1
    )
    first_sums = tok_sums(first_sums)
    encoded = first_sums[:, :width]
    back_hidden = first_sums[:, width:]
    alphas = jnp.arange(1, POINTS + 1, dtype=F32) / POINTS
    features = active.reshape(POINTS, SEQ, width).astype(F32) * (
        alphas[:, None, None] * encoded[None] + enc_bias
    )
    sent_features = features.reshape(own_rows, width).astype(B16)
    decoded = feat_sums(dot(tok_rows_wide(sent_features, core), dec_weight))

    first_token = (feat // POINTS) * SEQ
    error_rows = lax.dynamic_slice_in_dim(sae_error, first_token, SEQ, 0).astype(F32)
    cot_rows = lax.dynamic_slice_in_dim(cotangent, first_token, SEQ, 0).astype(F32)
    hidden_in = decoded + dec_bias + error_rows

    gained = feat_rows((hidden_in * attn_gain).astype(B16))
    squares = jnp.sum(jnp.square(gained.astype(F32) * (1.0 / attn_gain)), axis=1, keepdims=True)
    qkv_weight = jnp.concatenate([query_weight, own_keyval_weight(kv_weight)], axis=1)
    projections = jnp.concatenate(
        [dot(gained, qkv_weight).astype(B16), split_column(squares)], axis=1
    )
    projections = tok_sums(projections)
    qkv_width = qkv_weight.shape[1]
    scale_rows = lax.rsqrt(joined_column(projections[:, qkv_width:]) / D + epsilon)
    query_rows = projections[:, :head_width] * scale_rows
    keyval_rows = (projections[:, head_width:qkv_width] * scale_rows).astype(B16).astype(F32)

    position_rows = jnp.broadcast_to(positions.reshape(1, SEQ), (POINTS, SEQ)).reshape(own_rows, 1)
    frequency = rope_base ** (-jnp.arange(HD // 2, dtype=F32) * 2.0 / HD)
    angles = position_rows.astype(F32) * frequency
    cosine, sine = jnp.cos(angles), jnp.sin(angles)
    heads = head_width // HD
    row_of = lax.broadcasted_iota(jnp.int32, (heads * own_rows, own_rows), 0) % own_rows
    key_of = lax.broadcasted_iota(jnp.int32, (heads * own_rows, own_rows), 1)
    visible = (row_of // SEQ == key_of // SEQ) & (row_of >= key_of)
    attended, pullback = jax.vjp(
        lambda left, right: attend(left, right, cosine, sine, visible), query_rows, keyval_rows
    )
    projected = feat_sums(dot(tok_rows(attended.astype(B16)), out_weight))
    middle = hidden_in + projected

    gained = feat_rows((middle * mlp_gain).astype(B16))
    squares = jnp.sum(jnp.square(gained.astype(F32) * (1.0 / mlp_gain)), axis=1, keepdims=True)
    gate_up = jnp.concatenate(
        [dot(gained, gate_weight), dot(gained, up_weight), split_column(squares).astype(F32)],
        axis=1,
    )
    gate_up = tok_sums_wide(gate_up, core)
    scale_mlp = lax.rsqrt(joined_column(gate_up[:, 2 * hidden :]) / D + epsilon)
    gate_value = gate_up[:, :hidden] * scale_mlp
    up_value = gate_up[:, hidden : 2 * hidden] * scale_mlp
    back_rows = jnp.broadcast_to(back_hidden[None], (POINTS, SEQ, hidden)).reshape(own_rows, hidden)
    sigmoid_gate = jax.nn.sigmoid(gate_value)
    grad_gate = back_rows * up_value * sigmoid_gate * (1.0 + gate_value * (1.0 - sigmoid_gate))
    grad_up = back_rows * gate_value * sigmoid_gate
    mlp_grads = jnp.concatenate(
        [grad_gate.astype(B16), grad_up.astype(B16), split_column(scale_rows), split_column(scale_mlp)],
        axis=1,
    )
    mlp_grads = tok_rows_wide(mlp_grads, core)
    back_second = feat_sums(
        dot_t(mlp_grads[:, :hidden], gate_weight) + dot_t(mlp_grads[:, hidden : 2 * hidden], up_weight)
    )
    scales = lax.dynamic_slice_in_dim(mlp_grads[:, 2 * hidden :], feat * SEQ, SEQ, 0)
    scale_first = joined_column(scales[:, :128])
    scale_second = joined_column(scales[:, 128:])

    weighted_second = back_second * mlp_gain
    grad_middle = (
        cot_rows
        + scale_second * weighted_second
        - middle * scale_second**3 * (row_total(weighted_second * middle) / D)
    )
    grad_attended = tok_sums(dot_t(feat_rows(grad_middle.astype(B16)), out_weight))
    grad_query, grad_keyval = pullback(grad_attended)
    attn_grads = jnp.concatenate([grad_query, grad_keyval], axis=1).astype(B16)
    back_first = feat_sums(dot_t(tok_rows(attn_grads), qkv_weight))
    weighted_first = back_first * attn_gain
    grad_hidden = (
        grad_middle
        + scale_first * weighted_first
        - hidden_in * scale_first**3 * (row_total(weighted_first * hidden_in) / D)
    )
    feature_grads = tok_sums_wide(dot_t(feat_rows(grad_hidden.astype(B16)), dec_weight), core)
    previous = jnp.concatenate([jnp.zeros_like(features[:1]), features[:-1]], axis=0)
    return jnp.sum(feature_grads.reshape(POINTS, SEQ, width) * (features - previous), axis=0)


def solution(mesh):
    fine = Mesh(mesh.devices.reshape(NY, NZ, NX, NC), FEAT + TOK)
    in_specs = (
        P(None, TOK),
        P(TOK, FEAT),
        P(FEAT),
        P(TOK, FEAT),
        P(FEAT, TOK),
        P(TOK),
        P(None, TOK),
        P(TOK, None),
        P(TOK),
        P(TOK, FEAT),
        P(TOK, FEAT),
        P(FEAT, TOK),
        P(TOK),
        P(TOK, FEAT),
        P(TOK, FEAT),
        P(FEAT, TOK),
        P(None, TOK),
    )
    return jax.shard_map(
        local, mesh=fine, in_specs=in_specs, out_specs=P(TOK, FEAT), check_vma=False
    )
```

time: 1830 us -> 474 us (0.26)
  waiting for transfers between devices: 1570 us -> 95 us
  blocking collectives: 157 us -> 236 us
  starting transfers between devices: 0.85 us -> 69.8 us
    reduce_scatter x9 -> x0, waiting for transfers between devices: 1000 us -> none  [the longest x4 838 us: feature_sums(): lax.psum_scatter(product_term(jnp.int32(0), share_rows * lax.axis_size('f...]
    all_gather x6 -> x0, waiting for transfers between devices: 325 us -> none  [the longest x4 269 us: feature_rows(): return lax.all_gather(piece, 'feat', axis=0, tiled=True)]
    unnamed x19 -> x0, waiting for transfers between devices: 242 us -> none
    all_to_all x0 -> x17, blocking collectives: none -> 236 us  [swap(): return lax.all_to_all(blocks, axes, 0, 0, tiled=True)]
    all_gather x3 -> x0, blocking collectives: 85.2 us -> none  [the longest x2 46.6 us: token_rows(): return lax.all_gather(piece, 'tok', axis=0, tiled=True)]
    all_to_all x0 -> x10, waiting for transfers between devices: none -> 75.2 us  [swap(): return lax.all_to_all(blocks, axes, 0, 0, tiled=True)]
    psum x4 -> x0, blocking collectives: 71.8 us -> none  [row_total(): return lax.psum(jnp.sum(values, axis=1, keepdims=True), 'tok')]
    all_to_all x0 -> x10, starting transfers between devices: none -> 52.9 us  [swap(): return lax.all_to_all(blocks, axes, 0, 0, tiled=True)]
  transfers between devices with their start and end apart: 17 -> 18, of which waited for: 17 -> 15; matrix products, arithmetic and copies ran while one was open for 1% -> 3% of each run, Pallas kernels for 0% -> 0%
where the time goes in v1:
time: 474 us; the launch traced here: 472 us
  blocking collectives  236 us (50%)
  waiting for transfers between devices  95 us (20%)
  starting transfers between devices  69.8 us (15%)
  other arithmetic  26.5 us (6%)
  local copies, waits for them, and re-layouts  22.2 us (5%)
  matrix products  21 us (4%)
    all_to_all x17, blocking collectives, swap(): return lax.all_to_all(blocks, axes, 0, 0, tiled=True)  236 us
    all_to_all x10, waiting for transfers between devices, swap(): return lax.all_to_all(blocks, axes, 0, 0, tiled=True)  75.2 us
    all_to_all x10, starting transfers between devices, swap(): return lax.all_to_all(blocks, axes, 0, 0, tiled=True)  52.9 us
    ppermute x4, waiting for transfers between devices, own_keyval_weight(): parts.append(lax.ppermute(kv_weight, FEAT, moves))  13.3 us
    ppermute x4, starting transfers between devices, other_core(): return lax.ppermute(values, 'c', [(0, 1), (1, 0)])  13.1 us
    dot_general x6, matrix products, dot(): return jnp.dot(left_side, right_side, preferred_element_type=F32)  9.62 us
  transfers between devices with their start and end apart: 18, of which 15 were waited for; matrix products, arithmetic and copies ran while one was open for 3% of the time, Pallas kernels for 0%

profile of v1, /device:TPU:1, one launch (start us, length us, event | category | flops | bytes accessed | tf_op | source)
XLA Modules:
  0.0 471.7 jit_solution(2554582441849444079)
XLA Ops:
  0.0 1.9 convolution_convert_fusion.6
  2.0 2.2 convolution_convert_fusion.5
  4.9 6.6 %all-to-all-start = ((bf16[8,16,1536]{2,1,0:T(8,128)(2,1)}), bf16[8,16,1536]{2,1,0:T(8,128)(2,1)S(1)}, u32[]{:S(2)}, u32[]{:S(2)}) async-start(bf16[8,16,1536]{2,1,0:T(8,128)(2,1)} %pad_maximum_fusion.5), calls=%async_computation | async-start | bytes 786432 | tf_op jit(solution)/shard_map/all_to_all | solution.py:35
  11.7 7.9 %all-to-all-done = bf16[8,16,1536]{2,1,0:T(8,128)(2,1)S(1)} async-done(((bf16[8,16,1536]{2,1,0:T(8,128)(2,1)}), bf16[8,16,1536]{2,1,0:T(8,128)(2,1)S(1)}, u32[]{:S(2)}, u32[]{:S(2)}) %all-to-all-start) | async-done | bytes 393248 | tf_op jit(solution)/shard_map/all_to_all | solution.py:35
  20.3 11.0 %all_to_all.135 = bf16[4,64,1024]{2,1,0:T(8,128)(2,1)S(1)} all-to-all(bf16[4,64,1024]{2,1,0:T(8,128)(2,1)S(1)} %broadcast_in_dim.199), channel_id=1, replica_groups=mesh['y'=4,'z'=8,'x'=4,'c'=2] {'x'}, dimensions={0} | all-to-all | bytes 1048576 | tf_op jit(solution)/shard_map/all_to_all | solution.py:35
  31.3 1.8 collective-permute-start
  33.1 1.5 collective-permute-done
  36.2 17.4 %all_to_all.136 = bf16[4,128,1024]{2,1,0:T(8,128)(2,1)S(1)} all-to-all(bf16[4,128,1024]{2,1,0:T(8,128)(2,1)S(1)} %bitcast.146), channel_id=1, replica_groups=mesh['y'=4,'z'=8,'x'=4,'c'=2] {'y'}, dimensions={0} | all-to-all | bytes 2097152 | tf_op jit(solution)/shard_map/all_to_all | solution.py:35
  54.5 8.2 %all-to-all-start.3 = ((bf16[8,16,1024]{2,1,0:T(8,128)(2,1)}), bf16[8,16,1024]{2,1,0:T(8,128)(2,1)S(1)}, u32[]{:S(2)}, u32[]{:S(2)}) async-start(bf16[8,16,1024]{2,1,0:T(8,128)(2,1)} %bitcast.9), calls=%async_computation.3 | async-start | bytes 524288 | tf_op jit(solution)/shard_map/all_to_all | solution.py:35
  62.7 9.2 %all-to-all-done.3 = bf16[8,16,1024]{2,1,0:T(8,128)(2,1)S(1)} async-done(((bf16[8,16,1024]{2,1,0:T(8,128)(2,1)}), bf16[8,16,1024]{2,1,0:T(8,128)(2,1)S(1)}, u32[]{:S(2)}, u32[]{:S(2)}) %all-to-all-start.3) | async-done | bytes 262176 | tf_op jit(solution)/shard_map/all_to_all | solution.py:35
  72.8 11.9 %all_to_all.137 = bf16[8,16,1024]{2,1,0:T(8,128)(2,1)S(1)} all-to-all(bf16[8,16,1024]{2,1,0:T(8,128)(2,1)S(1)} %broadcast_in_dim.200), channel_id=1, replica_groups=mesh['y'=4,'z'=8,'x'=4,'c'=2] {'z'}, dimensions={0} | all-to-all | bytes 524288 | tf_op jit(solution)/shard_map/all_to_all | solution.py:35
  85.8 3.5 all-to-all-start.5
  90.9 2.1 collective-permute-start.1
  94.3 12.6 %collective-permute-done.3 = bf16[1024,64]{0,1:T(8,128)(2,1)S(1)} collective-permute-done((bf16[1024,64]{0,1:T(8,128)(2,1)}, bf16[1024,64]{0,1:T(8,128)(2,1)S(1)}, u32[]{:S(2)}, u32[]{:S(2)}) %collective-permute-start.3) | collective-permute-done | bytes 131104 | tf_op jit(solution)/shard_map/ppermute | solution.py:144
  109.8 1.8 copy.46
  111.5 1.8 copy.47
  113.3 1.7 copy.48
  115.0 3.4 concatenate.55
  118.8 2.0 convolution_convert_fusion.3
  122.1 7.5 %all-to-all-start.6 = ((bf16[8,64,640]{2,1,0:T(8,128)(2,1)}), bf16[8,64,640]{2,1,0:T(8,128)(2,1)S(1)}, u32[]{:S(2)}, u32[]{:S(2)}) async-start(bf16[8,64,640]{2,1,0:T(8,128)(2,1)} %bitcast.21), calls=%async_computation.6 | async-start | bytes 1310720 | tf_op jit(solution)/shard_map/all_to_all | solution.py:35
  129.8 10.7 %all-to-all-done.6 = bf16[8,64,640]{2,1,0:T(8,128)(2,1)S(1)} async-done(((bf16[8,64,640]{2,1,0:T(8,128)(2,1)}), bf16[8,64,640]{2,1,0:T(8,128)(2,1)S(1)}, u32[]{:S(2)}, u32[]{:S(2)}) %all-to-all-start.6) | async-done | bytes 655392 | tf_op jit(solution)/shard_map/all_to_all | solution.py:35
  142.7 9.8 %all_to_all.138 = bf16[8,64,256]{2,1,0:T(8,128)(2,1)S(1)} all-to-all(bf16[8,64,256]{2,1,0:T(8,128)(2,1)S(1)} %broadcast_in_dim.208), channel_id=1, replica_groups=mesh['y'=4,'z'=8,'x'=4,'c'=2] {'x','c'}, dimensions={0} | all-to-all | bytes 524288 | tf_op jit(solution)/shard_map/all_to_all | solution.py:35
  152.4 1.5 convolution_convert_fusion
  154.0 23.4 %all_to_all.139 = bf16[4,128,1024]{2,1,0:T(8,128)(2,1)S(1)} all-to-all(bf16[4,128,1024]{2,1,0:T(8,128)(2,1)S(1)} %bitcast.128), channel_id=1, replica_groups=mesh['y'=4,'z'=8,'x'=4,'c'=2] {'y'}, dimensions={0} | all-to-all | bytes 2097152 | tf_op jit(solution)/shard_map/all_to_all | solution.py:35
  177.7 11.8 %all_to_all.140 = bf16[8,16,1024]{2,1,0:T(8,128)(2,1)S(1)} all-to-all(bf16[8,16,1024]{2,1,0:T(8,128)(2,1)S(1)} %bitcast.140), channel_id=1, replica_groups=mesh['y'=4,'z'=8,'x'=4,'c'=2] {'z'}, dimensions={0} | all-to-all | bytes 524288 | tf_op jit(solution)/shard_map/all_to_all | solution.py:35
  189.6 1.4 multiply_convert_fusion
  191.0 11.9 %all_to_all.141 = bf16[8,16,1024]{2,1,0:T(8,128)(2,1)S(1)} all-to-all(bf16[8,16,1024]{2,1,0:T(8,128)(2,1)S(1)} %broadcast_in_dim.209), channel_id=1, replica_groups=mesh['y'=4,'z'=8,'x'=4,'c'=2] {'z'}, dimensions={0} | all-to-all | bytes 524288 | tf_op jit(solution)/shard_map/all_to_all | solution.py:35
  204.0 3.7 all-to-all-start.11
  207.7 10.0 %all-to-all-done.11 = bf16[4,128,1024]{2,1,0:T(8,128)(2,1)S(1)} async-done(((bf16[4,128,1024]{2,1,0:T(8,128)(2,1)}), bf16[4,128,1024]{2,1,0:T(8,128)(2,1)S(1)}, u32[]{:S(2)}, u32[]{:S(2)}) %all-to-all-start.11) | async-done | bytes 1048608 | tf_op jit(solution)/shard_map/all_to_all | solution.py:35
  218.2 2.0 fusion.114
  221.1 1.6 pad_maximum_fusion
  222.7 3.1 copy.50
  225.7 1.3 fusion.5
  227.1 5.9 %collective-permute-start.5 = (bf16[4,64,1152]{2,1,0:T(8,128)(2,1)S(1)}, bf16[4,64,1152]{2,1,0:T(8,128)(2,1)S(1)}, u32[]{:S(2)}, u32[]{:S(2)}) collective-permute-start(bf16[4,64,1152]{2,1,0:T(8,128)(2,1)S(1)} %fusion.5), channel_id=1, source_target_pairs={{0,1},{1,0},{2,3},{3,2},{4,5},{5,4},{6,7},{7,6},{8,9},{9,8},{10,11... | collective-permute-start | bytes 1769480 | tf_op jit(solution)/shard_map/ppermute | solution.py:64
  232.9 1.6 collective-permute-done.5
  234.6 2.2 fusion.2
  236.8 3.5 all-to-all-start.12
  240.3 9.9 %all-to-all-done.12 = bf16[4,64,1152]{2,1,0:T(8,128)(2,1)S(1)} async-done(((bf16[4,64,1152]{2,1,0:T(8,128)(2,1)}), bf16[4,64,1152]{2,1,0:T(8,128)(2,1)S(1)}, u32[]{:S(2)}, u32[]{:S(2)}) %all-to-all-start.12) | async-done | bytes 589856 | tf_op jit(solution)/shard_map/all_to_all | solution.py:35
  250.8 12.1 %all_to_all.142 = bf16[4,64,1280]{2,1,0:T(8,128)(2,1)S(1)} all-to-all(bf16[4,64,1280]{2,1,0:T(8,128)(2,1)S(1)} %broadcast_in_dim.223), channel_id=1, replica_groups=mesh['y'=4,'z'=8,'x'=4,'c'=2] {'x'}, dimensions={0} | all-to-all | bytes 1310720 | tf_op jit(solution)/shard_map/all_to_all | solution.py:35
  262.9 2.1 collective-permute-start.6
  265.1 1.7 collective-permute-done.6
  269.6 18.0 %all_to_all.143 = bf16[4,128,1024]{2,1,0:T(8,128)(2,1)} all-to-all(bf16[4,128,1024]{2,1,0:T(8,128)(2,1)S(1)} %bitcast.132), channel_id=1, replica_groups=mesh['y'=4,'z'=8,'x'=4,'c'=2] {'y'}, dimensions={0} | all-to-all | bytes 2097152 | tf_op jit(solution)/shard_map/all_to_all | solution.py:35
  287.6 2.2 reduce_sum.252
  289.8 4.0 all-to-all-start.15
  294.6 9.4 %all-to-all-done.15 = bf16[8,16,1024]{2,1,0:T(8,128)(2,1)} async-done(((bf16[8,16,1024]{2,1,0:T(8,128)(2,1)}), bf16[8,16,1024]{2,1,0:T(8,128)(2,1)}, u32[]{:S(2)}, u32[]{:S(2)}) %all-to-all-start.15) | async-done | bytes 262176 | tf_op jit(solution)/shard_map/all_to_all | solution.py:35
  306.6 5.9 %all-to-all-start.16 = ((f32[8,1,16]{2,1,0:T(1,128)}), f32[8,1,16]{2,1,0:T(1,128)S(1)}, u32[]{:S(2)}, u32[]{:S(2)}) async-start(f32[8,1,16]{2,1,0:T(1,128)} %broadcast_in_dim.224), calls=%async_computation.16 | async-start | bytes 8192 | tf_op jit(solution)/shard_map/all_to_all | solution.py:35
  312.5 1.5 fusion.90
  314.0 3.1 all-to-all-done.16
  317.1 1.6 fusion.106
  318.7 13.4 %all_to_all.144 = bf16[8,16,1024]{2,1,0:T(8,128)(2,1)S(1)} all-to-all(bf16[8,16,1024]{2,1,0:T(8,128)(2,1)S(1)} %broadcast_in_dim.225), channel_id=1, replica_groups=mesh['y'=4,'z'=8,'x'=4,'c'=2] {'z'}, dimensions={0} | all-to-all | bytes 524288 | tf_op jit(solution)/shard_map/all_to_all | solution.py:35
  332.2 15.3 %all_to_all.145 = bf16[4,128,1024]{2,1,0:T(8,128)(2,1)S(1)} all-to-all(bf16[4,128,1024]{2,1,0:T(8,128)(2,1)S(1)} %broadcast_in_dim.227), channel_id=1, replica_groups=mesh['y'=4,'z'=8,'x'=4,'c'=2] {'y'}, dimensions={0} | all-to-all | bytes 2097152 | tf_op jit(solution)/shard_map/all_to_all | solution.py:35
  348.7 6.5 %all-to-all-start.19 = ((bf16[8,64,256]{2,1,0:T(8,128)(2,1)}), bf16[8,64,256]{2,1,0:T(8,128)(2,1)S(1)}, u32[]{:S(2)}, u32[]{:S(2)}) async-start(bf16[8,64,256]{2,1,0:T(8,128)(2,1)} %bitcast.40), calls=%async_computation.19 | async-start | bytes 524288 | tf_op jit(solution)/shard_map/all_to_all | solution.py:35
  355.8 5.9 %all-to-all-done.19 = bf16[8,64,256]{2,1,0:T(8,128)(2,1)S(1)} async-done(((bf16[8,64,256]{2,1,0:T(8,128)(2,1)}), bf16[8,64,256]{2,1,0:T(8,128)(2,1)S(1)}, u32[]{:S(2)}, u32[]{:S(2)}) %all-to-all-start.19) | async-done | bytes 262176 | tf_op jit(solution)/shard_map/all_to_all | solution.py:35
  367.9 12.8 %all_to_all.146 = bf16[8,64,512]{2,1,0:T(8,128)(2,1)S(1)} all-to-all(bf16[8,64,512]{2,1,0:T(8,128)(2,1)S(1)} %broadcast_in_dim.231), channel_id=1, replica_groups=mesh['y'=4,'z'=8,'x'=4,'c'=2] {'x','c'}, dimensions={0} | all-to-all | bytes 1048576 | tf_op jit(solution)/shard_map/all_to_all | solution.py:35
  381.5 16.5 %all_to_all.147 = bf16[4,128,1024]{2,1,0:T(8,128)(2,1)S(1)} all-to-all(bf16[4,128,1024]{2,1,0:T(8,128)(2,1)S(1)} %bitcast.145), channel_id=1, replica_groups=mesh['y'=4,'z'=8,'x'=4,'c'=2] {'y'}, dimensions={0} | all-to-all | bytes 2097152 | tf_op jit(solution)/shard_map/all_to_all | solution.py:35
  398.2 11.6 %all_to_all.148 = bf16[8,16,1024]{2,1,0:T(8,128)(2,1)S(1)} all-to-all(bf16[8,16,1024]{2,1,0:T(8,128)(2,1)S(1)} %bitcast.137), channel_id=1, replica_groups=mesh['y'=4,'z'=8,'x'=4,'c'=2] {'z'}, dimensions={0} | all-to-all | bytes 524288 | tf_op jit(solution)/shard_map/all_to_all | solution.py:35
  410.7 10.6 %all_to_all.149 = f32[8,1,16]{2,1,0:T(1,128)S(1)} all-to-all(f32[8,1,16]{2,1,0:T(1,128)S(1)} %broadcast_in_dim.232), channel_id=1, replica_groups=mesh['y'=4,'z'=8,'x'=4,'c'=2] {'x','c'}, dimensions={0} | all-to-all | bytes 1024 | tf_op jit(solution)/shard_map/all_to_all | solution.py:35
  422.3 13.3 %all_to_all.150 = bf16[8,16,1024]{2,1,0:T(8,128)(2,1)S(1)} all-to-all(bf16[8,16,1024]{2,1,0:T(8,128)(2,1)S(1)} %broadcast_in_dim.233), channel_id=1, replica_groups=mesh['y'=4,'z'=8,'x'=4,'c'=2] {'z'}, dimensions={0} | all-to-all | bytes 524288 | tf_op jit(solution)/shard_map/all_to_all | solution.py:35
  435.7 15.3 %all_to_all.151 = bf16[4,128,1024]{2,1,0:T(8,128)(2,1)S(1)} all-to-all(bf16[4,128,1024]{2,1,0:T(8,128)(2,1)S(1)} %broadcast_in_dim.235), channel_id=1, replica_groups=mesh['y'=4,'z'=8,'x'=4,'c'=2] {'y'}, dimensions={0} | all-to-all | bytes 2097152 | tf_op jit(solution)/shard_map/all_to_all | solution.py:35
  451.0 1.3 fusion
  452.4 3.3 collective-permute-start.7
  455.6 1.5 collective-permute-done.7
  458.1 3.5 all-to-all-start.26
  461.8 9.0 %all-to-all-done.26 = bf16[4,64,1024]{2,1,0:T(8,128)(2,1)S(1)} async-done(((bf16[4,64,1024]{2,1,0:T(8,128)(2,1)}), bf16[4,64,1024]{2,1,0:T(8,128)(2,1)S(1)}, u32[]{:S(2)}, u32[]{:S(2)}) %all-to-all-start.26) | async-done | bytes 524320 | tf_op jit(solution)/shard_map/all_to_all | solution.py:35
  (205 shorter events, 37.8 us)
Async XLA Ops:
  0.0 34.8 %copy-start = (bf16[1024,1024]{1,0:T(8,128)(2,1)S(1)}, bf16[1024,1024]{1,0:T(8,128)(2,1)}, u32[]{:S(2)}) copy-start(bf16[1024,1024]{1,0:T(8,128)(2,1)} %param.21) | copy-start | bytes 6291460
  1.9 17.7 %copy-start.1 = (s32[64,1024]{1,0:T(8,128)S(1)}, s32[64,1024]{1,0:T(8,128)}, u32[]{:S(2)}) copy-start(s32[64,1024]{1,0:T(8,128)} %param.20) | copy-start | bytes 786436
  2.0 17.7 %copy-start.13 = (f32[1024]{0:T(1024)S(1)}, f32[1024]{0:T(1024)}, u32[]{:S(2)}) copy-start(f32[1024]{0:T(1024)} %param.19) | copy-start | bytes 12292
  4.9 14.7 %all-to-all-start = ((bf16[8,16,1536]{2,1,0:T(8,128)(2,1)}), bf16[8,16,1536]{2,1,0:T(8,128)(2,1)S(1)}, u32[]{:S(2)}, u32[]{:S(2)}) async-start(bf16[8,16,1536]{2,1,0:T(8,128)(2,1)} %pad_maximum_fusion.5), calls=%async_computation | async-start | bytes 786432 | tf_op jit(solution)/shard_map/all_to_all | solution.py:35
  11.5 23.2 %copy-start.29 = (f32[4]{0:T(128)}, f32[4]{0:T(128)S(1)}, u32[]{:S(2)}) copy-start(f32[4]{0:T(128)S(1)} %add_multiply_fusion.2) | copy-start | bytes 52
  19.7 0.6 copy-start.8
  31.3 3.4 collective-permute-start
  36.1 35.8 %copy-start.10 = (f32[1024]{0:T(1024)S(1)}, f32[1024]{0:T(1024)}, u32[]{:S(2)}) copy-start(f32[1024]{0:T(1024)} %param.22) | copy-start | bytes 12292
  36.1 35.8 %copy-start.12 = (f32[1024]{0:T(1024)S(1)}, f32[1024]{0:T(1024)}, u32[]{:S(2)}) copy-start(f32[1024]{0:T(1024)} %param.25) | copy-start | bytes 12292
  54.5 17.4 %all-to-all-start.3 = ((bf16[8,16,1024]{2,1,0:T(8,128)(2,1)}), bf16[8,16,1024]{2,1,0:T(8,128)(2,1)S(1)}, u32[]{:S(2)}, u32[]{:S(2)}) async-start(bf16[8,16,1024]{2,1,0:T(8,128)(2,1)} %bitcast.9), calls=%async_computation.3 | async-start | bytes 524288 | tf_op jit(solution)/shard_map/all_to_all | solution.py:35
  85.8 32.6 %all-to-all-start.5 = ((bf16[4,128,1024]{2,1,0:T(8,128)(2,1)}), bf16[4,128,1024]{2,1,0:T(8,128)(2,1)S(1)}, u32[]{:S(2)}, u32[]{:S(2)}) async-start(bf16[4,128,1024]{2,1,0:T(8,128)(2,1)} %broadcast_in_dim.202), calls=%async_computation.5 | async-start | bytes 2097152 | tf_op jit(solution)/shard_map/all_to_all | solution.py:35
  89.3 5.0 %collective-permute-start.4 = (bf16[1024,64]{0,1:T(8,128)(2,1)}, bf16[1024,64]{0,1:T(8,128)(2,1)S(1)}, u32[]{:S(2)}, u32[]{:S(2)}) collective-permute-start(bf16[1024,64]{0,1:T(8,128)(2,1)} %param.27), channel_id=1, source_target_pairs={{0,24},{8,0},{16,56},{24,32},{32,88},{40,64},{48,120},{56,96},{64,... | collective-permute-start | bytes 393224 | tf_op jit(solution)/shard_map/ppermute | solution.py:144
  89.5 17.4 %collective-permute-start.3 = (bf16[1024,64]{0,1:T(8,128)(2,1)}, bf16[1024,64]{0,1:T(8,128)(2,1)S(1)}, u32[]{:S(2)}, u32[]{:S(2)}) collective-permute-start(bf16[1024,64]{0,1:T(8,128)(2,1)} %param.27), channel_id=1, source_target_pairs={{0,16},{8,24},{16,48},{24,56},{32,80},{40,88},{48,112},{56,120},{6... | collective-permute-start | bytes 393224 | tf_op jit(solution)/shard_map/ppermute | solution.py:144
  90.3 16.6 %collective-permute-start.2 = (bf16[1024,64]{0,1:T(8,128)(2,1)}, bf16[1024,64]{0,1:T(8,128)(2,1)}, u32[]{:S(2)}, u32[]{:S(2)}) collective-permute-start(bf16[1024,64]{0,1:T(8,128)(2,1)} %param.27), channel_id=1, source_target_pairs={{0,8},{8,16},{16,40},{24,48},{32,72},{40,80},{48,104},{56,112},{64... | collective-permute-start | bytes 393224 | tf_op jit(solution)/shard_map/ppermute | solution.py:144
  90.9 16.0 %collective-permute-start.1 = (bf16[1024,64]{0,1:T(8,128)(2,1)}, bf16[1024,64]{0,1:T(8,128)(2,1)}, u32[]{:S(2)}, u32[]{:S(2)}) collective-permute-start(bf16[1024,64]{0,1:T(8,128)(2,1)} %param.27), channel_id=1, source_target_pairs={{0,0},{8,8},{16,32},{24,40},{32,64},{40,72},{48,96},{56,104},{64,1... | collective-permute-start | bytes 393224 | tf_op jit(solution)/shard_map/ppermute | solution.py:144
  118.4 2.4 copy-start.21
  118.4 2.4 copy-start.24
  120.8 8.8 %copy-start.37 = (s32[1,16]{1,0:T(1,128)S(1)}, s32[1,16]{1,0:T(1,128)}, u32[]{:S(2)}) copy-start(s32[1,16]{1,0:T(1,128)} %param.24) | copy-start | bytes 196
  122.1 18.4 %all-to-all-start.6 = ((bf16[8,64,640]{2,1,0:T(8,128)(2,1)}), bf16[8,64,640]{2,1,0:T(8,128)(2,1)S(1)}, u32[]{:S(2)}, u32[]{:S(2)}) async-start(bf16[8,64,640]{2,1,0:T(8,128)(2,1)} %bitcast.21), calls=%async_computation.6 | async-start | bytes 1310720 | tf_op jit(solution)/shard_map/all_to_all | solution.py:35
  129.7 12.4 %copy-start.27 = (f32[64]{0:T(128)}, f32[64]{0:T(128)S(1)}, u32[]{:S(2)}) copy-start(f32[64]{0:T(128)S(1)} %convert_element_type.196) | copy-start | bytes 772
  129.7 24.2 %copy-start.31 = (f32[64]{0:T(128)}, f32[64]{0:T(128)S(1)}, u32[]{:S(2)}) copy-start(f32[64]{0:T(128)S(1)} %multiply_power_fusion) | copy-start | bytes 772
  129.7 12.3 %copy-start.42 = (pred[64]{0:T(512)(128)(4,1)}, pred[64]{0:T(512)(128)(4,1)S(1)}, u32[]{:S(2)}) copy-start(pred[64]{0:T(512)(128)(4,1)S(1)} %compare_and_fusion) | copy-start | bytes 196
  129.8 12.3 %copy-start.43 = (pred[128]{0:T(512)(128)(4,1)}, pred[128]{0:T(512)(128)(4,1)S(1)}, u32[]{:S(2)}) copy-start(pred[128]{0:T(512)(128)(4,1)S(1)} %compare_and_fusion.1) | copy-start | bytes 388
  129.8 12.3 %copy-start.38 = (s32[64]{0:T(128)}, s32[64]{0:T(128)S(1)}, u32[]{:S(2)}) copy-start(s32[64]{0:T(128)S(1)} %get-tuple-element.68) | copy-start | bytes 772
  129.8 12.3 %copy-start.39 = (s32[64]{0:T(128)}, s32[64]{0:T(128)S(1)}, u32[]{:S(2)}) copy-start(s32[64]{0:T(128)S(1)} %get-tuple-element.69) | copy-start | bytes 772
  129.8 12.3 %copy-start.40 = (s32[128]{0:T(128)}, s32[128]{0:T(128)S(1)}, u32[]{:S(2)}) copy-start(s32[128]{0:T(128)S(1)} %get-tuple-element.70) | copy-start | bytes 1540
  129.8 12.3 %copy-start.41 = (s32[128]{0:T(128)}, s32[128]{0:T(128)S(1)}, u32[]{:S(2)}) copy-start(s32[128]{0:T(128)S(1)} %get-tuple-element.71) | copy-start | bytes 1540
  141.4 12.6 %copy-start.20 = (bf16[64,256]{1,0:T(8,128)(2,1)}, bf16[64,256]{1,0:T(8,128)(2,1)S(1)}, u32[]{:S(2)}) copy-start(bf16[64,256]{1,0:T(8,128)(2,1)S(1)} %get-tuple-element.24) | copy-start | bytes 98308
  141.6 12.3 %copy-start.14 = (f32[64,64]{1,0:T(8,128)}, f32[64,64]{1,0:T(8,128)S(1)}, u32[]{:S(2)}) copy-start(f32[64,64]{1,0:T(8,128)S(1)} %get-tuple-element.40) | copy-start | bytes 49156
  141.6 12.3 %copy-start.15 = (f32[64,64]{1,0:T(8,128)}, f32[64,64]{1,0:T(8,128)S(1)}, u32[]{:S(2)}) copy-start(f32[64,64]{1,0:T(8,128)S(1)} %get-tuple-element.41) | copy-start | bytes 49156
  141.7 12.3 %copy-start.16 = (f32[64,64]{1,0:T(8,128)}, f32[64,64]{1,0:T(8,128)S(1)}, u32[]{:S(2)}) copy-start(f32[64,64]{1,0:T(8,128)S(1)} %get-tuple-element.42) | copy-start | bytes 49156
  141.7 12.3 %copy-start.17 = (f32[64,64]{1,0:T(8,128)}, f32[64,64]{1,0:T(8,128)S(1)}, u32[]{:S(2)}) copy-start(f32[64,64]{1,0:T(8,128)S(1)} %get-tuple-element.43) | copy-start | bytes 49156
  141.7 12.3 %copy-start.18 = (f32[64,64]{1,0:T(8,128)}, f32[64,64]{1,0:T(8,128)S(1)}, u32[]{:S(2)}) copy-start(f32[64,64]{1,0:T(8,128)S(1)} %get-tuple-element.61) | copy-start | bytes 49156
  141.7 12.3 %copy-start.19 = (f32[64,64]{1,0:T(8,128)}, f32[64,64]{1,0:T(8,128)S(1)}, u32[]{:S(2)}) copy-start(f32[64,64]{1,0:T(8,128)S(1)} %get-tuple-element.62) | copy-start | bytes 49156
  142.0 0.6 copy-start.9
  142.0 12.0 %copy-start.32 = (f32[128]{0:T(128)}, f32[128]{0:T(128)S(1)}, u32[]{:S(2)}) copy-start(f32[128]{0:T(128)S(1)} %get-tuple-element.63) | copy-start | bytes 1540
  142.1 11.9 %copy-start.33 = (f32[128]{0:T(128)}, f32[128]{0:T(128)S(1)}, u32[]{:S(2)}) copy-start(f32[128]{0:T(128)S(1)} %fusion.74) | copy-start | bytes 1540
  154.0 35.5 %copy-start.11 = (f32[1024]{0:T(1024)S(1)}, f32[1024]{0:T(1024)}, u32[]{:S(2)}) copy-start(f32[1024]{0:T(1024)} %param.29) | copy-start | bytes 12292
  204.0 13.8 %all-to-all-start.11 = ((bf16[4,128,1024]{2,1,0:T(8,128)(2,1)}), bf16[4,128,1024]{2,1,0:T(8,128)(2,1)S(1)}, u32[]{:S(2)}, u32[]{:S(2)}) async-start(bf16[4,128,1024]{2,1,0:T(8,128)(2,1)} %broadcast_in_dim.211), calls=%async_computation.11 | async-start | bytes 2097152 | tf_op jit(solution)/shard_map/all_to_all | solution.py:35
  217.8 2.3 copy-start.3
  220.1 0.8 copy-start.22
  220.2 0.8 copy-start.25
  227.1 7.5 %collective-permute-start.5 = (bf16[4,64,1152]{2,1,0:T(8,128)(2,1)S(1)}, bf16[4,64,1152]{2,1,0:T(8,128)(2,1)S(1)}, u32[]{:S(2)}, u32[]{:S(2)}) collective-permute-start(bf16[4,64,1152]{2,1,0:T(8,128)(2,1)S(1)} %fusion.5), channel_id=1, source_target_pairs={{0,1},{1,0},{2,3},{3,2},{4,5},{5,4},{6,7},{7,6},{8,9},{9,8},{10,11... | collective-permute-start | bytes 1769480 | tf_op jit(solution)/shard_map/ppermute | solution.py:64
  232.9 17.5 %slice-start = ((f32[16,1536]{1,0:T(8,128)}), f32[16,512]{1,0:T(8,128)S(1)}, s32[]{:S(2)}) async-start(f32[16,1536]{1,0:T(8,128)} %copy-done.8), calls=%async_computation.27 | async-start | bytes 65536 | tf_op jit(solution)/shard_map/slice | solution.py:184
  234.6 16.0 %copy-start.23 = (pred[128]{0:T(512)(128)(4,1)S(1)}, pred[128]{0:T(512)(128)(4,1)}, u32[]{:S(2)}) copy-start(pred[128]{0:T(512)(128)(4,1)} %get-tuple-element.66) | copy-start | bytes 388
  234.6 16.1 %copy-start.26 = (pred[128]{0:T(512)(128)(4,1)S(1)}, pred[128]{0:T(512)(128)(4,1)}, u32[]{:S(2)}) copy-start(pred[128]{0:T(512)(128)(4,1)} %get-tuple-element.67) | copy-start | bytes 388
  234.6 16.1 %copy-start.35 = (bf16[64]{0:T(256)(128)(2,1)S(1)}, bf16[64]{0:T(256)(128)(2,1)}, u32[]{:S(2)}) copy-start(bf16[64]{0:T(256)(128)(2,1)} %get-tuple-element.12) | copy-start | bytes 388
  234.6 16.1 %copy-start.36 = (bf16[64]{0:T(256)(128)(2,1)S(1)}, bf16[64]{0:T(256)(128)(2,1)}, u32[]{:S(2)}) copy-start(bf16[64]{0:T(256)(128)(2,1)} %get-tuple-element.13) | copy-start | bytes 388
  236.8 13.4 %all-to-all-start.12 = ((bf16[4,64,1152]{2,1,0:T(8,128)(2,1)}), bf16[4,64,1152]{2,1,0:T(8,128)(2,1)S(1)}, u32[]{:S(2)}, u32[]{:S(2)}) async-start(bf16[4,64,1152]{2,1,0:T(8,128)(2,1)} %fusion.2), calls=%async_computation.12 | async-start | bytes 1179648 | tf_op jit(solution)/shard_map/all_to_all | solution.py:35
  262.9 3.9 collective-permute-start.6
  266.9 1.2 copy-start.4
  267.1 1.7 copy-start.6
  289.8 14.2 %all-to-all-start.15 = ((bf16[8,16,1024]{2,1,0:T(8,128)(2,1)}), bf16[8,16,1024]{2,1,0:T(8,128)(2,1)}, u32[]{:S(2)}, u32[]{:S(2)}) async-start(bf16[8,16,1024]{2,1,0:T(8,128)(2,1)} %bitcast.135), calls=%async_computation.15 | async-start | bytes 524288 | tf_op jit(solution)/shard_map/all_to_all | solution.py:35
  306.6 10.5 %all-to-all-start.16 = ((f32[8,1,16]{2,1,0:T(1,128)}), f32[8,1,16]{2,1,0:T(1,128)S(1)}, u32[]{:S(2)}, u32[]{:S(2)}) async-start(f32[8,1,16]{2,1,0:T(1,128)} %broadcast_in_dim.224), calls=%async_computation.16 | async-start | bytes 8192 | tf_op jit(solution)/shard_map/all_to_all | solution.py:35
  318.7 28.8 %copy-start.7 = (bf16[256,1024]{1,0:T(8,128)(2,1)S(1)}, bf16[256,1024]{1,0:T(8,128)(2,1)}, u32[]{:S(2)}) copy-start(bf16[256,1024]{1,0:T(8,128)(2,1)} %param.28) | copy-start | bytes 1572868
  332.2 23.0 %copy-start.34 = (f32[128]{0:T(128)S(1)}, f32[128]{0:T(128)}, u32[]{:S(2)}) copy-start(f32[128]{0:T(128)} %copy-done.33) | copy-start | bytes 1540
  347.5 19.3 %copy-start.28 = (f32[64]{0:T(128)S(1)}, f32[64]{0:T(128)}, u32[]{:S(2)}) copy-start(f32[64]{0:T(128)} %copy-done.27) | copy-start | bytes 772
  348.7 13.0 %all-to-all-start.19 = ((bf16[8,64,256]{2,1,0:T(8,128)(2,1)}), bf16[8,64,256]{2,1,0:T(8,128)(2,1)S(1)}, u32[]{:S(2)}, u32[]{:S(2)}) async-start(bf16[8,64,256]{2,1,0:T(8,128)(2,1)} %bitcast.40), calls=%async_computation.19 | async-start | bytes 524288 | tf_op jit(solution)/shard_map/all_to_all | solution.py:35
  355.8 25.0 %copy-start.5 = (bf16[1024,512]{1,0:T(8,128)(2,1)S(1)}, bf16[1024,512]{1,0:T(8,128)(2,1)}, u32[]{:S(2)}) copy-start(bf16[1024,512]{1,0:T(8,128)(2,1)} %concatenate.55) | copy-start | bytes 3145732
  452.3 9.4 %copy-start.2 = (s32[64,1024]{1,0:T(8,128)S(1)}, s32[64,1024]{1,0:T(8,128)}, u32[]{:S(2)}) copy-start(s32[64,1024]{1,0:T(8,128)} %param.20) | copy-start | bytes 786436
  452.4 9.3 %copy-start.30 = (f32[4]{0:T(128)S(1)}, f32[4]{0:T(128)}, u32[]{:S(2)}) copy-start(f32[4]{0:T(128)} %copy-done.29) | copy-start | bytes 52
  452.4 4.8 %collective-permute-start.7 = (bf16[4,64,1024]{2,1,0:T(8,128)(2,1)S(1)}, bf16[4,64,1024]{2,1,0:T(8,128)(2,1)S(1)}, u32[]{:S(2)}, u32[]{:S(2)}) collective-permute-start(bf16[4,64,1024]{2,1,0:T(8,128)(2,1)S(1)} %fusion.6), channel_id=1, source_target_pairs={{0,1},{1,0},{2,3},{3,2},{4,5},{5,4},{6,7},{7,6},{8,9},{9,8},{10,11... | collective-permute-start | bytes 1572872 | tf_op jit(solution)/shard_map/ppermute | solution.py:64
  458.1 12.7 %all-to-all-start.26 = ((bf16[4,64,1024]{2,1,0:T(8,128)(2,1)}), bf16[4,64,1024]{2,1,0:T(8,128)(2,1)S(1)}, u32[]{:S(2)}, u32[]{:S(2)}) async-start(bf16[4,64,1024]{2,1,0:T(8,128)(2,1)} %fusion.4), calls=%async_computation.26 | async-start | bytes 1048576 | tf_op jit(solution)/shard_map/all_to_all | solution.py:35

commit v2 on v1

v2 whole, which is shorter than its diff:
```python
import jax
import jax.numpy as jnp
import numpy as np
from jax import lax
from jax.sharding import Mesh
from jax.sharding import PartitionSpec as P

D = 8192
HD = 128
POINTS = 4
SEQ = 16
NY, NZ, NX, NC = 4, 8, 4, 2
QUAD = 4
Z = ("half", "quad")
FEAT = ("y", "half", "quad")
TOK = ("x", "c")

epsilon = 1e-05
rope_base = 500000.0
F32 = jnp.float32
B16 = jnp.bfloat16


def dot(left_side, right_side):
    return jnp.dot(left_side, right_side, preferred_element_type=F32)


def dot_t(left_side, right_side):
    return lax.dot_general(
        left_side, right_side, (((1,), (1,)), ((), ())), preferred_element_type=F32
    )


def exact(left_side, right_side, left_dim, right_dim):
    return lax.dot_general(
        left_side,
        right_side,
        (((left_dim,), (right_dim,)), ((), ())),
        precision=lax.Precision.HIGHEST,
        preferred_element_type=F32,
    )


def swap(blocks, axes):
    return lax.all_to_all(blocks, axes, 0, 0, tiled=True)


def spread(piece, axes, count):
    blocks = jnp.broadcast_to(piece[None], (count,) + piece.shape)
    return swap(lax.optimization_barrier(blocks), axes).reshape((-1,) + piece.shape[1:])


def added(blocks):
    return jnp.sum(blocks.astype(F32), axis=0)


def feat_sums(partial):
    rows, width = partial.shape
    blocks = swap(partial.astype(B16).reshape(NY, rows // NY, width), "y")
    blocks = added(blocks).astype(B16).reshape(NZ, rows // (NY * NZ), width)
    return added(swap(blocks, Z))


def feat_rows(piece, first_core=None):
    piece = spread(piece, Z, NZ)
    if first_core is not None:
        halves = piece.reshape((2, -1) + piece.shape[1:])
        piece = jnp.where(first_core, halves, halves[::-1]).reshape(piece.shape)
    return spread(piece, "y", NY)


def tok_sums(partial):
    rows, width = partial.shape
    return added(swap(partial.astype(B16).reshape(NX * NC, rows // (NX * NC), width), TOK))


def other_core(values):
    return lax.ppermute(values, "c", [(0, 1), (1, 0)])


def tok_sums_core_first(rows, product):
    blocks = rows.reshape(NX, NC, -1, rows.shape[-1])
    height = blocks.shape[2]
    other = product(blocks[:, 1].reshape(NX * height, -1))
    received = other_core(other.astype(B16))
    own = product(blocks[:, 0].reshape(NX * height, -1))
    own = (own + received.astype(F32)).astype(B16)
    return added(swap(own.reshape(NX, height, -1), "x"))


def tok_rows(piece):
    return spread(piece, TOK, NX * NC)


def both_cores(own, first_core, piece):
    own = own.reshape((NX,) + piece.shape)
    other = other_core(own)
    first = jnp.where(first_core, own, other)
    second = jnp.where(first_core, other, own)
    return jnp.stack([first, second], axis=1).reshape((-1,) + piece.shape[1:])


def split_column(masks, *columns):
    block = jnp.zeros((columns[0].shape[0], 128), F32)
    for index, values in enumerate(columns):
        high = lax.reduce_precision(values, 8, 7)
        block = jnp.where(masks[2 * index], high, block)
        block = jnp.where(masks[2 * index + 1], values - high, block)
    return block.astype(B16)


def joined_column(block, first=0):
    return block[:, first : first + 1].astype(F32) + block[:, first + 1 : first + 2].astype(F32)


def rotate(vectors, cosine, sine):
    half = vectors.shape[-1] // 2
    first, second = vectors[:, :half], vectors[:, half:]
    return jnp.concatenate(
        [first * cosine - second * sine, second * cosine + first * sine], axis=-1
    )


def stacked_heads(values):
    heads = values.shape[1] // HD
    return jnp.concatenate([values[:, h * HD : (h + 1) * HD] for h in range(heads)], axis=0)


def side_by_side(values):
    heads = values.shape[0] // SEQ
    return jnp.concatenate([values[h * SEQ : (h + 1) * SEQ] for h in range(heads)], axis=1)


def attend(query_rows, keyval_rows, cosine, sine, visible):
    half = keyval_rows.shape[1] // 2
    tables = [
        jnp.concatenate([table] * (width // HD), axis=0)
        for width in (query_rows.shape[1], half)
        for table in (cosine, sine)
    ]
    queries = rotate(stacked_heads(query_rows), tables[0], tables[1])
    keys = rotate(stacked_heads(keyval_rows[:, :half]), tables[2], tables[3])
    values = stacked_heads(keyval_rows[:, half:])
    scores = exact(queries, keys, 1, 1) * HD ** (-0.5)
    scores = jnp.where(visible, scores, -1e30)
    weights = jnp.exp(scores - jnp.max(scores, axis=-1, keepdims=True))
    weights = weights / jnp.sum(weights, axis=-1, keepdims=True)
    saved = (queries, keys, values, weights, tables)
    return side_by_side(exact(weights, values, 1, 0)), saved


def attend_back(grad_attended, saved):
    queries, keys, values, weights, tables = saved
    grads = stacked_heads(grad_attended)
    grad_values = exact(weights, grads, 0, 0)
    grad_weights = exact(grads, values, 1, 1)
    mean_grad = jnp.sum(grad_weights * weights, axis=-1, keepdims=True)
    grad_scores = weights * (grad_weights - mean_grad) * HD ** (-0.5)
    grad_queries = rotate(exact(grad_scores, keys, 1, 0), tables[0], -tables[1])
    grad_keys = rotate(exact(grad_scores, queries, 0, 0), tables[2], -tables[3])
    return side_by_side(grad_queries), jnp.concatenate(
        [side_by_side(grad_keys), side_by_side(grad_values)], axis=1
    )


def turned(weight):
    return dot_t(jnp.eye(weight.shape[1], dtype=B16), weight).astype(B16)


def placed_block(block):
    moves = []
    for source in range(NY * NZ):
        row, place = divmod(source, NZ)
        half = (place // 2) % 2
        moves.append((source, NZ * row + QUAD * half + 2 * (place // QUAD) + place % 2))
    return lax.ppermute(block, FEAT, moves)


def prepared(attn_gain, mlp_gain, sae_error, cotangent):
    feat = lax.axis_index(FEAT)
    first_token = (feat // POINTS) * SEQ
    row = np.arange(NZ * SEQ)
    key = np.arange(NY * SEQ)
    visible = (row[:, None] // (2 * SEQ) == key // SEQ) & (row[:, None] % SEQ >= key % SEQ)
    return dict(
        own_prompt=2 * lax.axis_index("y") + lax.axis_index(TOK) // POINTS,
        first_core=lax.axis_index("c") == 0,
        visible=jnp.asarray(visible),
        masks=[jnp.asarray(np.arange(128)[None, :] == lane) for lane in range(6)],
        attn_unscaled=1.0 / attn_gain,
        mlp_unscaled=1.0 / mlp_gain,
        error_rows=lax.dynamic_slice_in_dim(sae_error, first_token, SEQ, 0).astype(F32),
        cot_rows=lax.dynamic_slice_in_dim(cotangent, first_token, SEQ, 0).astype(F32),
    )


def feat_part_rows(piece):
    return spread(piece, Z, NZ)


def feat_part_sums(partial):
    rows, width = partial.shape
    return added(swap(partial.astype(B16).reshape(NZ, rows // NZ, width), Z))


def local(
    layer_input,
    enc_weight,
    enc_bias,
    active,
    dec_weight,
    dec_bias,
    sae_error,
    positions,
    attn_gain,
    query_weight,
    kv_weight,
    out_weight,
    mlp_gain,
    gate_weight,
    up_weight,
    down_weight,
    cotangent,
):
    width = enc_weight.shape[1]
    hidden = gate_weight.shape[1]
    model_width = dec_weight.shape[1]

    first_sums = jnp.concatenate(
        [dot(layer_input, enc_weight).astype(B16), dot_t(cotangent, down_weight).astype(B16)],
        axis=1,
    ).reshape(NX * NC, SEQ, width + hidden)
    own_positions = jnp.broadcast_to(
        positions.reshape(1, SEQ, 1).astype(B16), (NX * NC, SEQ, 128)
    )
    blocks = swap(jnp.concatenate([first_sums, own_positions], axis=2), TOK)
    ready = prepared(attn_gain, mlp_gain, sae_error, cotangent)
    active_rows = active.reshape(POINTS, SEQ, width).astype(F32)
    turned_rows = jnp.concatenate(
        [turned(query_weight), placed_block(turned(kv_weight))], axis=0
    )
    turned_rows = lax.all_gather(turned_rows, "y", axis=0, tiled=True)
    blocks, ready, active_rows, gate_weight, up_weight = lax.optimization_barrier(
        (blocks, ready, active_rows, gate_weight, up_weight)
    )
    first_core, masks = ready["first_core"], ready["masks"]
    first_sums = added(blocks[:, :, : width + hidden])
    own_positions = lax.dynamic_index_in_dim(
        blocks[:, :, width + hidden], ready["own_prompt"], 0, keepdims=False
    ).astype(F32)
    frequency = (rope_base ** (-np.arange(HD // 2) * 2.0 / HD)).astype(np.float32)
    angles = own_positions[:, None] * frequency
    cosine, sine = jnp.cos(angles), jnp.sin(angles)
    encoded = first_sums[:, :width]
    back_hidden = first_sums[:, width:]
    features = [
        active_rows[k] * ((k + 1) / POINTS * encoded + enc_bias) for k in range(POINTS)
    ]
    changes = [features[0]] + [features[k] - features[k - 1] for k in range(1, POINTS)]
    changes = jnp.concatenate(changes, axis=0)
    sent_features = jnp.concatenate(features, axis=0).astype(B16)
    own_rows = spread(sent_features, "x", NX)
    back_rows = jnp.concatenate([back_hidden] * POINTS, axis=0)
    gate_up_weight = jnp.concatenate([gate_weight, up_weight], axis=1)
    own_rows, changes, back_rows, gate_up_weight, cosine, sine = lax.optimization_barrier(
        (own_rows, changes, back_rows, gate_up_weight, cosine, sine)
    )
    gathered = both_cores(own_rows, first_core, sent_features)
    decoded = feat_sums(dot(gathered, dec_weight))
    out_rows = lax.all_gather(out_weight, "y", axis=0, tiled=True)
    hidden_in = decoded + dec_bias + ready["error_rows"]

    gained = feat_part_rows((hidden_in * attn_gain).astype(B16))
    squares = jnp.sum(
        jnp.square(gained.astype(F32) * ready["attn_unscaled"]), axis=1, keepdims=True
    )
    projections = tok_sums(
        jnp.concatenate(
            [dot_t(gained, turned_rows).astype(B16), split_column(masks, squares)], axis=1
        )
    )
    projections, out_rows = lax.optimization_barrier((projections, out_rows))
    head_part = query_weight.shape[1]
    qkv_width = turned_rows.shape[0]
    scale_rows = lax.rsqrt(joined_column(projections[:, qkv_width:]) / D + epsilon)
    own_qkv = (projections[:, :qkv_width] * scale_rows).reshape(SEQ, NY, qkv_width // NY)
    kv_part = own_qkv.shape[2] - head_part
    own_keyval = own_qkv[:, :, head_part:].astype(B16).reshape(SEQ, NY * kv_part)
    keyval = spread(own_keyval, "quad", QUAD).reshape(QUAD, SEQ, NY, kv_part)
    attended, saved = attend(
        own_qkv[:, :, :head_part].reshape(SEQ, -1),
        keyval.transpose(1, 2, 0, 3).reshape(SEQ, -1).astype(F32),
        cosine,
        sine,
        ready["visible"],
    )
    attended, saved = lax.optimization_barrier((attended.astype(B16), saved))
    projected = feat_part_sums(dot(tok_rows(attended), out_rows))
    middle = hidden_in + projected

    gained = feat_rows((middle * mlp_gain).astype(B16), first_core)

    def gate_up_product(rows):
        squares = jnp.sum(
            jnp.square(rows.astype(F32) * ready["mlp_unscaled"]), axis=1, keepdims=True
        )
        return jnp.concatenate(
            [dot(rows, gate_up_weight).astype(B16), split_column(masks, squares)], axis=1
        ).astype(F32)

    gate_up = tok_sums_core_first(gained, gate_up_product)
    scale_mlp = lax.rsqrt(joined_column(gate_up[:, 2 * hidden :]) / D + epsilon)
    gate_raw = gate_up[:, :hidden]
    up_raw = gate_up[:, hidden : 2 * hidden]
    gate_value = gate_raw * scale_mlp
    up_value = up_raw * scale_mlp
    sigmoid_gate = jax.nn.sigmoid(gate_value)
    grad_gate = back_rows * up_value * sigmoid_gate * (1.0 + gate_value * (1.0 - sigmoid_gate))
    grad_up = back_rows * gate_value * sigmoid_gate
    grad_gate, grad_up = grad_gate.astype(B16), grad_up.astype(B16)
    meeting = jnp.sum(
        grad_gate.astype(F32) * gate_raw + grad_up.astype(F32) * up_raw, axis=1, keepdims=True
    )
    mlp_grads = jnp.concatenate(
        [grad_gate, grad_up, split_column(masks, scale_mlp, meeting)], axis=1
    )
    mlp_grads = both_cores(spread(mlp_grads, "x", NX), first_core, mlp_grads)
    back_second = feat_sums(
        jnp.concatenate(
            [
                dot_t(mlp_grads[:, : 2 * hidden], gate_up_weight).astype(B16),
                mlp_grads[:, 2 * hidden :],
            ],
            axis=1,
        )
    )
    extras = back_second[:, model_width:]
    scale_second = joined_column(extras) / (NY * NZ)
    total = joined_column(extras, 2)
    weighted_second = back_second[:, :model_width] * mlp_gain
    grad_middle = (
        ready["cot_rows"]
        + scale_second * weighted_second
        - middle * scale_second**3 * (total / D)
    )
    gathered = feat_part_rows(grad_middle.astype(B16))
    grad_attended = tok_sums(dot_t(gathered, out_rows))
    grad_query, grad_keyval = attend_back(grad_attended, saved)
    grad_keyval = grad_keyval.astype(B16).reshape(SEQ, NY, QUAD, kv_part)
    grad_keyval = added(swap(grad_keyval.transpose(2, 0, 1, 3).reshape(QUAD, SEQ, -1), "quad"))
    attn_grads = jnp.concatenate(
        [grad_query.reshape(SEQ, NY, head_part), grad_keyval.reshape(SEQ, NY, kv_part)], axis=2
    )
    attn_grads = attn_grads.reshape(SEQ, qkv_width).astype(B16)
    meeting = jnp.sum(
        attn_grads.astype(F32) * projections[:, :qkv_width], axis=1, keepdims=True
    )
    gathered = tok_rows(
        jnp.concatenate([attn_grads, split_column(masks, meeting, scale_rows)], axis=1)
    )
    back_first = feat_part_sums(
        jnp.concatenate(
            [
                dot(gathered[:, :qkv_width], turned_rows).astype(B16),
                gathered[:, qkv_width:],
            ],
            axis=1,
        )
    )
    extras = back_first[:, model_width:]
    total = joined_column(extras)
    scale_first = joined_column(extras, 2) / NZ
    weighted_first = back_first[:, :model_width] * attn_gain
    grad_hidden = (
        grad_middle
        + scale_first * weighted_first
        - hidden_in * scale_first**3 * (total / D)
    )
    gathered = feat_rows(grad_hidden.astype(B16), first_core)
    feature_grads = tok_sums_core_first(gathered, lambda rows: dot_t(rows, dec_weight))
    return jnp.sum((feature_grads * changes).reshape(POINTS, SEQ, width), axis=0)


def solution(mesh):
    fine = Mesh(mesh.devices.reshape(NY, NZ // QUAD, QUAD, NX, NC), FEAT + TOK)
    in_specs = (
        P(None, TOK),
        P(TOK, FEAT),
        P(FEAT),
        P(TOK, FEAT),
        P(FEAT, TOK),
        P(TOK),
        P(None, TOK),
        P(TOK, None),
        P(TOK),
        P(TOK, FEAT),
        P(TOK, FEAT),
        P(FEAT, TOK),
        P(TOK),
        P(TOK, FEAT),
        P(TOK, FEAT),
        P(FEAT, TOK),
        P(None, TOK),
    )
    return jax.shard_map(
        local, mesh=fine, in_specs=in_specs, out_specs=P(TOK, FEAT), check_vma=False
    )
```

time: 474 us -> 384 us (0.81)
  waiting for transfers between devices: 95 us -> 50.1 us
  starting transfers between devices: 69.8 us -> 42 us
  local copies, waits for them, and re-layouts: 22.2 us -> 7.74 us
  between operations: 1.11 us -> 14.7 us
  blocking collectives: 236 us -> 224 us
    all_to_all x10 -> x6, waiting for transfers between devices: 75.2 us -> 43.8 us  [swap(): return lax.all_to_all(blocks, axes, 0, 0, tiled=True)]
    all_to_all x10 -> x6, starting transfers between devices: 52.9 us -> 27.4 us  [swap(): return lax.all_to_all(blocks, axes, 0, 0, tiled=True)]
    ppermute x4 -> x1, waiting for transfers between devices: 13.3 us -> 0.01 us  [placed_block(): return lax.ppermute(block, FEAT, moves)]
    all_to_all x17, blocking collectives: 236 us -> 224 us  [swap(): return lax.all_to_all(blocks, axes, 0, 0, tiled=True)]
    concatenate x6 -> x19, other arithmetic: 2.43 us -> 10.9 us  [the longest x1 3.32 us: local(): gate_up_weight = jnp.concatenate([gate_weight, up_weight], axis=1)]
    squeeze x5 -> x0, local copies, waits for them, and re-layouts: 7.14 us -> none  [own_keyval_weight(): lax.dynamic_index_in_dim(parts, lax.rem(group - kind + 4, 4), 0, keepdims...]
    concatenate x3 -> x8, local copies, waits for them, and re-layouts: 7.53 us -> 0.64 us  [the longest x2 0.25 us: attend(): jnp.concatenate([table] * (width // HD), axis=0)]
    dot_general x6 -> x8, matrix products: 6.64 us -> 10.7 us  [dot_t(): lax.dot_general(left_side, right_side, (((1,), (1,)), ((), ())), preferre...]
  transfers between devices with their start and end apart: 18 -> 13, of which waited for: 15 -> 10; matrix products, arithmetic and copies ran while one was open for 3% -> 6% of each run, Pallas kernels for 0% -> 0%
where the time goes in v2:
time: 384 us; the launch traced here: 382 us
  blocking collectives  224 us (58%)
  waiting for transfers between devices  50.1 us (13%)
  starting transfers between devices  42 us (11%)
  other arithmetic  22 us (6%)
  matrix products  21.4 us (6%)
  between operations  14.7 us (4%)
  local copies, waits for them, and re-layouts  7.74 us (2%)
    all_to_all x17, blocking collectives, swap(): return lax.all_to_all(blocks, axes, 0, 0, tiled=True)  224 us
    all_to_all x6, waiting for transfers between devices, swap(): return lax.all_to_all(blocks, axes, 0, 0, tiled=True)  43.8 us
    all_to_all x6, starting transfers between devices, swap(): return lax.all_to_all(blocks, axes, 0, 0, tiled=True)  27.4 us
    ppermute x4, starting transfers between devices, other_core(): return lax.ppermute(values, 'c', [(0, 1), (1, 0)])  13.8 us
    dot_general x8, matrix products, dot_t(): lax.dot_general(left_side, right_side, (((1,), (1,)), ((), ())), preferre...  10.7 us
    dot_general x6, matrix products, dot(): return jnp.dot(left_side, right_side, preferred_element_type=F32)  8.53 us
  transfers between devices with their start and end apart: 13, of which 10 were waited for; matrix products, arithmetic and copies ran while one was open for 6% of the time, Pallas kernels for 0%

profile of v2, /device:TPU:1, one launch (start us, length us, event | category | flops | bytes accessed | tf_op | source)
XLA Modules:
  0.0 382.2 jit_solution(2826601582160114140)
XLA Ops:
  6.5 1.2 convolution_convert_fusion.11
  7.8 0.8 collective-permute-start.1
  8.6 1.4 convolution_convert_fusion.6
  10.0 1.8 convolution_convert_fusion.12
  12.4 0.9 pad_maximum_fusion.4
  13.4 0.8 pad_maximum_fusion.6
  14.2 6.6 %all-to-all-start = ((bf16[8,16,1664]{2,1,0:T(8,128)(2,1)}), bf16[8,16,1664]{2,1,0:T(8,128)(2,1)S(1)}, u32[]{:S(2)}, u32[]{:S(2)}) async-start(bf16[8,16,1664]{2,1,0:T(8,128)(2,1)} %pad_maximum_fusion.6), calls=%async_computation | async-start | bytes 851968 | tf_op jit(solution)/shard_map/all_to_all | solution.py:45
  20.8 1.4 dynamic-slice_convert_fusion
  22.3 7.0 %all-to-all-done = bf16[8,16,1664]{2,1,0:T(8,128)(2,1)S(1)} async-done(((bf16[8,16,1664]{2,1,0:T(8,128)(2,1)}), bf16[8,16,1664]{2,1,0:T(8,128)(2,1)S(1)}, u32[]{:S(2)}, u32[]{:S(2)}) %all-to-all-start) | async-done | bytes 426016 | tf_op jit(solution)/shard_map/all_to_all | solution.py:45
  30.2 0.9 broadcast_in_dim.286
  31.1 3.5 all-to-all-start.1
  34.5 1.0 pad_maximum_fusion.12
  35.5 1.6 pad_maximum_fusion.11
  37.2 3.3 pad_maximum_fusion
  40.8 2.4 all-to-all-done.1
  43.2 1.8 collective-permute-start
  44.9 1.5 collective-permute-done
  46.7 2.2 convolution_convert_fusion.2
  48.9 3.5 all-to-all-start.2
  53.2 20.1 %all-to-all-done.2 = bf16[4,128,1024]{2,1,0:T(8,128)(2,1)S(1)} async-done(((bf16[4,128,1024]{2,1,0:T(8,128)(2,1)}), bf16[4,128,1024]{2,1,0:T(8,128)(2,1)S(1)}, u32[]{:S(2)}, u32[]{:S(2)}) %all-to-all-start.2) | async-done | bytes 1048608 | tf_op jit(solution)/shard_map/all_to_all | solution.py:45
  73.5 18.1 %all_to_all.115 = bf16[8,16,1024]{2,1,0:T(8,128)(2,1)S(1)} all-to-all(bf16[8,16,1024]{2,1,0:T(8,128)(2,1)S(1)} %bitcast.122), channel_id=1, replica_groups=mesh['y'=4,'half'=2,'quad'=4,'x'=4,'c'=2] {'half','quad'}, dimensions={0} | all-to-all | bytes 524288 | tf_op jit(solution)/shard_map/all_to_all | solution.py:45
  91.6 0.9 multiply_convert_fusion.3
  92.5 12.4 %all_to_all.116 = bf16[8,16,1024]{2,1,0:T(8,128)(2,1)S(1)} all-to-all(bf16[8,16,1024]{2,1,0:T(8,128)(2,1)S(1)} %broadcast_in_dim.287), channel_id=1, replica_groups=mesh['y'=4,'half'=2,'quad'=4,'x'=4,'c'=2] {'half','quad'}, dimensions={0} | all-to-all | bytes 524288 | tf_op jit(solution)/shard_map/all_to_all | solution.py:45
  105.2 2.7 convolution_convert_fusion
  108.0 0.8 pad_maximum_fusion.8
  108.8 7.2 %all-to-all-start.5 = ((bf16[8,16,1408]{2,1,0:T(8,128)(2,1)}), bf16[8,16,1408]{2,1,0:T(8,128)(2,1)S(1)}, u32[]{:S(2)}, u32[]{:S(2)}) async-start(bf16[8,16,1408]{2,1,0:T(8,128)(2,1)} %bitcast.18), calls=%async_computation.5 | async-start | bytes 720896 | tf_op jit(solution)/shard_map/all_to_all | solution.py:45
  116.3 7.5 %all-to-all-done.5 = bf16[8,16,1408]{2,1,0:T(8,128)(2,1)S(1)} async-done(((bf16[8,16,1408]{2,1,0:T(8,128)(2,1)}), bf16[8,16,1408]{2,1,0:T(8,128)(2,1)S(1)}, u32[]{:S(2)}, u32[]{:S(2)}) %all-to-all-start.5) | async-done | bytes 360480 | tf_op jit(solution)/shard_map/all_to_all | solution.py:45
  123.8 0.8 fusion.20
  125.5 3.3 all-to-all-start.6
  129.9 3.4 all-to-all-done.6
  133.9 0.7 pad_maximum_fusion.21
  135.3 1.0 fusion.46
  136.9 10.9 %all_to_all.117 = bf16[8,16,1024]{2,1,0:T(8,128)(2,1)S(1)} all-to-all(bf16[8,16,1024]{2,1,0:T(8,128)(2,1)S(1)} %broadcast_in_dim.298), channel_id=1, replica_groups=mesh['y'=4,'half'=2,'quad'=4,'x'=4,'c'=2] {'x','c'}, dimensions={0} | all-to-all | bytes 524288 | tf_op jit(solution)/shard_map/all_to_all | solution.py:45
  148.3 12.6 %all_to_all.118 = bf16[8,16,1024]{2,1,0:T(8,128)(2,1)S(1)} all-to-all(bf16[8,16,1024]{2,1,0:T(8,128)(2,1)S(1)} %bitcast.124), channel_id=1, replica_groups=mesh['y'=4,'half'=2,'quad'=4,'x'=4,'c'=2] {'half','quad'}, dimensions={0} | all-to-all | bytes 524288 | tf_op jit(solution)/shard_map/all_to_all | solution.py:45
  161.6 12.0 %all_to_all.119 = bf16[8,16,1024]{2,1,0:T(8,128)(2,1)S(1)} all-to-all(bf16[8,16,1024]{2,1,0:T(8,128)(2,1)S(1)} %broadcast_in_dim.299), channel_id=1, replica_groups=mesh['y'=4,'half'=2,'quad'=4,'x'=4,'c'=2] {'half','quad'}, dimensions={0} | all-to-all | bytes 524288 | tf_op jit(solution)/shard_map/all_to_all | solution.py:45
  173.8 13.8 %all_to_all.120 = bf16[4,128,1024]{2,1,0:T(8,128)(2,1)S(1)} all-to-all(bf16[4,128,1024]{2,1,0:T(8,128)(2,1)S(1)} %broadcast_in_dim.301), channel_id=1, replica_groups=mesh['y'=4,'half'=2,'quad'=4,'x'=4,'c'=2] {'y'}, dimensions={0} | all-to-all | bytes 2097152 | tf_op jit(solution)/shard_map/all_to_all | solution.py:45
  187.6 0.9 fusion.40
  189.0 2.4 convolution_convert_fusion.4
  191.7 4.8 %collective-permute-start.2 = (bf16[256,1152]{1,0:T(8,128)(2,1)S(1)}, bf16[256,1152]{1,0:T(8,128)(2,1)S(1)}, u32[]{:S(2)}, u32[]{:S(2)}) collective-permute-start(bf16[256,1152]{1,0:T(8,128)(2,1)S(1)} %pad_maximum_fusion.5), channel_id=1, source_target_pairs={{0,1},{1,0},{2,3},{3,2},{4,5},{5,4},{6,7},{7,6},{8,9},{9,8},{10,11... | collective-permute-start | bytes 1769480 | tf_op jit(solution)/shard_map/ppermute | solution.py:78
  197.3 0.9 collective-permute-done.2
  198.4 12.2 %all_to_all.121 = bf16[4,64,1152]{2,1,0:T(8,128)(2,1)S(1)} all-to-all(bf16[4,64,1152]{2,1,0:T(8,128)(2,1)S(1)} %bitcast.106), channel_id=1, replica_groups=mesh['y'=4,'half'=2,'quad'=4,'x'=4,'c'=2] {'x'}, dimensions={0} | all-to-all | bytes 1179648 | tf_op jit(solution)/shard_map/all_to_all | solution.py:45
  211.8 11.1 %all_to_all.122 = bf16[4,64,1152]{2,1,0:T(8,128)(2,1)S(1)} all-to-all(bf16[4,64,1152]{2,1,0:T(8,128)(2,1)S(1)} %broadcast_in_dim.321), channel_id=1, replica_groups=mesh['y'=4,'half'=2,'quad'=4,'x'=4,'c'=2] {'x'}, dimensions={0} | all-to-all | bytes 1179648 | tf_op jit(solution)/shard_map/all_to_all | solution.py:45
  222.9 2.4 collective-permute-start.3
  225.3 1.6 collective-permute-done.3
  227.2 1.3 convolution_convert_fusion.1
  228.6 18.7 %all_to_all.123 = bf16[4,128,1152]{2,1,0:T(8,128)(2,1)S(1)} all-to-all(bf16[4,128,1152]{2,1,0:T(8,128)(2,1)S(1)} %bitcast.104), channel_id=1, replica_groups=mesh['y'=4,'half'=2,'quad'=4,'x'=4,'c'=2] {'y'}, dimensions={0} | all-to-all | bytes 2359296 | tf_op jit(solution)/shard_map/all_to_all | solution.py:45
  247.3 0.9 reduce_sum.206
  248.3 14.1 %all_to_all.124 = bf16[8,16,1152]{2,1,0:T(8,128)(2,1)S(1)} all-to-all(bf16[8,16,1152]{2,1,0:T(8,128)(2,1)} %bitcast.116), channel_id=1, replica_groups=mesh['y'=4,'half'=2,'quad'=4,'x'=4,'c'=2] {'half','quad'}, dimensions={0} | all-to-all | bytes 589824 | tf_op jit(solution)/shard_map/all_to_all | solution.py:45
  262.6 1.0 fusion.35
  263.6 12.7 %all_to_all.125 = bf16[8,16,1024]{2,1,0:T(8,128)(2,1)S(1)} all-to-all(bf16[8,16,1024]{2,1,0:T(8,128)(2,1)S(1)} %broadcast_in_dim.322), channel_id=1, replica_groups=mesh['y'=4,'half'=2,'quad'=4,'x'=4,'c'=2] {'half','quad'}, dimensions={0} | all-to-all | bytes 524288 | tf_op jit(solution)/shard_map/all_to_all | solution.py:45
  276.3 0.8 convolution_convert_fusion.7
  277.2 12.4 %all_to_all.126 = bf16[8,16,1024]{2,1,0:T(8,128)(2,1)S(1)} all-to-all(bf16[8,16,1024]{2,1,0:T(8,128)(2,1)S(1)} %bitcast.121), channel_id=1, replica_groups=mesh['y'=4,'half'=2,'quad'=4,'x'=4,'c'=2] {'x','c'}, dimensions={0} | all-to-all | bytes 524288 | tf_op jit(solution)/shard_map/all_to_all | solution.py:45
  292.1 3.3 all-to-all-start.17
  296.3 3.5 all-to-all-done.17
  300.3 12.3 %all_to_all.127 = bf16[8,16,1408]{2,1,0:T(8,128)(2,1)S(1)} all-to-all(bf16[8,16,1408]{2,1,0:T(8,128)(2,1)S(1)} %broadcast_in_dim.334), channel_id=1, replica_groups=mesh['y'=4,'half'=2,'quad'=4,'x'=4,'c'=2] {'x','c'}, dimensions={0} | all-to-all | bytes 720896 | tf_op jit(solution)/shard_map/all_to_all | solution.py:45
  312.7 2.2 convolution_convert_fusion.10
  315.0 13.3 %all_to_all.128 = bf16[8,16,1152]{2,1,0:T(8,128)(2,1)S(1)} all-to-all(bf16[8,16,1152]{2,1,0:T(8,128)(2,1)S(1)} %bitcast.115), channel_id=1, replica_groups=mesh['y'=4,'half'=2,'quad'=4,'x'=4,'c'=2] {'half','quad'}, dimensions={0} | all-to-all | bytes 589824 | tf_op jit(solution)/shard_map/all_to_all | solution.py:45
  328.6 12.5 %all_to_all.129 = bf16[8,16,1024]{2,1,0:T(8,128)(2,1)S(1)} all-to-all(bf16[8,16,1024]{2,1,0:T(8,128)(2,1)S(1)} %broadcast_in_dim.335), channel_id=1, replica_groups=mesh['y'=4,'half'=2,'quad'=4,'x'=4,'c'=2] {'half','quad'}, dimensions={0} | all-to-all | bytes 524288 | tf_op jit(solution)/shard_map/all_to_all | solution.py:45
  341.3 13.7 %all_to_all.130 = bf16[4,128,1024]{2,1,0:T(8,128)(2,1)S(1)} all-to-all(bf16[4,128,1024]{2,1,0:T(8,128)(2,1)S(1)} %broadcast_in_dim.337), channel_id=1, replica_groups=mesh['y'=4,'half'=2,'quad'=4,'x'=4,'c'=2] {'y'}, dimensions={0} | all-to-all | bytes 2097152 | tf_op jit(solution)/shard_map/all_to_all | solution.py:45
  355.1 0.7 convolution_convert_fusion.3
  355.9 4.8 %collective-permute-start.4 = (bf16[256,1024]{1,0:T(8,128)(2,1)S(1)}, bf16[256,1024]{1,0:T(8,128)(2,1)S(1)}, u32[]{:S(2)}, u32[]{:S(2)}) collective-permute-start(bf16[256,1024]{1,0:T(8,128)(2,1)S(1)} %convolution_convert_fusion.3), channel_id=1, source_target_pairs={{0,1},{1,0},{2,3},{3,2},{4,5},{5,4},{6,7},{7,6},{8,9},{9,8},{10,11... | collective-permute-start | bytes 1572872 | tf_op jit(solution)/shard_map/ppermute | solution.py:78
  360.7 1.5 collective-permute-done.4
  362.2 0.7 add_convert_fusion.1
  363.0 11.6 %all_to_all.131 = bf16[4,64,1024]{2,1,0:T(8,128)(2,1)S(1)} all-to-all(bf16[4,64,1024]{2,1,0:T(8,128)(2,1)S(1)} %bitcast.133), channel_id=1, replica_groups=mesh['y'=4,'half'=2,'quad'=4,'x'=4,'c'=2] {'x'}, dimensions={0} | all-to-all | bytes 1048576 | tf_op jit(solution)/shard_map/all_to_all | solution.py:45
  (235 shorter events, 17.4 us)
Async XLA Ops:
  6.5 40.1 %copy-start = (bf16[1024,1024]{1,0:T(8,128)(2,1)S(1)}, bf16[1024,1024]{1,0:T(8,128)(2,1)}, u32[]{:S(2)}) copy-start(bf16[1024,1024]{1,0:T(8,128)(2,1)} %param.27) | copy-start | bytes 6291460
  6.5 5.3 %copy-start.13 = (bf16[128,1024]{1,0:T(8,128)(2,1)S(1)}, bf16[128,1024]{1,0:T(8,128)(2,1)}, u32[]{:S(2)}) copy-start(bf16[128,1024]{1,0:T(8,128)(2,1)} %param.23) | copy-start | bytes 786436
  6.5 98.7 %all-gather.3.cloned.1.call-start = ((), (), s32[]{:S(2)}) async-start(), calls=%async_computation.23 | async-start | bytes 3276800 | tf_op jit(solution)/shard_map/all_gather | solution.py:242
  6.5 5.3 %copy-start.3 = (bf16[1024,1024]{1,0:T(8,128)(2,1)S(1)}, bf16[1024,1024]{1,0:T(8,128)(2,1)}, u32[]{:S(2)}) copy-start(bf16[1024,1024]{1,0:T(8,128)(2,1)} %param.24) | copy-start | bytes 6291460
  7.8 4.6 %collective-permute-start.1 = (bf16[64,1024]{1,0:T(8,128)(2,1)S(1)}, bf16[64,1024]{1,0:T(8,128)(2,1)S(1)}, u32[]{:S(2)}, u32[]{:S(2)}) collective-permute-start(bf16[64,1024]{1,0:T(8,128)(2,1)S(1)} %convolution_convert_fusion.11), channel_id=1, source_target_pairs={{0,0},{8,8},{16,32},{24,40},{32,16},{40,24},{48,48},{56,56},{64,64... | collective-permute-start | bytes 393224 | tf_op jit(solution)/shard_map/ppermute | solution.py:176
  10.0 2.3 copy-start.31
  12.3 8.5 %copy-start.16 = (s32[64,1024]{1,0:T(8,128)S(1)}, s32[64,1024]{1,0:T(8,128)}, u32[]{:S(2)}) copy-start(s32[64,1024]{1,0:T(8,128)} %param.26) | copy-start | bytes 786436
  12.3 9.9 %copy-start.19 = (f32[1024]{0:T(1024)S(1)}, f32[1024]{0:T(1024)}, u32[]{:S(2)}) copy-start(f32[1024]{0:T(1024)} %param.35) | copy-start | bytes 12292
  12.3 9.9 %copy-start.21 = (f32[1024]{0:T(1024)S(1)}, f32[1024]{0:T(1024)}, u32[]{:S(2)}) copy-start(f32[1024]{0:T(1024)} %param.31) | copy-start | bytes 12292
  13.3 16.0 %copy-start.20 = (f32[1024]{0:T(1024)S(1)}, f32[1024]{0:T(1024)}, u32[]{:S(2)}) copy-start(f32[1024]{0:T(1024)} %param.25) | copy-start | bytes 12292
  14.2 15.1 %all-to-all-start = ((bf16[8,16,1664]{2,1,0:T(8,128)(2,1)}), bf16[8,16,1664]{2,1,0:T(8,128)(2,1)S(1)}, u32[]{:S(2)}, u32[]{:S(2)}) async-start(bf16[8,16,1664]{2,1,0:T(8,128)(2,1)} %pad_maximum_fusion.6), calls=%async_computation | async-start | bytes 851968 | tf_op jit(solution)/shard_map/all_to_all | solution.py:45
  31.1 12.1 %all-to-all-start.1 = ((bf16[4,64,1024]{2,1,0:T(8,128)(2,1)}), bf16[4,64,1024]{2,1,0:T(8,128)(2,1)S(1)}, u32[]{:S(2)}, u32[]{:S(2)}) async-start(bf16[4,64,1024]{2,1,0:T(8,128)(2,1)} %broadcast_in_dim.286), calls=%async_computation.1 | async-start | bytes 1048576 | tf_op jit(solution)/shard_map/all_to_all | solution.py:45
  37.2 3.3 copy-start.30
  43.2 3.3 collective-permute-start
  48.9 24.4 %all-to-all-start.2 = ((bf16[4,128,1024]{2,1,0:T(8,128)(2,1)}), bf16[4,128,1024]{2,1,0:T(8,128)(2,1)S(1)}, u32[]{:S(2)}, u32[]{:S(2)}) async-start(bf16[4,128,1024]{2,1,0:T(8,128)(2,1)} %bitcast.127), calls=%async_computation.2 | async-start | bytes 2097152 | tf_op jit(solution)/shard_map/all_to_all | solution.py:45
  52.4 52.7 %copy-start.22 = (pred[1,128]{1,0:T(4,128)(4,1)S(1)}, pred[1,128]{1,0:T(4,128)(4,1)}, u32[]{:S(2)}) copy-start(pred[1,128]{1,0:T(4,128)(4,1)} %constant.113.clone) | copy-start | bytes 388
  52.4 52.7 %copy-start.23 = (pred[1,128]{1,0:T(4,128)(4,1)S(1)}, pred[1,128]{1,0:T(4,128)(4,1)}, u32[]{:S(2)}) copy-start(pred[1,128]{1,0:T(4,128)(4,1)} %constant.114.clone) | copy-start | bytes 388
  52.4 71.4 %all-gather.5.cloned.1.call-start = ((), (), s32[]{:S(2)}) async-start(), calls=%async_computation.24 | async-start | bytes 2621440 | tf_op jit(solution)/shard_map/all_gather | solution.py:270
  108.8 15.0 %all-to-all-start.5 = ((bf16[8,16,1408]{2,1,0:T(8,128)(2,1)}), bf16[8,16,1408]{2,1,0:T(8,128)(2,1)S(1)}, u32[]{:S(2)}, u32[]{:S(2)}) async-start(bf16[8,16,1408]{2,1,0:T(8,128)(2,1)} %bitcast.18), calls=%async_computation.5 | async-start | bytes 720896 | tf_op jit(solution)/shard_map/all_to_all | solution.py:45
  116.1 17.5 %copy-start.9 = (f32[128,64]{0,1:T(8,128)}, f32[128,64]{0,1:T(8,128)S(1)}, u32[]{:S(2)}) copy-start(f32[128,64]{0,1:T(8,128)S(1)} %concatenate.108) | copy-start | bytes 98308
  116.3 17.4 %copy-start.11 = (f32[128,64]{0,1:T(8,128)}, f32[128,64]{0,1:T(8,128)S(1)}, u32[]{:S(2)}) copy-start(f32[128,64]{0,1:T(8,128)S(1)} %concatenate.109) | copy-start | bytes 98308
  125.5 7.7 %all-to-all-start.6 = ((bf16[4,16,256]{2,1,0:T(8,128)(2,1)}), bf16[4,16,256]{2,1,0:T(8,128)(2,1)S(1)}, u32[]{:S(2)}, u32[]{:S(2)}) async-start(bf16[4,16,256]{2,1,0:T(8,128)(2,1)} %broadcast_in_dim.296), calls=%async_computation.6 | async-start | bytes 65536 | tf_op jit(solution)/shard_map/all_to_all | solution.py:45
  133.6 14.2 %copy-start.1 = (bf16[1024,1024]{1,0:T(8,128)(2,1)S(1)}, bf16[1024,1024]{1,0:T(8,128)(2,1)}, u32[]{:S(2)}) copy-start(bf16[1024,1024]{1,0:T(8,128)(2,1)} %all-gather.5.cloned.1.call-done) | copy-start | bytes 6291460
  189.0 7.5 %copy-start.4 = (bf16[1024,1024]{1,0:T(8,128)(2,1)S(1)}, bf16[1024,1024]{1,0:T(8,128)(2,1)}, u32[]{:S(2)}) copy-start(bf16[1024,1024]{1,0:T(8,128)(2,1)} %pad_maximum_fusion) | copy-start | bytes 6291460
  189.0 7.5 %copy-start.8 = (bf16[4,1,64,1024]{3,2,1,0:T(8,128)(2,1)S(1)}, bf16[4,1,64,1024]{3,2,1,0:T(8,128)(2,1)}, u32[]{:S(2)}) copy-start(bf16[4,1,64,1024]{3,2,1,0:T(8,128)(2,1)} %get-tuple-element.101) | copy-start | bytes 1572868
  191.7 6.4 %collective-permute-start.2 = (bf16[256,1152]{1,0:T(8,128)(2,1)S(1)}, bf16[256,1152]{1,0:T(8,128)(2,1)S(1)}, u32[]{:S(2)}, u32[]{:S(2)}) collective-permute-start(bf16[256,1152]{1,0:T(8,128)(2,1)S(1)} %pad_maximum_fusion.5), channel_id=1, source_target_pairs={{0,1},{1,0},{2,3},{3,2},{4,5},{5,4},{6,7},{7,6},{8,9},{9,8},{10,11... | collective-permute-start | bytes 1769480 | tf_op jit(solution)/shard_map/ppermute | solution.py:78
  198.3 12.8 %copy-start.7 = (f32[64,512]{0,1:T(8,128)S(1)}, f32[64,512]{0,1:T(8,128)}, u32[]{:S(2)}) copy-start(f32[64,512]{0,1:T(8,128)} %pad_maximum_fusion.12) | copy-start | bytes 393220
  198.3 13.0 %copy-start.24 = (pred[1,128]{1,0:T(4,128)(4,1)S(1)}, pred[1,128]{1,0:T(4,128)(4,1)}, u32[]{:S(2)}) copy-start(pred[1,128]{1,0:T(4,128)(4,1)} %constant.115.clone) | copy-start | bytes 388
  198.4 13.0 %copy-start.26 = (pred[1,128]{1,0:T(4,128)(4,1)S(1)}, pred[1,128]{1,0:T(4,128)(4,1)}, u32[]{:S(2)}) copy-start(pred[1,128]{1,0:T(4,128)(4,1)} %constant.116.clone) | copy-start | bytes 388
  222.9 4.3 %copy-start.5 = (bf16[1024,1024]{1,0:T(8,128)(2,1)S(1)}, bf16[1024,1024]{1,0:T(8,128)(2,1)}, u32[]{:S(2)}) copy-start(bf16[1024,1024]{1,0:T(8,128)(2,1)} %pad_maximum_fusion) | copy-start | bytes 6291460
  222.9 4.0 %collective-permute-start.3 = (bf16[4,64,1152]{2,1,0:T(8,128)(2,1)S(1)}, bf16[4,64,1152]{2,1,0:T(8,128)(2,1)S(1)}, u32[]{:S(2)}, u32[]{:S(2)}) collective-permute-start(bf16[4,64,1152]{2,1,0:T(8,128)(2,1)S(1)} %all_to_all.122), channel_id=1, source_target_pairs={{0,1},{1,0},{2,3},{3,2},{4,5},{5,4},{6,7},{7,6},{8,9},{9,8},{10,11... | collective-permute-start | bytes 1769480 | tf_op jit(solution)/shard_map/ppermute | solution.py:78
  248.2 28.0 %copy-start.2 = (bf16[1024,1024]{1,0:T(8,128)(2,1)S(1)}, bf16[1024,1024]{1,0:T(8,128)(2,1)}, u32[]{:S(2)}) copy-start(bf16[1024,1024]{1,0:T(8,128)(2,1)} %all-gather.5.cloned.1.call-done) | copy-start | bytes 6291460
  263.6 26.6 %copy-start.14 = (f32[128,128]{0,1:T(8,128)S(1)}, f32[128,128]{0,1:T(8,128)}, u32[]{:S(2)}) copy-start(f32[128,128]{0,1:T(8,128)} %pad_maximum_fusion.14) | copy-start | bytes 196612
  276.3 14.1 %copy-start.15 = (f32[64,128]{0,1:T(8,128)S(1)}, f32[64,128]{0,1:T(8,128)}, u32[]{:S(2)}) copy-start(f32[64,128]{0,1:T(8,128)} %pad_maximum_fusion.16) | copy-start | bytes 98308
  276.3 14.3 %copy-start.17 = (f32[64,64]{0,1:T(8,128)S(1)}, f32[64,64]{0,1:T(8,128)}, u32[]{:S(2)}) copy-start(f32[64,64]{0,1:T(8,128)} %get-tuple-element.67) | copy-start | bytes 49156
  276.3 14.4 %copy-start.18 = (f32[64,64]{0,1:T(8,128)S(1)}, f32[64,64]{0,1:T(8,128)}, u32[]{:S(2)}) copy-start(f32[64,64]{0,1:T(8,128)} %get-tuple-element.66) | copy-start | bytes 49156
  276.3 19.1 %copy-start.10 = (f32[128,64]{0,1:T(8,128)S(1)}, f32[128,64]{0,1:T(8,128)}, u32[]{:S(2)}) copy-start(f32[128,64]{0,1:T(8,128)} %copy-done.9) | copy-start | bytes 98308
  276.3 19.1 %copy-start.12 = (f32[128,64]{0,1:T(8,128)S(1)}, f32[128,64]{0,1:T(8,128)}, u32[]{:S(2)}) copy-start(f32[128,64]{0,1:T(8,128)} %copy-done.11) | copy-start | bytes 98308
  277.1 23.1 %copy-start.25 = (pred[1,128]{1,0:T(4,128)(4,1)S(1)}, pred[1,128]{1,0:T(4,128)(4,1)}, u32[]{:S(2)}) copy-start(pred[1,128]{1,0:T(4,128)(4,1)} %constant.115.clone) | copy-start | bytes 388
  277.1 23.0 %copy-start.27 = (pred[1,128]{1,0:T(4,128)(4,1)S(1)}, pred[1,128]{1,0:T(4,128)(4,1)}, u32[]{:S(2)}) copy-start(pred[1,128]{1,0:T(4,128)(4,1)} %constant.116.clone) | copy-start | bytes 388
  277.2 23.0 %copy-start.28 = (bf16[16]{0:T(256)(128)(2,1)S(1)}, bf16[16]{0:T(256)(128)(2,1)}, u32[]{:S(2)}) copy-start(bf16[16]{0:T(256)(128)(2,1)} %get-tuple-element.74) | copy-start | bytes 100
  277.2 23.0 %copy-start.29 = (bf16[16]{0:T(256)(128)(2,1)S(1)}, bf16[16]{0:T(256)(128)(2,1)}, u32[]{:S(2)}) copy-start(bf16[16]{0:T(256)(128)(2,1)} %get-tuple-element.75) | copy-start | bytes 100
  292.1 7.7 %all-to-all-start.17 = ((bf16[4,16,256]{2,1,0:T(8,128)(2,1)}), bf16[4,16,256]{2,1,0:T(8,128)(2,1)S(1)}, u32[]{:S(2)}, u32[]{:S(2)}) async-start(bf16[4,16,256]{2,1,0:T(8,128)(2,1)} %reshape.260), calls=%async_computation.17 | async-start | bytes 65536 | tf_op jit(solution)/shard_map/all_to_all | solution.py:45
  355.9 6.4 %collective-permute-start.4 = (bf16[256,1024]{1,0:T(8,128)(2,1)S(1)}, bf16[256,1024]{1,0:T(8,128)(2,1)S(1)}, u32[]{:S(2)}, u32[]{:S(2)}) collective-permute-start(bf16[256,1024]{1,0:T(8,128)(2,1)S(1)} %convolution_convert_fusion.3), channel_id=1, source_target_pairs={{0,1},{1,0},{2,3},{3,2},{4,5},{5,4},{6,7},{7,6},{8,9},{9,8},{10,11... | collective-permute-start | bytes 1572872 | tf_op jit(solution)/shard_map/ppermute | solution.py:78
  362.2 12.5 %copy-start.6 = (f32[64,1024]{1,0:T(8,128)S(1)}, f32[64,1024]{1,0:T(8,128)}, u32[]{:S(2)}) copy-start(f32[64,1024]{1,0:T(8,128)} %pad_maximum_fusion.11) | copy-start | bytes 786436
Sparse Core Ops, SparseCore 0:
  13.4 53.7 all-gather.2
  69.0 33.0 all-gather.4

commit v3 on v2

--- a/solution.py
+++ b/solution.py
@@ -81,11 +81,15 @@
 def tok_sums_core_first(rows, product):
     blocks = rows.reshape(NX, NC, -1, rows.shape[-1])
     height = blocks.shape[2]
-    other = product(blocks[:, 1].reshape(NX * height, -1))
-    received = other_core(other.astype(B16))
-    own = product(blocks[:, 0].reshape(NX * height, -1))
-    own = (own + received.astype(F32)).astype(B16)
-    return added(swap(own.reshape(NX, height, -1), "x"))
+    if height == SEQ:
+        sums = product(rows).astype(B16).reshape(NX, NC, height, -1)
+        own, other = sums[:, 0], sums[:, 1]
+    else:
+        other = product(blocks[:, 1].reshape(NX * height, -1)).astype(B16)
+        own = product(blocks[:, 0].reshape(NX * height, -1))
+    received = other_core(other).astype(F32).reshape(NX, height, -1)
+    own = (own.astype(F32).reshape(NX, height, -1) + received).astype(B16)
+    return added(swap(own, "x"))
 
 
 def tok_rows(piece):
@@ -131,13 +135,8 @@
     return jnp.concatenate([values[h * SEQ : (h + 1) * SEQ] for h in range(heads)], axis=1)
 
 
-def attend(query_rows, keyval_rows, cosine, sine, visible):
+def attend(query_rows, keyval_rows, tables, visible):
     half = keyval_rows.shape[1] // 2
-    tables = [
-        jnp.concatenate([table] * (width // HD), axis=0)
-        for width in (query_rows.shape[1], half)
-        for table in (cosine, sine)
-    ]
     queries = rotate(stacked_heads(query_rows), tables[0], tables[1])
     keys = rotate(stacked_heads(keyval_rows[:, :half]), tables[2], tables[3])
     values = stacked_heads(keyval_rows[:, half:])
@@ -184,6 +183,7 @@
     visible = (row[:, None] // (2 * SEQ) == key // SEQ) & (row[:, None] % SEQ >= key % SEQ)
     return dict(
         own_prompt=2 * lax.axis_index("y") + lax.axis_index(TOK) // POINTS,
+        late_prompt=lax.axis_index(TOK) // POINTS == 1,
         first_core=lax.axis_index("c") == 0,
         visible=jnp.asarray(visible),
         masks=[jnp.asarray(np.arange(128)[None, :] == lane) for lane in range(6)],
@@ -250,7 +250,11 @@
     ).astype(F32)
     frequency = (rope_base ** (-np.arange(HD // 2) * 2.0 / HD)).astype(np.float32)
     angles = own_positions[:, None] * frequency
-    cosine, sine = jnp.cos(angles), jnp.sin(angles)
+    tables = [
+        jnp.concatenate([table] * count, axis=0)
+        for count in (NZ, NY)
+        for table in (jnp.cos(angles), jnp.sin(angles))
+    ]
     encoded = first_sums[:, :width]
     back_hidden = first_sums[:, width:]
     features = [
@@ -258,16 +262,30 @@
     ]
     changes = [features[0]] + [features[k] - features[k - 1] for k in range(1, POINTS)]
     changes = jnp.concatenate(changes, axis=0)
-    sent_features = jnp.concatenate(features, axis=0).astype(B16)
-    own_rows = spread(sent_features, "x", NX)
-    back_rows = jnp.concatenate([back_hidden] * POINTS, axis=0)
-    gate_up_weight = jnp.concatenate([gate_weight, up_weight], axis=1)
-    own_rows, changes, back_rows, gate_up_weight, cosine, sine = lax.optimization_barrier(
-        (own_rows, changes, back_rows, gate_up_weight, cosine, sine)
-    )
-    gathered = both_cores(own_rows, first_core, sent_features)
-    decoded = feat_sums(dot(gathered, dec_weight))
+    sent_rows = jnp.concatenate(
+        features + [back_hidden.reshape(-1, width)], axis=0
+    ).astype(B16)
+    feature_rows = POINTS * SEQ
+    own_rows = spread(sent_rows, "x", NX)
+    gate_up_turned = jnp.concatenate([turned(gate_weight), turned(up_weight)], axis=0)
+    own_rows, changes, gate_up_turned, tables = lax.optimization_barrier(
+        (own_rows, changes, gate_up_turned, tables)
+    )
+    gathered = both_cores(own_rows, first_core, sent_rows).reshape((NX * NC,) + sent_rows.shape)
+    features = gathered[:, :feature_rows].reshape(-1, width)
+    back_hidden = gathered[:, feature_rows:].reshape(NY, -1, width)
+    decoded = dot(features, dec_weight).astype(B16).reshape(NY, -1, model_width)
+    blocks = swap(jnp.concatenate([decoded, back_hidden], axis=1), "y")
+    chunk_rows = decoded.shape[1]
+    back_hidden = blocks[:, chunk_rows:].reshape(NY, 2, SEQ, hidden)
+    back_hidden = jnp.where(ready["late_prompt"], back_hidden[:, 1], back_hidden[:, 0])
+    back_hidden = back_hidden.transpose(1, 0, 2).astype(F32)
+    decoded = added(blocks[:, :chunk_rows]).astype(B16).reshape(NZ, SEQ, model_width)
+    decoded, back_hidden = lax.optimization_barrier((decoded, back_hidden))
+    decoded = added(swap(decoded, Z))
     out_rows = lax.all_gather(out_weight, "y", axis=0, tiled=True)
+    decoded, gate_up_turned = lax.optimization_barrier((decoded, gate_up_turned))
+    gate_up_turned = lax.all_gather(gate_up_turned, "y", axis=0, tiled=True)
     hidden_in = decoded + dec_bias + ready["error_rows"]
 
     gained = feat_part_rows((hidden_in * attn_gain).astype(B16))
@@ -290,53 +308,56 @@
     attended, saved = attend(
         own_qkv[:, :, :head_part].reshape(SEQ, -1),
         keyval.transpose(1, 2, 0, 3).reshape(SEQ, -1).astype(F32),
-        cosine,
-        sine,
+        tables,
         ready["visible"],
     )
     attended, saved = lax.optimization_barrier((attended.astype(B16), saved))
     projected = feat_part_sums(dot(tok_rows(attended), out_rows))
     middle = hidden_in + projected
 
-    gained = feat_rows((middle * mlp_gain).astype(B16), first_core)
+    gained = feat_part_rows((middle * mlp_gain).astype(B16))
+    gained = gained.reshape(NX, NC, SEQ, model_width)
+    gained = jnp.where(first_core, gained, gained[:, ::-1])
 
     def gate_up_product(rows):
         squares = jnp.sum(
             jnp.square(rows.astype(F32) * ready["mlp_unscaled"]), axis=1, keepdims=True
         )
         return jnp.concatenate(
-            [dot(rows, gate_up_weight).astype(B16), split_column(masks, squares)], axis=1
+            [dot_t(rows, gate_up_turned).astype(B16), split_column(masks, squares)], axis=1
         ).astype(F32)
 
-    gate_up = tok_sums_core_first(gained, gate_up_product)
-    scale_mlp = lax.rsqrt(joined_column(gate_up[:, 2 * hidden :]) / D + epsilon)
-    gate_raw = gate_up[:, :hidden]
-    up_raw = gate_up[:, hidden : 2 * hidden]
-    gate_value = gate_raw * scale_mlp
-    up_value = up_raw * scale_mlp
+    gate_up = tok_sums_core_first(gained.reshape(-1, model_width), gate_up_product)
+    scale_mlp = lax.rsqrt(joined_column(gate_up[:, NY * 2 * hidden :]) / D + epsilon)
+    gate_up = gate_up[:, : NY * 2 * hidden].reshape(SEQ, NY, 2 * hidden)
+    gate_raw = gate_up[:, :, :hidden]
+    up_raw = gate_up[:, :, hidden:]
+    gate_value = gate_raw * scale_mlp[:, :, None]
+    up_value = up_raw * scale_mlp[:, :, None]
     sigmoid_gate = jax.nn.sigmoid(gate_value)
-    grad_gate = back_rows * up_value * sigmoid_gate * (1.0 + gate_value * (1.0 - sigmoid_gate))
-    grad_up = back_rows * gate_value * sigmoid_gate
+    grad_gate = back_hidden * up_value * sigmoid_gate * (1.0 + gate_value * (1.0 - sigmoid_gate))
+    grad_up = back_hidden * gate_value * sigmoid_gate
     grad_gate, grad_up = grad_gate.astype(B16), grad_up.astype(B16)
     meeting = jnp.sum(
-        grad_gate.astype(F32) * gate_raw + grad_up.astype(F32) * up_raw, axis=1, keepdims=True
-    )
-    mlp_grads = jnp.concatenate(
-        [grad_gate, grad_up, split_column(masks, scale_mlp, meeting)], axis=1
-    )
+        grad_gate.astype(F32) * gate_raw + grad_up.astype(F32) * up_raw, axis=(1, 2)
+    )[:, None]
+    mlp_grads = jnp.concatenate([grad_gate, grad_up], axis=2).reshape(SEQ, -1)
+    mlp_grads = jnp.concatenate([mlp_grads, split_column(masks, scale_mlp, meeting)], axis=1)
     mlp_grads = both_cores(spread(mlp_grads, "x", NX), first_core, mlp_grads)
-    back_second = feat_sums(
+    mlp_width = NY * 2 * hidden
+    back_second = feat_part_sums(
         jnp.concatenate(
             [
-                dot_t(mlp_grads[:, : 2 * hidden], gate_up_weight).astype(B16),
-                mlp_grads[:, 2 * hidden :],
+                dot(mlp_grads[:, :mlp_width], gate_up_turned).astype(B16),
+                mlp_grads[:, mlp_width:],
             ],
             axis=1,
         )
     )
     extras = back_second[:, model_width:]
-    scale_second = joined_column(extras) / (NY * NZ)
+    scale_second = joined_column(extras) / NZ
     total = joined_column(extras, 2)
+
     weighted_second = back_second[:, :model_width] * mlp_gain
     grad_middle = (
         ready["cot_rows"]

time: 384 us -> 372 us (0.969)
  waiting for transfers between devices: 50.1 us -> 33.4 us
  starting transfers between devices: 42 us -> 28.3 us
  blocking collectives: 224 us -> 236 us
  matrix products: 21.4 us -> 29.2 us
  other arithmetic: 22 us -> 15.8 us
  local copies, waits for them, and re-layouts: 7.74 us -> 13.4 us
    all_to_all x6 -> x4, waiting for transfers between devices: 43.8 us -> 15.8 us  [swap(): return lax.all_to_all(blocks, axes, 0, 0, tiled=True)]
    all_gather x0 -> x1, waiting for transfers between devices: none -> 11.8 us  [local(): gate_up_turned = lax.all_gather(gate_up_turned, 'y', axis=0, tiled=True)]
    all_to_all x17, blocking collectives: 224 us -> 236 us  [swap(): return lax.all_to_all(blocks, axes, 0, 0, tiled=True)]
    all_to_all x6 -> x4, starting transfers between devices: 27.4 us -> 17.2 us  [swap(): return lax.all_to_all(blocks, axes, 0, 0, tiled=True)]
    dot_general x8 -> x10, matrix products: 10.7 us -> 18.5 us  [dot_t(): lax.dot_general(left_side, right_side, (((1,), (1,)), ((), ())), preferre...]
    dot_general x6 -> x5, matrix products: 8.53 us -> 9.22 us  [dot(): return jnp.dot(left_side, right_side, preferred_element_type=F32)]
  transfers between devices with their start and end apart: 13 -> 12, of which waited for: 10 -> 9; matrix products, arithmetic and copies ran while one was open for 6% -> 9% of each run, Pallas kernels for 0% -> 0%
where the time goes in v3:
time: 372 us; the launch traced here: 371 us
  blocking collectives  236 us (63%)
  waiting for transfers between devices  33.4 us (9%)
  matrix products  29.2 us (8%)
  starting transfers between devices  28.3 us (8%)
  other arithmetic  15.8 us (4%)
  between operations  14.5 us (4%)
  local copies, waits for them, and re-layouts  13.4 us (4%)
    all_to_all x17, blocking collectives, swap(): return lax.all_to_all(blocks, axes, 0, 0, tiled=True)  236 us
    dot_general x10, matrix products, dot_t(): lax.dot_general(left_side, right_side, (((1,), (1,)), ((), ())), preferre...  18.5 us
    all_to_all x4, starting transfers between devices, swap(): return lax.all_to_all(blocks, axes, 0, 0, tiled=True)  17.2 us
    all_to_all x4, waiting for transfers between devices, swap(): return lax.all_to_all(blocks, axes, 0, 0, tiled=True)  15.8 us
    all_gather x1, waiting for transfers between devices, local(): gate_up_turned = lax.all_gather(gate_up_turned, 'y', axis=0, tiled=True)  11.8 us
    ppermute x4, starting transfers between devices, other_core(): return lax.ppermute(values, 'c', [(0, 1), (1, 0)])  10.2 us
    dot_general x5, matrix products, dot(): return jnp.dot(left_side, right_side, preferred_element_type=F32)  9.22 us
  transfers between devices with their start and end apart: 12, of which 9 were waited for; matrix products, arithmetic and copies ran while one was open for 9% of the time, Pallas kernels for 0%

profile of v3, /device:TPU:1, one launch (start us, length us, event | category | flops | bytes accessed | tf_op | source)
XLA Modules:
  0.0 370.5 jit_solution(3874797900661655570)
XLA Ops:
  6.5 1.2 convolution_convert_fusion.12
  7.8 0.8 collective-permute-start.1
  8.6 1.4 convolution_convert_fusion.6
  10.0 1.8 convolution_convert_fusion.13
  12.4 0.9 pad_maximum_fusion.5
  13.4 0.8 pad_maximum_fusion.6
  14.2 6.6 %all-to-all-start = ((bf16[8,16,1664]{2,1,0:T(8,128)(2,1)}), bf16[8,16,1664]{2,1,0:T(8,128)(2,1)S(1)}, u32[]{:S(2)}, u32[]{:S(2)}) async-start(bf16[8,16,1664]{2,1,0:T(8,128)(2,1)} %pad_maximum_fusion.6), calls=%async_computation | async-start | bytes 851968 | tf_op jit(solution)/shard_map/all_to_all | solution.py:45
  20.8 1.4 dynamic-slice_convert_fusion
  22.3 7.0 %all-to-all-done = bf16[8,16,1664]{2,1,0:T(8,128)(2,1)S(1)} async-done(((bf16[8,16,1664]{2,1,0:T(8,128)(2,1)}), bf16[8,16,1664]{2,1,0:T(8,128)(2,1)S(1)}, u32[]{:S(2)}, u32[]{:S(2)}) %all-to-all-start) | async-done | bytes 426016 | tf_op jit(solution)/shard_map/all_to_all | solution.py:45
  29.7 0.7 concatenate.108
  30.4 0.7 concatenate.107
  31.5 0.9 broadcast_in_dim.230
  32.4 3.5 all-to-all-start.1
  37.4 2.0 convolution_convert_fusion.4
  39.4 0.7 convolution_convert_fusion.3
  40.2 1.5 pad_maximum_fusion
  41.6 3.5 all-to-all-done.1
  45.2 1.8 collective-permute-start
  47.0 1.7 collective-permute-done
  48.7 1.2 select_bitcast_fusion.1
  50.1 1.3 convolution_convert_fusion.2
  51.5 22.8 %all_to_all.105 = bf16[4,144,1024]{2,1,0:T(8,128)(2,1)S(1)} all-to-all(bf16[4,144,1024]{2,1,0:T(8,128)(2,1)S(1)} %pad_maximum_fusion.2), channel_id=1, replica_groups=mesh['y'=4,'half'=2,'quad'=4,'x'=4,'c'=2] {'y'}, dimensions={0} | all-to-all | bytes 2359296 | tf_op jit(solution)/shard_map/all_to_all | solution.py:45
  74.9 1.6 reshape.257
  76.8 0.9 fusion.45
  77.8 20.4 %all_to_all.106 = bf16[8,16,1024]{2,1,0:T(8,128)(2,1)S(1)} all-to-all(bf16[8,16,1024]{2,1,0:T(8,128)(2,1)S(1)} %bitcast.153), channel_id=1, replica_groups=mesh['y'=4,'half'=2,'quad'=4,'x'=4,'c'=2] {'half','quad'}, dimensions={0} | all-to-all | bytes 524288 | tf_op jit(solution)/shard_map/all_to_all | solution.py:45
  98.3 12.2 %all_to_all.107 = bf16[8,16,1024]{2,1,0:T(8,128)(2,1)S(1)} all-to-all(bf16[8,16,1024]{2,1,0:T(8,128)(2,1)S(1)} %broadcast_in_dim.231), channel_id=1, replica_groups=mesh['y'=4,'half'=2,'quad'=4,'x'=4,'c'=2] {'half','quad'}, dimensions={0} | all-to-all | bytes 524288 | tf_op jit(solution)/shard_map/all_to_all | solution.py:45
  110.9 2.7 convolution_convert_fusion.1
  113.7 14.7 %all_to_all.108 = bf16[8,16,1408]{2,1,0:T(8,128)(2,1)S(1)} all-to-all(bf16[8,16,1408]{2,1,0:T(8,128)(2,1)S(1)} %bitcast.147), channel_id=1, replica_groups=mesh['y'=4,'half'=2,'quad'=4,'x'=4,'c'=2] {'x','c'}, dimensions={0} | all-to-all | bytes 720896 | tf_op jit(solution)/shard_map/all_to_all | solution.py:45
  128.5 0.7 fusion.21
  130.1 3.9 %all-to-all-start.6 = ((bf16[4,16,256]{2,1,0:T(8,128)(2,1)}), bf16[4,16,256]{2,1,0:T(8,128)(2,1)}, u32[]{:S(2)}, u32[]{:S(2)}) async-start(bf16[4,16,256]{2,1,0:T(8,128)(2,1)} %broadcast_in_dim.239), calls=%async_computation.6 | async-start | bytes 65536 | tf_op jit(solution)/shard_map/all_to_all | solution.py:45
  134.2 0.7 fusion.44
  135.0 1.2 concatenate.114
  136.8 1.8 all-to-all-done.6
  138.6 0.9 reshape.286
  141.5 10.8 %all_to_all.109 = bf16[8,16,1024]{2,1,0:T(8,128)(2,1)S(1)} all-to-all(bf16[8,16,1024]{2,1,0:T(8,128)(2,1)S(1)} %broadcast_in_dim.241), channel_id=1, replica_groups=mesh['y'=4,'half'=2,'quad'=4,'x'=4,'c'=2] {'x','c'}, dimensions={0} | all-to-all | bytes 524288 | tf_op jit(solution)/shard_map/all_to_all | solution.py:45
  152.8 12.6 %all_to_all.110 = bf16[8,16,1024]{2,1,0:T(8,128)(2,1)S(1)} all-to-all(bf16[8,16,1024]{2,1,0:T(8,128)(2,1)S(1)} %bitcast.157), channel_id=1, replica_groups=mesh['y'=4,'half'=2,'quad'=4,'x'=4,'c'=2] {'half','quad'}, dimensions={0} | all-to-all | bytes 524288 | tf_op jit(solution)/shard_map/all_to_all | solution.py:45
  166.1 12.1 %all_to_all.111 = bf16[8,16,1024]{2,1,0:T(8,128)(2,1)S(1)} all-to-all(bf16[8,16,1024]{2,1,0:T(8,128)(2,1)S(1)} %broadcast_in_dim.242), channel_id=1, replica_groups=mesh['y'=4,'half'=2,'quad'=4,'x'=4,'c'=2] {'half','quad'}, dimensions={0} | all-to-all | bytes 524288 | tf_op jit(solution)/shard_map/all_to_all | solution.py:45
  178.7 11.8 %all-gather.8.cloned.1.call-done = bf16[4096,1024]{1,0:T(8,128)(2,1)} async-done(((bf16[1024,1024]{1,0:T(8,128)(2,1)}), bf16[4096,1024]{1,0:T(8,128)(2,1)}) %all-gather.8.cloned.1.call-update) | async-done | bytes 8388624 | tf_op jit(solution)/shard_map/all_gather | solution.py:288
  190.5 6.2 %convolution_convert_fusion = bf16[128,4096]{1,0:T(8,128)(2,1)S(1)} fusion(bf16[128,1024]{1,0:T(8,128)(2,1)S(1)} %bitcast.150, bf16[4096,1024]{1,0:T(8,128)(2,1)} %all-gather.8.cloned.1.call-done), kind=kOutput, calls=%fused_computation | convolution fusion | flops 1074266112 | bytes 9699328 | tf_op jit(solution)/shard_map/dot_general | solution.py:29
  196.9 0.8 collective-permute-start.2
  197.6 1.6 collective-permute-done.2
  199.4 12.8 %all_to_all.112 = bf16[4,16,4224]{2,1,0:T(8,128)(2,1)S(1)} all-to-all(bf16[4,16,4224]{2,1,0:T(8,128)(2,1)S(1)} %fusion.3), channel_id=1, replica_groups=mesh['y'=4,'half'=2,'quad'=4,'x'=4,'c'=2] {'x'}, dimensions={0} | all-to-all | bytes 1081344 | tf_op jit(solution)/shard_map/all_to_all | solution.py:45
  213.4 10.2 %all_to_all.113 = bf16[4,16,4224]{2,1,0:T(8,128)(2,1)S(1)} all-to-all(bf16[4,16,4224]{2,1,0:T(8,128)(2,1)S(1)} %broadcast_in_dim.257), channel_id=1, replica_groups=mesh['y'=4,'half'=2,'quad'=4,'x'=4,'c'=2] {'x'}, dimensions={0} | all-to-all | bytes 1081344 | tf_op jit(solution)/shard_map/all_to_all | solution.py:45
  223.6 2.7 collective-permute-start.3
  226.4 1.6 collective-permute-done.3
  228.2 4.8 %convolution_convert_fusion.8 = bf16[128,1024]{1,0:T(8,128)(2,1)S(1)} fusion(bf16[4096,1024]{1,0:T(8,128)(2,1)} %all-gather.8.cloned.1.call-done, bf16[128,4224]{1,0:T(8,128)(2,1)S(1)} %bitcast.130), kind=kOutput, calls=%fused_computation.11 | convolution fusion | flops 1073872896 | bytes 9699328 | tf_op jit(solution)/shard_map/dot_general | solution.py:25
  233.0 18.9 %all_to_all.114 = bf16[8,16,1152]{2,1,0:T(8,128)(2,1)S(1)} all-to-all(bf16[8,16,1152]{2,1,0:T(8,128)(2,1)S(1)} %bitcast.148), channel_id=1, replica_groups=mesh['y'=4,'half'=2,'quad'=4,'x'=4,'c'=2] {'half','quad'}, dimensions={0} | all-to-all | bytes 589824 | tf_op jit(solution)/shard_map/all_to_all | solution.py:45
  252.2 0.7 fusion.40
  252.9 12.6 %all_to_all.115 = bf16[8,16,1024]{2,1,0:T(8,128)(2,1)S(1)} all-to-all(bf16[8,16,1024]{2,1,0:T(8,128)(2,1)S(1)} %broadcast_in_dim.258), channel_id=1, replica_groups=mesh['y'=4,'half'=2,'quad'=4,'x'=4,'c'=2] {'half','quad'}, dimensions={0} | all-to-all | bytes 524288 | tf_op jit(solution)/shard_map/all_to_all | solution.py:45
  265.5 0.8 convolution_convert_fusion.7
  266.4 11.6 %all_to_all.116 = bf16[8,16,1024]{2,1,0:T(8,128)(2,1)S(1)} all-to-all(bf16[8,16,1024]{2,1,0:T(8,128)(2,1)S(1)} %bitcast.155), channel_id=1, replica_groups=mesh['y'=4,'half'=2,'quad'=4,'x'=4,'c'=2] {'x','c'}, dimensions={0} | all-to-all | bytes 524288 | tf_op jit(solution)/shard_map/all_to_all | solution.py:45
  279.8 0.7 reshape.273
  280.5 3.3 all-to-all-start.15
  284.8 3.5 all-to-all-done.15
  288.8 12.3 %all_to_all.117 = bf16[8,16,1408]{2,1,0:T(8,128)(2,1)S(1)} all-to-all(bf16[8,16,1408]{2,1,0:T(8,128)(2,1)S(1)} %broadcast_in_dim.265), channel_id=1, replica_groups=mesh['y'=4,'half'=2,'quad'=4,'x'=4,'c'=2] {'x','c'}, dimensions={0} | all-to-all | bytes 720896 | tf_op jit(solution)/shard_map/all_to_all | solution.py:45
  301.1 2.3 convolution_convert_fusion.11
  303.5 13.5 %all_to_all.118 = bf16[8,16,1152]{2,1,0:T(8,128)(2,1)S(1)} all-to-all(bf16[8,16,1152]{2,1,0:T(8,128)(2,1)S(1)} %bitcast.149), channel_id=1, replica_groups=mesh['y'=4,'half'=2,'quad'=4,'x'=4,'c'=2] {'half','quad'}, dimensions={0} | all-to-all | bytes 589824 | tf_op jit(solution)/shard_map/all_to_all | solution.py:45
  317.4 11.9 %all_to_all.119 = bf16[8,16,1024]{2,1,0:T(8,128)(2,1)S(1)} all-to-all(bf16[8,16,1024]{2,1,0:T(8,128)(2,1)S(1)} %broadcast_in_dim.266), channel_id=1, replica_groups=mesh['y'=4,'half'=2,'quad'=4,'x'=4,'c'=2] {'half','quad'}, dimensions={0} | all-to-all | bytes 524288 | tf_op jit(solution)/shard_map/all_to_all | solution.py:45
  329.5 14.7 %all_to_all.120 = bf16[4,128,1024]{2,1,0:T(8,128)(2,1)S(1)} all-to-all(bf16[4,128,1024]{2,1,0:T(8,128)(2,1)S(1)} %broadcast_in_dim.268), channel_id=1, replica_groups=mesh['y'=4,'half'=2,'quad'=4,'x'=4,'c'=2] {'y'}, dimensions={0} | all-to-all | bytes 2097152 | tf_op jit(solution)/shard_map/all_to_all | solution.py:45
  344.3 0.7 convolution_convert_fusion.5
  345.0 4.9 %collective-permute-start.4 = (bf16[256,1024]{1,0:T(8,128)(2,1)S(1)}, bf16[256,1024]{1,0:T(8,128)(2,1)S(1)}, u32[]{:S(2)}, u32[]{:S(2)}) collective-permute-start(bf16[256,1024]{1,0:T(8,128)(2,1)S(1)} %convolution_convert_fusion.5), channel_id=1, source_target_pairs={{0,1},{1,0},{2,3},{3,2},{4,5},{5,4},{6,7},{7,6},{8,9},{9,8},{10,11... | collective-permute-start | bytes 1572872 | tf_op jit(solution)/shard_map/ppermute | solution.py:78
  349.9 0.7 fusion
  350.7 0.8 collective-permute-done.4
  351.6 11.6 %all_to_all.121 = bf16[4,64,1024]{2,1,0:T(8,128)(2,1)S(1)} all-to-all(bf16[4,64,1024]{2,1,0:T(8,128)(2,1)S(1)} %fusion.5), channel_id=1, replica_groups=mesh['y'=4,'half'=2,'quad'=4,'x'=4,'c'=2] {'x'}, dimensions={0} | all-to-all | bytes 1048576 | tf_op jit(solution)/shard_map/all_to_all | solution.py:45
  (244 shorter events, 16.1 us)
Async XLA Ops:
  6.5 43.6 %copy-start = (bf16[1024,1024]{1,0:T(8,128)(2,1)S(1)}, bf16[1024,1024]{1,0:T(8,128)(2,1)}, u32[]{:S(2)}) copy-start(bf16[1024,1024]{1,0:T(8,128)(2,1)} %param.27) | copy-start | bytes 6291460
  6.5 5.3 %copy-start.9 = (bf16[128,1024]{1,0:T(8,128)(2,1)S(1)}, bf16[128,1024]{1,0:T(8,128)(2,1)}, u32[]{:S(2)}) copy-start(bf16[128,1024]{1,0:T(8,128)(2,1)} %param.23) | copy-start | bytes 786436
  6.5 104.4 %all-gather.4.cloned.1.call-start = ((), (), s32[]{:S(2)}) async-start(), calls=%async_computation.21 | async-start | bytes 3276800 | tf_op jit(solution)/shard_map/all_gather | solution.py:242
  6.5 5.3 %copy-start.3 = (bf16[1024,1024]{1,0:T(8,128)(2,1)S(1)}, bf16[1024,1024]{1,0:T(8,128)(2,1)}, u32[]{:S(2)}) copy-start(bf16[1024,1024]{1,0:T(8,128)(2,1)} %param.24) | copy-start | bytes 6291460
  7.8 4.6 %collective-permute-start.1 = (bf16[64,1024]{1,0:T(8,128)(2,1)S(1)}, bf16[64,1024]{1,0:T(8,128)(2,1)S(1)}, u32[]{:S(2)}, u32[]{:S(2)}) collective-permute-start(bf16[64,1024]{1,0:T(8,128)(2,1)S(1)} %convolution_convert_fusion.12), channel_id=1, source_target_pairs={{0,0},{8,8},{16,32},{24,40},{32,16},{40,24},{48,48},{56,56},{64,64... | collective-permute-start | bytes 393224 | tf_op jit(solution)/shard_map/ppermute | solution.py:175
  10.0 2.3 copy-start.32
  12.3 8.5 %copy-start.12 = (s32[64,1024]{1,0:T(8,128)S(1)}, s32[64,1024]{1,0:T(8,128)}, u32[]{:S(2)}) copy-start(s32[64,1024]{1,0:T(8,128)} %param.26) | copy-start | bytes 786436
  12.3 9.9 %copy-start.18 = (f32[1024]{0:T(1024)S(1)}, f32[1024]{0:T(1024)}, u32[]{:S(2)}) copy-start(f32[1024]{0:T(1024)} %param.35) | copy-start | bytes 12292
  12.3 9.9 %copy-start.19 = (f32[1024]{0:T(1024)S(1)}, f32[1024]{0:T(1024)}, u32[]{:S(2)}) copy-start(f32[1024]{0:T(1024)} %param.31) | copy-start | bytes 12292
  13.3 16.2 %copy-start.30 = (f32[64]{0:T(128)S(1)}, f32[64]{0:T(128)}, u32[]{:S(2)}) copy-start(f32[64]{0:T(128)} %constant.113.clone) | copy-start | bytes 772
  13.3 18.0 %copy-start.17 = (f32[1024]{0:T(1024)S(1)}, f32[1024]{0:T(1024)}, u32[]{:S(2)}) copy-start(f32[1024]{0:T(1024)} %param.25) | copy-start | bytes 12292
  14.2 15.1 %all-to-all-start = ((bf16[8,16,1664]{2,1,0:T(8,128)(2,1)}), bf16[8,16,1664]{2,1,0:T(8,128)(2,1)S(1)}, u32[]{:S(2)}, u32[]{:S(2)}) async-start(bf16[8,16,1664]{2,1,0:T(8,128)(2,1)} %pad_maximum_fusion.6), calls=%async_computation | async-start | bytes 851968 | tf_op jit(solution)/shard_map/all_to_all | solution.py:45
  32.4 12.8 %all-to-all-start.1 = ((bf16[4,72,1024]{2,1,0:T(8,128)(2,1)}), bf16[4,72,1024]{2,1,0:T(8,128)(2,1)S(1)}, u32[]{:S(2)}, u32[]{:S(2)}) async-start(bf16[4,72,1024]{2,1,0:T(8,128)(2,1)} %broadcast_in_dim.230), calls=%async_computation.1 | async-start | bytes 1179648 | tf_op jit(solution)/shard_map/all_to_all | solution.py:45
  35.8 92.6 %all-gather.6.cloned.1.call-start = ((), (), s32[]{:S(2)}) async-start(), calls=%async_computation.22 | async-start | bytes 2621440 | tf_op jit(solution)/shard_map/all_gather | solution.py:286
  35.9 3.5 copy-start.31
  45.2 3.5 collective-permute-start
  47.0 143.5 %all-gather.8.cloned.1.call-start = ((), (), s32[]{:S(2)}) async-start(), calls=%async_computation.23 | async-start | bytes 10485760 | tf_op jit(solution)/shard_map/all_gather | solution.py:288
  76.7 21.6 %copy-start.15 = (f32[16,1024]{1,0:T(8,128)S(1)}, f32[16,1024]{1,0:T(8,128)}, u32[]{:S(2)}) copy-start(f32[16,1024]{1,0:T(8,128)} %get-tuple-element.56) | copy-start | bytes 196612
  76.7 21.5 %copy-start.25 = (f32[1024]{0:T(1024)S(1)}, f32[1024]{0:T(1024)}, u32[]{:S(2)}) copy-start(f32[1024]{0:T(1024)} %param.28) | copy-start | bytes 12292
  77.8 33.0 %copy-start.20 = (pred[1,128]{1,0:T(4,128)(4,1)S(1)}, pred[1,128]{1,0:T(4,128)(4,1)}, u32[]{:S(2)}) copy-start(pred[1,128]{1,0:T(4,128)(4,1)} %constant.109.clone) | copy-start | bytes 388
  77.8 33.0 %copy-start.22 = (pred[1,128]{1,0:T(4,128)(4,1)S(1)}, pred[1,128]{1,0:T(4,128)(4,1)}, u32[]{:S(2)}) copy-start(pred[1,128]{1,0:T(4,128)(4,1)} %constant.110.clone) | copy-start | bytes 388
  113.7 22.4 %copy-start.4 = (f32[128,64]{0,1:T(8,128)S(1)}, f32[128,64]{0,1:T(8,128)}, u32[]{:S(2)}) copy-start(f32[128,64]{0,1:T(8,128)} %concatenate.108) | copy-start | bytes 98308
  113.7 22.4 %copy-start.5 = (f32[128,64]{0,1:T(8,128)S(1)}, f32[128,64]{0,1:T(8,128)}, u32[]{:S(2)}) copy-start(f32[128,64]{0,1:T(8,128)} %concatenate.107) | copy-start | bytes 98308
  130.1 8.5 %all-to-all-start.6 = ((bf16[4,16,256]{2,1,0:T(8,128)(2,1)}), bf16[4,16,256]{2,1,0:T(8,128)(2,1)}, u32[]{:S(2)}, u32[]{:S(2)}) async-start(bf16[4,16,256]{2,1,0:T(8,128)(2,1)} %broadcast_in_dim.239), calls=%async_computation.6 | async-start | bytes 65536 | tf_op jit(solution)/shard_map/all_to_all | solution.py:45
  134.2 5.7 %copy-start.7 = (f32[64,64]{0,1:T(8,128)S(1)}, f32[64,64]{0,1:T(8,128)}, u32[]{:S(2)}) copy-start(f32[64,64]{0,1:T(8,128)} %pad_maximum_fusion.21) | copy-start | bytes 49156
  134.2 5.7 %copy-start.8 = (f32[64,64]{0,1:T(8,128)S(1)}, f32[64,64]{0,1:T(8,128)}, u32[]{:S(2)}) copy-start(f32[64,64]{0,1:T(8,128)} %pad_maximum_fusion.20) | copy-start | bytes 49156
  134.2 5.8 %copy-start.24 = (pred[128,64]{0,1:T(32,128)(4,1)S(1)}, pred[128,64]{0,1:T(32,128)(4,1)}, u32[]{:S(2)}) copy-start(pred[128,64]{0,1:T(32,128)(4,1)} %constant.108.clone) | copy-start | bytes 24580
  139.8 12.6 %copy-start.1 = (bf16[1024,1024]{1,0:T(8,128)(2,1)S(1)}, bf16[1024,1024]{1,0:T(8,128)(2,1)}, u32[]{:S(2)}) copy-start(bf16[1024,1024]{1,0:T(8,128)(2,1)} %all-gather.6.cloned.1.call-done) | copy-start | bytes 6291460
  152.3 26.2 %copy-start.21 = (pred[1,128]{1,0:T(4,128)(4,1)S(1)}, pred[1,128]{1,0:T(4,128)(4,1)}, u32[]{:S(2)}) copy-start(pred[1,128]{1,0:T(4,128)(4,1)} %constant.109.clone) | copy-start | bytes 388
  152.3 26.2 %copy-start.23 = (pred[1,128]{1,0:T(4,128)(4,1)S(1)}, pred[1,128]{1,0:T(4,128)(4,1)}, u32[]{:S(2)}) copy-start(pred[1,128]{1,0:T(4,128)(4,1)} %constant.110.clone) | copy-start | bytes 388
  196.9 2.4 collective-permute-start.2
  199.3 13.9 %copy-start.26 = (pred[1,128]{1,0:T(4,128)(4,1)S(1)}, pred[1,128]{1,0:T(4,128)(4,1)}, u32[]{:S(2)}) copy-start(pred[1,128]{1,0:T(4,128)(4,1)} %constant.111.clone) | copy-start | bytes 388
  199.4 13.9 %copy-start.27 = (pred[1,128]{1,0:T(4,128)(4,1)S(1)}, pred[1,128]{1,0:T(4,128)(4,1)}, u32[]{:S(2)}) copy-start(pred[1,128]{1,0:T(4,128)(4,1)} %constant.112.clone) | copy-start | bytes 388
  223.6 4.3 %collective-permute-start.3 = (bf16[4,16,4224]{2,1,0:T(8,128)(2,1)S(1)}, bf16[4,16,4224]{2,1,0:T(8,128)(2,1)S(1)}, u32[]{:S(2)}, u32[]{:S(2)}) collective-permute-start(bf16[4,16,4224]{2,1,0:T(8,128)(2,1)S(1)} %all_to_all.113), channel_id=1, source_target_pairs={{0,1},{1,0},{2,3},{3,2},{4,5},{5,4},{6,7},{7,6},{8,9},{9,8},{10,11... | collective-permute-start | bytes 1622024 | tf_op jit(solution)/shard_map/ppermute | solution.py:78
  228.2 24.0 %copy-start.13 = (f32[16,1024]{1,0:T(8,128)S(1)}, f32[16,1024]{1,0:T(8,128)}, u32[]{:S(2)}) copy-start(f32[16,1024]{1,0:T(8,128)} %get-tuple-element.44) | copy-start | bytes 196612
  228.2 24.0 %copy-start.16 = (f32[16,1024]{1,0:T(8,128)S(1)}, f32[16,1024]{1,0:T(8,128)}, u32[]{:S(2)}) copy-start(f32[16,1024]{1,0:T(8,128)} %get-tuple-element.101) | copy-start | bytes 196612
  233.0 32.6 %copy-start.2 = (bf16[1024,1024]{1,0:T(8,128)(2,1)S(1)}, bf16[1024,1024]{1,0:T(8,128)(2,1)}, u32[]{:S(2)}) copy-start(bf16[1024,1024]{1,0:T(8,128)(2,1)} %all-gather.6.cloned.1.call-done) | copy-start | bytes 6291460
  252.9 25.8 %copy-start.10 = (f32[128,128]{0,1:T(8,128)S(1)}, f32[128,128]{0,1:T(8,128)}, u32[]{:S(2)}) copy-start(f32[128,128]{0,1:T(8,128)} %pad_maximum_fusion.14) | copy-start | bytes 196612
  265.5 13.4 %copy-start.11 = (f32[64,128]{0,1:T(8,128)S(1)}, f32[64,128]{0,1:T(8,128)}, u32[]{:S(2)}) copy-start(f32[64,128]{0,1:T(8,128)} %pad_maximum_fusion.16) | copy-start | bytes 98308
  265.5 18.3 %copy-start.6 = (f32[128,64]{0,1:T(8,128)S(1)}, f32[128,64]{0,1:T(8,128)}, u32[]{:S(2)}) copy-start(f32[128,64]{0,1:T(8,128)} %concatenate.107) | copy-start | bytes 98308
  266.4 22.3 %copy-start.28 = (bf16[16]{0:T(256)(128)(2,1)S(1)}, bf16[16]{0:T(256)(128)(2,1)}, u32[]{:S(2)}) copy-start(bf16[16]{0:T(256)(128)(2,1)} %get-tuple-element.84) | copy-start | bytes 100
  266.4 22.3 %copy-start.29 = (bf16[16]{0:T(256)(128)(2,1)S(1)}, bf16[16]{0:T(256)(128)(2,1)}, u32[]{:S(2)}) copy-start(bf16[16]{0:T(256)(128)(2,1)} %get-tuple-element.85) | copy-start | bytes 100
  280.5 7.7 %all-to-all-start.15 = ((bf16[4,16,256]{2,1,0:T(8,128)(2,1)}), bf16[4,16,256]{2,1,0:T(8,128)(2,1)S(1)}, u32[]{:S(2)}, u32[]{:S(2)}) async-start(bf16[4,16,256]{2,1,0:T(8,128)(2,1)} %reshape.273), calls=%async_computation.15 | async-start | bytes 65536 | tf_op jit(solution)/shard_map/all_to_all | solution.py:45
  301.1 16.1 %copy-start.14 = (f32[16,1024]{1,0:T(8,128)S(1)}, f32[16,1024]{1,0:T(8,128)}, u32[]{:S(2)}) copy-start(f32[16,1024]{1,0:T(8,128)} %get-tuple-element.94) | copy-start | bytes 196612
  345.0 6.4 %collective-permute-start.4 = (bf16[256,1024]{1,0:T(8,128)(2,1)S(1)}, bf16[256,1024]{1,0:T(8,128)(2,1)S(1)}, u32[]{:S(2)}, u32[]{:S(2)}) collective-permute-start(bf16[256,1024]{1,0:T(8,128)(2,1)S(1)} %convolution_convert_fusion.5), channel_id=1, source_target_pairs={{0,1},{1,0},{2,3},{3,2},{4,5},{5,4},{6,7},{7,6},{8,9},{9,8},{10,11... | collective-permute-start | bytes 1572872 | tf_op jit(solution)/shard_map/ppermute | solution.py:78
Sparse Core Ops, SparseCore 0:
  13.4 53.2 all-gather.3
  68.6 34.3 all-gather.5
  104.7 85.6 all-gather.7

commit v4 on v3

--- a/solution.py
+++ b/solution.py
@@ -226,6 +226,7 @@
     hidden = gate_weight.shape[1]
     model_width = dec_weight.shape[1]
 
+    out_rows = lax.all_gather(out_weight, "y", axis=0, tiled=True)
     first_sums = jnp.concatenate(
         [dot(layer_input, enc_weight).astype(B16), dot_t(cotangent, down_weight).astype(B16)],
         axis=1,
@@ -239,10 +240,12 @@
     turned_rows = jnp.concatenate(
         [turned(query_weight), placed_block(turned(kv_weight))], axis=0
     )
+    blocks, ready, active_rows, gate_weight, up_weight, turned_rows = (
+        lax.optimization_barrier(
+            (blocks, ready, active_rows, gate_weight, up_weight, turned_rows)
+        )
+    )
     turned_rows = lax.all_gather(turned_rows, "y", axis=0, tiled=True)
-    blocks, ready, active_rows, gate_weight, up_weight = lax.optimization_barrier(
-        (blocks, ready, active_rows, gate_weight, up_weight)
-    )
     first_core, masks = ready["first_core"], ready["masks"]
     first_sums = added(blocks[:, :, : width + hidden])
     own_positions = lax.dynamic_index_in_dim(
@@ -276,16 +279,13 @@
     back_hidden = gathered[:, feature_rows:].reshape(NY, -1, width)
     decoded = dot(features, dec_weight).astype(B16).reshape(NY, -1, model_width)
     blocks = swap(jnp.concatenate([decoded, back_hidden], axis=1), "y")
+    blocks, out_rows, gate_up_turned = lax.optimization_barrier(
+        (blocks, out_rows, gate_up_turned)
+    )
+    gate_up_turned = lax.all_gather(gate_up_turned, "y", axis=0, tiled=True)
     chunk_rows = decoded.shape[1]
-    back_hidden = blocks[:, chunk_rows:].reshape(NY, 2, SEQ, hidden)
-    back_hidden = jnp.where(ready["late_prompt"], back_hidden[:, 1], back_hidden[:, 0])
-    back_hidden = back_hidden.transpose(1, 0, 2).astype(F32)
     decoded = added(blocks[:, :chunk_rows]).astype(B16).reshape(NZ, SEQ, model_width)
-    decoded, back_hidden = lax.optimization_barrier((decoded, back_hidden))
     decoded = added(swap(decoded, Z))
-    out_rows = lax.all_gather(out_weight, "y", axis=0, tiled=True)
-    decoded, gate_up_turned = lax.optimization_barrier((decoded, gate_up_turned))
-    gate_up_turned = lax.all_gather(gate_up_turned, "y", axis=0, tiled=True)
     hidden_in = decoded + dec_bias + ready["error_rows"]
 
     gained = feat_part_rows((hidden_in * attn_gain).astype(B16))
@@ -297,14 +297,20 @@
             [dot_t(gained, turned_rows).astype(B16), split_column(masks, squares)], axis=1
         )
     )
-    projections, out_rows = lax.optimization_barrier((projections, out_rows))
     head_part = query_weight.shape[1]
     qkv_width = turned_rows.shape[0]
     scale_rows = lax.rsqrt(joined_column(projections[:, qkv_width:]) / D + epsilon)
     own_qkv = (projections[:, :qkv_width] * scale_rows).reshape(SEQ, NY, qkv_width // NY)
     kv_part = own_qkv.shape[2] - head_part
     own_keyval = own_qkv[:, :, head_part:].astype(B16).reshape(SEQ, NY * kv_part)
-    keyval = spread(own_keyval, "quad", QUAD).reshape(QUAD, SEQ, NY, kv_part)
+    keyval = jnp.broadcast_to(own_keyval[None], (QUAD,) + own_keyval.shape)
+    keyval, blocks = lax.optimization_barrier((keyval, blocks))
+    keyval = swap(keyval, "quad")
+    back_hidden = blocks[:, chunk_rows:].reshape(NY, 2, SEQ, hidden)
+    back_hidden = jnp.where(ready["late_prompt"], back_hidden[:, 1], back_hidden[:, 0])
+    back_hidden = back_hidden.transpose(1, 0, 2).astype(F32)
+    keyval, back_hidden = lax.optimization_barrier((keyval, back_hidden))
+    keyval = keyval.reshape(QUAD, SEQ, NY, kv_part)
     attended, saved = attend(
         own_qkv[:, :, :head_part].reshape(SEQ, -1),
         keyval.transpose(1, 2, 0, 3).reshape(SEQ, -1).astype(F32),

time: 372 us -> 363 us (0.976)
  waiting for transfers between devices: 33.4 us -> 17 us
    all_gather x1, waiting for transfers between devices: 11.8 us -> 0.02 us  [local(): gate_up_turned = lax.all_gather(gate_up_turned, 'y', axis=0, tiled=True)]
    all_to_all x4, waiting for transfers between devices: 15.8 us -> 11.4 us  [swap(): return lax.all_to_all(blocks, axes, 0, 0, tiled=True)]
  transfers between devices with their start and end apart: 12 -> 12, of which waited for: 9 -> 8; matrix products, arithmetic and copies ran while one was open for 9% -> 10% of each run, Pallas kernels for 0% -> 0%
where the time goes in v4:
time: 363 us; the launch traced here: 361 us
  blocking collectives  237 us (65%)
  matrix products  31.5 us (9%)
  starting transfers between devices  30.5 us (8%)
  other arithmetic  19 us (5%)
  waiting for transfers between devices  17 us (5%)
  between operations  14.4 us (4%)
  local copies, waits for them, and re-layouts  11.4 us (3%)
    all_to_all x17, blocking collectives, swap(): return lax.all_to_all(blocks, axes, 0, 0, tiled=True)  237 us
    dot_general x10, matrix products, dot_t(): lax.dot_general(left_side, right_side, (((1,), (1,)), ((), ())), preferre...  19.2 us
    all_to_all x4, starting transfers between devices, swap(): return lax.all_to_all(blocks, axes, 0, 0, tiled=True)  16.6 us
    ppermute x4, starting transfers between devices, other_core(): return lax.ppermute(values, 'c', [(0, 1), (1, 0)])  12.3 us
    all_to_all x4, waiting for transfers between devices, swap(): return lax.all_to_all(blocks, axes, 0, 0, tiled=True)  11.4 us
    dot_general x5, matrix products, dot(): return jnp.dot(left_side, right_side, preferred_element_type=F32)  10.8 us
  transfers between devices with their start and end apart: 12, of which 8 were waited for; matrix products, arithmetic and copies ran while one was open for 10% of the time, Pallas kernels for 0%

profile of v4, /device:TPU:1, one launch (start us, length us, event | category | flops | bytes accessed | tf_op | source)
XLA Modules:
  0.0 361.2 jit_solution(1601712867076719322)
XLA Ops:
  6.5 1.9 convolution_convert_fusion.12
  8.4 1.6 collective-permute-start
  10.6 1.8 convolution_convert_fusion.13
  12.5 2.0 convolution_convert_fusion.10
  14.6 0.8 pad_maximum_fusion.6
  15.5 6.6 %all-to-all-start = ((bf16[8,16,1664]{2,1,0:T(8,128)(2,1)}), bf16[8,16,1664]{2,1,0:T(8,128)(2,1)S(1)}, u32[]{:S(2)}, u32[]{:S(2)}) async-start(bf16[8,16,1664]{2,1,0:T(8,128)(2,1)} %pad_maximum_fusion.6), calls=%async_computation | async-start | bytes 851968 | tf_op jit(solution)/shard_map/all_to_all | solution.py:45
  22.1 1.4 convolution_convert_fusion.6
  24.1 1.0 convert_element_type.219
  25.1 1.4 dynamic-slice_convert_fusion
  26.5 0.9 pad_maximum_fusion.5
  27.4 3.1 all-to-all-done
  31.1 0.7 concatenate.108
  31.8 0.7 concatenate.109
  32.8 0.9 broadcast_in_dim.230
  33.7 3.5 all-to-all-start.1
  37.2 0.7 pad_maximum_fusion.20
  37.9 0.7 pad_maximum_fusion.21
  38.6 0.7 pad_maximum_fusion.11
  39.3 2.0 convolution_convert_fusion.3
  41.3 0.7 convolution_convert_fusion.4
  42.1 1.5 pad_maximum_fusion
  43.6 2.9 all-to-all-done.1
  46.5 1.8 collective-permute-start.1
  48.2 1.6 collective-permute-done.1
  50.2 1.3 convolution_convert_fusion.2
  51.6 21.9 %all_to_all.105 = bf16[4,144,1024]{2,1,0:T(8,128)(2,1)S(1)} all-to-all(bf16[4,144,1024]{2,1,0:T(8,128)(2,1)S(1)} %pad_maximum_fusion.2), channel_id=1, replica_groups=mesh['y'=4,'half'=2,'quad'=4,'x'=4,'c'=2] {'y'}, dimensions={0} | all-to-all | bytes 2359296 | tf_op jit(solution)/shard_map/all_to_all | solution.py:45
  73.7 23.8 %all_to_all.106 = bf16[8,16,1024]{2,1,0:T(8,128)(2,1)S(1)} all-to-all(bf16[8,16,1024]{2,1,0:T(8,128)(2,1)S(1)} %bitcast.157), channel_id=1, replica_groups=mesh['y'=4,'half'=2,'quad'=4,'x'=4,'c'=2] {'half','quad'}, dimensions={0} | all-to-all | bytes 524288 | tf_op jit(solution)/shard_map/all_to_all | solution.py:45
  98.2 11.7 %all_to_all.107 = bf16[8,16,1024]{2,1,0:T(8,128)(2,1)S(1)} all-to-all(bf16[8,16,1024]{2,1,0:T(8,128)(2,1)S(1)} %broadcast_in_dim.231), channel_id=1, replica_groups=mesh['y'=4,'half'=2,'quad'=4,'x'=4,'c'=2] {'half','quad'}, dimensions={0} | all-to-all | bytes 524288 | tf_op jit(solution)/shard_map/all_to_all | solution.py:45
  111.3 1.4 select_convert_fusion.1
  112.6 2.9 convolution_convert_fusion.1
  115.6 16.6 %all_to_all.108 = bf16[8,16,1408]{2,1,0:T(8,128)(2,1)S(1)} all-to-all(bf16[8,16,1408]{2,1,0:T(8,128)(2,1)S(1)} %bitcast.147), channel_id=1, replica_groups=mesh['y'=4,'half'=2,'quad'=4,'x'=4,'c'=2] {'x','c'}, dimensions={0} | all-to-all | bytes 720896 | tf_op jit(solution)/shard_map/all_to_all | solution.py:45
  132.3 0.8 fusion.21
  134.7 3.3 all-to-all-start.6
  138.0 1.0 copy.211
  139.8 1.1 concatenate.114
  141.6 1.1 all-to-all-done.6
  144.8 10.7 %all_to_all.109 = bf16[8,16,1024]{2,1,0:T(8,128)(2,1)S(1)} all-to-all(bf16[8,16,1024]{2,1,0:T(8,128)(2,1)S(1)} %broadcast_in_dim.241), channel_id=1, replica_groups=mesh['y'=4,'half'=2,'quad'=4,'x'=4,'c'=2] {'x','c'}, dimensions={0} | all-to-all | bytes 524288 | tf_op jit(solution)/shard_map/all_to_all | solution.py:45
  156.0 12.7 %all_to_all.110 = bf16[8,16,1024]{2,1,0:T(8,128)(2,1)S(1)} all-to-all(bf16[8,16,1024]{2,1,0:T(8,128)(2,1)S(1)} %bitcast.156), channel_id=1, replica_groups=mesh['y'=4,'half'=2,'quad'=4,'x'=4,'c'=2] {'half','quad'}, dimensions={0} | all-to-all | bytes 524288 | tf_op jit(solution)/shard_map/all_to_all | solution.py:45
  168.7 12.2 %all_to_all.111 = bf16[8,16,1024]{2,1,0:T(8,128)(2,1)S(1)} all-to-all(bf16[8,16,1024]{2,1,0:T(8,128)(2,1)S(1)} %broadcast_in_dim.242), channel_id=1, replica_groups=mesh['y'=4,'half'=2,'quad'=4,'x'=4,'c'=2] {'half','quad'}, dimensions={0} | all-to-all | bytes 524288 | tf_op jit(solution)/shard_map/all_to_all | solution.py:45
  181.4 6.2 %convolution_convert_fusion = bf16[128,4096]{1,0:T(8,128)(2,1)S(1)} fusion(bf16[128,1024]{1,0:T(8,128)(2,1)S(1)} %bitcast.150, bf16[4096,1024]{1,0:T(8,128)(2,1)} %all-gather.8.cloned.1.call-done), kind=kOutput, calls=%fused_computation | convolution fusion | flops 1074266112 | bytes 9699328 | tf_op jit(solution)/shard_map/dot_general | solution.py:29
  187.7 3.5 collective-permute-start.2
  191.2 1.6 collective-permute-done.2
  192.9 11.8 %all_to_all.112 = bf16[4,16,4224]{2,1,0:T(8,128)(2,1)S(1)} all-to-all(bf16[4,16,4224]{2,1,0:T(8,128)(2,1)S(1)} %fusion.2), channel_id=1, replica_groups=mesh['y'=4,'half'=2,'quad'=4,'x'=4,'c'=2] {'x'}, dimensions={0} | all-to-all | bytes 1081344 | tf_op jit(solution)/shard_map/all_to_all | solution.py:45
  205.9 10.9 %all_to_all.113 = bf16[4,16,4224]{2,1,0:T(8,128)(2,1)S(1)} all-to-all(bf16[4,16,4224]{2,1,0:T(8,128)(2,1)S(1)} %broadcast_in_dim.257), channel_id=1, replica_groups=mesh['y'=4,'half'=2,'quad'=4,'x'=4,'c'=2] {'x'}, dimensions={0} | all-to-all | bytes 1081344 | tf_op jit(solution)/shard_map/all_to_all | solution.py:45
  216.7 2.1 collective-permute-start.3
  218.9 1.6 collective-permute-done.3
  220.7 4.8 %convolution_convert_fusion.8 = bf16[128,1024]{1,0:T(8,128)(2,1)S(1)} fusion(bf16[4096,1024]{1,0:T(8,128)(2,1)} %all-gather.8.cloned.1.call-done, bf16[128,4224]{1,0:T(8,128)(2,1)S(1)} %bitcast.130), kind=kOutput, calls=%fused_computation.11 | convolution fusion | flops 1073872896 | bytes 9699328 | tf_op jit(solution)/shard_map/dot_general | solution.py:25
  225.5 16.8 %all_to_all.114 = bf16[8,16,1152]{2,1,0:T(8,128)(2,1)S(1)} all-to-all(bf16[8,16,1152]{2,1,0:T(8,128)(2,1)S(1)} %bitcast.148), channel_id=1, replica_groups=mesh['y'=4,'half'=2,'quad'=4,'x'=4,'c'=2] {'half','quad'}, dimensions={0} | all-to-all | bytes 589824 | tf_op jit(solution)/shard_map/all_to_all | solution.py:45
  242.7 12.6 %all_to_all.115 = bf16[8,16,1024]{2,1,0:T(8,128)(2,1)S(1)} all-to-all(bf16[8,16,1024]{2,1,0:T(8,128)(2,1)S(1)} %broadcast_in_dim.258), channel_id=1, replica_groups=mesh['y'=4,'half'=2,'quad'=4,'x'=4,'c'=2] {'half','quad'}, dimensions={0} | all-to-all | bytes 524288 | tf_op jit(solution)/shard_map/all_to_all | solution.py:45
  255.3 0.8 convolution_convert_fusion.7
  256.2 11.6 %all_to_all.116 = bf16[8,16,1024]{2,1,0:T(8,128)(2,1)S(1)} all-to-all(bf16[8,16,1024]{2,1,0:T(8,128)(2,1)S(1)} %bitcast.154), channel_id=1, replica_groups=mesh['y'=4,'half'=2,'quad'=4,'x'=4,'c'=2] {'x','c'}, dimensions={0} | all-to-all | bytes 524288 | tf_op jit(solution)/shard_map/all_to_all | solution.py:45
  270.5 0.7 reshape.274
  271.2 3.3 all-to-all-start.15
  274.6 4.4 %all-to-all-done.15 = bf16[4,16,256]{2,1,0:T(8,128)(2,1)S(1)} async-done(((bf16[4,16,256]{2,1,0:T(8,128)(2,1)}), bf16[4,16,256]{2,1,0:T(8,128)(2,1)S(1)}, u32[]{:S(2)}, u32[]{:S(2)}) %all-to-all-start.15) | async-done | bytes 32800 | tf_op jit(solution)/shard_map/all_to_all | solution.py:45
  279.5 12.3 %all_to_all.117 = bf16[8,16,1408]{2,1,0:T(8,128)(2,1)S(1)} all-to-all(bf16[8,16,1408]{2,1,0:T(8,128)(2,1)S(1)} %broadcast_in_dim.265), channel_id=1, replica_groups=mesh['y'=4,'half'=2,'quad'=4,'x'=4,'c'=2] {'x','c'}, dimensions={0} | all-to-all | bytes 720896 | tf_op jit(solution)/shard_map/all_to_all | solution.py:45
  291.8 2.2 convolution_convert_fusion.11
  294.1 13.5 %all_to_all.118 = bf16[8,16,1152]{2,1,0:T(8,128)(2,1)S(1)} all-to-all(bf16[8,16,1152]{2,1,0:T(8,128)(2,1)S(1)} %bitcast.149), channel_id=1, replica_groups=mesh['y'=4,'half'=2,'quad'=4,'x'=4,'c'=2] {'half','quad'}, dimensions={0} | all-to-all | bytes 589824 | tf_op jit(solution)/shard_map/all_to_all | solution.py:45
  308.0 12.0 %all_to_all.119 = bf16[8,16,1024]{2,1,0:T(8,128)(2,1)S(1)} all-to-all(bf16[8,16,1024]{2,1,0:T(8,128)(2,1)S(1)} %broadcast_in_dim.266), channel_id=1, replica_groups=mesh['y'=4,'half'=2,'quad'=4,'x'=4,'c'=2] {'half','quad'}, dimensions={0} | all-to-all | bytes 524288 | tf_op jit(solution)/shard_map/all_to_all | solution.py:45
  320.2 14.7 %all_to_all.120 = bf16[4,128,1024]{2,1,0:T(8,128)(2,1)S(1)} all-to-all(bf16[4,128,1024]{2,1,0:T(8,128)(2,1)S(1)} %broadcast_in_dim.268), channel_id=1, replica_groups=mesh['y'=4,'half'=2,'quad'=4,'x'=4,'c'=2] {'y'}, dimensions={0} | all-to-all | bytes 2097152 | tf_op jit(solution)/shard_map/all_to_all | solution.py:45
  334.9 0.7 convolution_convert_fusion.5
  335.7 4.9 %collective-permute-start.4 = (bf16[256,1024]{1,0:T(8,128)(2,1)S(1)}, bf16[256,1024]{1,0:T(8,128)(2,1)S(1)}, u32[]{:S(2)}, u32[]{:S(2)}) collective-permute-start(bf16[256,1024]{1,0:T(8,128)(2,1)S(1)} %convolution_convert_fusion.5), channel_id=1, source_target_pairs={{0,1},{1,0},{2,3},{3,2},{4,5},{5,4},{6,7},{7,6},{8,9},{9,8},{10,11... | collective-permute-start | bytes 1572872 | tf_op jit(solution)/shard_map/ppermute | solution.py:78
  340.6 0.7 fusion
  341.3 0.8 collective-permute-done.4
  342.3 11.6 %all_to_all.121 = bf16[4,64,1024]{2,1,0:T(8,128)(2,1)S(1)} all-to-all(bf16[4,64,1024]{2,1,0:T(8,128)(2,1)S(1)} %fusion.4), channel_id=1, replica_groups=mesh['y'=4,'half'=2,'quad'=4,'x'=4,'c'=2] {'x'}, dimensions={0} | all-to-all | bytes 1048576 | tf_op jit(solution)/shard_map/all_to_all | solution.py:45
  (238 shorter events, 17.3 us)
Async XLA Ops:
  6.5 43.7 %copy-start = (bf16[1024,1024]{1,0:T(8,128)(2,1)S(1)}, bf16[1024,1024]{1,0:T(8,128)(2,1)}, u32[]{:S(2)}) copy-start(bf16[1024,1024]{1,0:T(8,128)(2,1)} %param.27) | copy-start | bytes 6291460
  6.5 5.9 %copy-start.9 = (bf16[128,1024]{1,0:T(8,128)(2,1)S(1)}, bf16[128,1024]{1,0:T(8,128)(2,1)}, u32[]{:S(2)}) copy-start(bf16[128,1024]{1,0:T(8,128)(2,1)} %param.23) | copy-start | bytes 786436
  6.5 66.9 %all-gather.4.cloned.1.call-start = ((), (), s32[]{:S(2)}) async-start(), calls=%async_computation.21 | async-start | bytes 2621440 | tf_op jit(solution)/shard_map/all_gather | solution.py:229
  8.4 18.1 %collective-permute-start = (bf16[64,1024]{1,0:T(8,128)(2,1)}, bf16[64,1024]{1,0:T(8,128)(2,1)S(1)}, u32[]{:S(2)}, u32[]{:S(2)}) collective-permute-start(bf16[64,1024]{1,0:T(8,128)(2,1)} %convolution_convert_fusion.12), channel_id=1, source_target_pairs={{0,0},{8,8},{16,32},{24,40},{32,16},{40,24},{48,48},{56,56},{64,64... | collective-permute-start | bytes 393224 | tf_op jit(solution)/shard_map/ppermute | solution.py:175
  14.5 9.0 %copy-start.16 = (f32[1024]{0:T(1024)S(1)}, f32[1024]{0:T(1024)}, u32[]{:S(2)}) copy-start(f32[1024]{0:T(1024)} %param.35) | copy-start | bytes 12292
  14.5 9.0 %copy-start.17 = (f32[1024]{0:T(1024)S(1)}, f32[1024]{0:T(1024)}, u32[]{:S(2)}) copy-start(f32[1024]{0:T(1024)} %param.31) | copy-start | bytes 12292
  15.5 15.1 %all-to-all-start = ((bf16[8,16,1664]{2,1,0:T(8,128)(2,1)}), bf16[8,16,1664]{2,1,0:T(8,128)(2,1)S(1)}, u32[]{:S(2)}, u32[]{:S(2)}) async-start(bf16[8,16,1664]{2,1,0:T(8,128)(2,1)} %pad_maximum_fusion.6), calls=%async_computation | async-start | bytes 851968 | tf_op jit(solution)/shard_map/all_to_all | solution.py:45
  22.1 8.6 %copy-start.15 = (f32[1024]{0:T(1024)S(1)}, f32[1024]{0:T(1024)}, u32[]{:S(2)}) copy-start(f32[1024]{0:T(1024)} %param.25) | copy-start | bytes 12292
  22.1 90.6 %all-gather.6.cloned.1.call-start = ((), (), s32[]{:S(2)}) async-start(), calls=%async_computation.22 | async-start | bytes 3276800 | tf_op jit(solution)/shard_map/all_gather | solution.py:248
  24.1 6.7 %copy-start.28 = (f32[64]{0:T(128)S(1)}, f32[64]{0:T(128)}, u32[]{:S(2)}) copy-start(f32[64]{0:T(128)} %constant.113.clone) | copy-start | bytes 772
  33.7 12.8 %all-to-all-start.1 = ((bf16[4,72,1024]{2,1,0:T(8,128)(2,1)}), bf16[4,72,1024]{2,1,0:T(8,128)(2,1)S(1)}, u32[]{:S(2)}, u32[]{:S(2)}) async-start(bf16[4,72,1024]{2,1,0:T(8,128)(2,1)} %broadcast_in_dim.230), calls=%async_computation.1 | async-start | bytes 1179648 | tf_op jit(solution)/shard_map/all_to_all | solution.py:45
  37.1 144.2 %all-gather.8.cloned.1.call-start = ((), (), s32[]{:S(2)}) async-start(), calls=%async_computation.23 | async-start | bytes 10485760 | tf_op jit(solution)/shard_map/all_gather | solution.py:285
  37.2 4.1 %copy-start.29 = (bf16[1024,512]{1,0:T(8,128)(2,1)S(1)}, bf16[1024,512]{1,0:T(8,128)(2,1)}, u32[]{:S(2)}) copy-start(bf16[1024,512]{1,0:T(8,128)(2,1)} %param.36) | copy-start | bytes 3145732
  46.5 3.4 collective-permute-start.1
  73.5 24.0 %copy-start.21 = (f32[1024]{0:T(1024)S(1)}, f32[1024]{0:T(1024)}, u32[]{:S(2)}) copy-start(f32[1024]{0:T(1024)} %param.28) | copy-start | bytes 12292
  112.6 3.0 copy-start.13
  133.3 7.5 %copy-start.5 = (f32[128,64]{0,1:T(8,128)S(1)}, f32[128,64]{0,1:T(8,128)}, u32[]{:S(2)}) copy-start(f32[128,64]{0,1:T(8,128)} %concatenate.108) | copy-start | bytes 98308
  134.7 6.2 %copy-start.6 = (f32[128,64]{0,1:T(8,128)S(1)}, f32[128,64]{0,1:T(8,128)}, u32[]{:S(2)}) copy-start(f32[128,64]{0,1:T(8,128)} %concatenate.109) | copy-start | bytes 98308
  134.7 8.0 %all-to-all-start.6 = ((bf16[4,16,256]{2,1,0:T(8,128)(2,1)}), bf16[4,16,256]{2,1,0:T(8,128)(2,1)S(1)}, u32[]{:S(2)}, u32[]{:S(2)}) async-start(bf16[4,16,256]{2,1,0:T(8,128)(2,1)} %broadcast_in_dim.239), calls=%async_computation.6 | async-start | bytes 65536 | tf_op jit(solution)/shard_map/all_to_all | solution.py:45
  139.8 3.5 copy-start.7
  139.8 3.5 copy-start.8
  139.8 3.5 copy-start.14
  143.0 12.4 %copy-start.1 = (bf16[1024,1024]{1,0:T(8,128)(2,1)S(1)}, bf16[1024,1024]{1,0:T(8,128)(2,1)}, u32[]{:S(2)}) copy-start(bf16[1024,1024]{1,0:T(8,128)(2,1)} %all-gather.4.cloned.1.call-done) | copy-start | bytes 6291460
  144.8 23.9 %copy-start.4 = (f32[16,1024]{1,0:T(8,128)S(1)}, f32[16,1024]{1,0:T(8,128)}, u32[]{:S(2)}) copy-start(f32[16,1024]{1,0:T(8,128)} %get-tuple-element.107) | copy-start | bytes 196612
  155.5 25.4 %copy-start.18 = (f32[1024]{0:T(1024)S(1)}, f32[1024]{0:T(1024)}, u32[]{:S(2)}) copy-start(f32[1024]{0:T(1024)} %get-tuple-element.73) | copy-start | bytes 12292
  155.5 25.7 %copy-start.19 = (pred[1,128]{1,0:T(4,128)(4,1)S(1)}, pred[1,128]{1,0:T(4,128)(4,1)}, u32[]{:S(2)}) copy-start(pred[1,128]{1,0:T(4,128)(4,1)} %constant.110.clone) | copy-start | bytes 388
  155.5 25.7 %copy-start.20 = (pred[1,128]{1,0:T(4,128)(4,1)S(1)}, pred[1,128]{1,0:T(4,128)(4,1)}, u32[]{:S(2)}) copy-start(pred[1,128]{1,0:T(4,128)(4,1)} %constant.109.clone) | copy-start | bytes 388
  187.7 5.1 %collective-permute-start.2 = (bf16[4,16,4224]{2,1,0:T(8,128)(2,1)S(1)}, bf16[4,16,4224]{2,1,0:T(8,128)(2,1)S(1)}, u32[]{:S(2)}, u32[]{:S(2)}) collective-permute-start(bf16[4,16,4224]{2,1,0:T(8,128)(2,1)S(1)} %slice_bitcast_fusion), channel_id=1, source_target_pairs={{0,1},{1,0},{2,3},{3,2},{4,5},{5,4},{6,7},{7,6},{8,9},{9,8},{10,11... | collective-permute-start | bytes 1622024 | tf_op jit(solution)/shard_map/ppermute | solution.py:78
  192.9 12.8 %copy-start.22 = (pred[1,128]{1,0:T(4,128)(4,1)S(1)}, pred[1,128]{1,0:T(4,128)(4,1)}, u32[]{:S(2)}) copy-start(pred[1,128]{1,0:T(4,128)(4,1)} %constant.112.clone) | copy-start | bytes 388
  192.9 12.8 %copy-start.24 = (pred[1,128]{1,0:T(4,128)(4,1)S(1)}, pred[1,128]{1,0:T(4,128)(4,1)}, u32[]{:S(2)}) copy-start(pred[1,128]{1,0:T(4,128)(4,1)} %constant.111.clone) | copy-start | bytes 388
  216.7 3.7 %collective-permute-start.3 = (bf16[4,16,4224]{2,1,0:T(8,128)(2,1)S(1)}, bf16[4,16,4224]{2,1,0:T(8,128)(2,1)S(1)}, u32[]{:S(2)}, u32[]{:S(2)}) collective-permute-start(bf16[4,16,4224]{2,1,0:T(8,128)(2,1)S(1)} %all_to_all.113), channel_id=1, source_target_pairs={{0,1},{1,0},{2,3},{3,2},{4,5},{5,4},{6,7},{7,6},{8,9},{9,8},{10,11... | collective-permute-start | bytes 1622024 | tf_op jit(solution)/shard_map/ppermute | solution.py:78
  220.7 21.9 %copy-start.12 = (f32[16,1024]{1,0:T(8,128)S(1)}, f32[16,1024]{1,0:T(8,128)}, u32[]{:S(2)}) copy-start(f32[16,1024]{1,0:T(8,128)} %get-tuple-element.46) | copy-start | bytes 196612
  225.5 29.9 %copy-start.2 = (bf16[1024,1024]{1,0:T(8,128)(2,1)S(1)}, bf16[1024,1024]{1,0:T(8,128)(2,1)}, u32[]{:S(2)}) copy-start(bf16[1024,1024]{1,0:T(8,128)(2,1)} %all-gather.4.cloned.1.call-done) | copy-start | bytes 6291460
  242.7 25.8 %copy-start.11 = (f32[64,128]{0,1:T(8,128)S(1)}, f32[64,128]{0,1:T(8,128)}, u32[]{:S(2)}) copy-start(f32[64,128]{0,1:T(8,128)} %pad_maximum_fusion.16) | copy-start | bytes 98308
  255.3 14.2 %copy-start.10 = (f32[128,128]{0,1:T(8,128)S(1)}, f32[128,128]{0,1:T(8,128)}, u32[]{:S(2)}) copy-start(f32[128,128]{0,1:T(8,128)} %pad_maximum_fusion.14) | copy-start | bytes 196612
  256.2 23.2 %copy-start.23 = (pred[1,128]{1,0:T(4,128)(4,1)S(1)}, pred[1,128]{1,0:T(4,128)(4,1)}, u32[]{:S(2)}) copy-start(pred[1,128]{1,0:T(4,128)(4,1)} %constant.112.clone) | copy-start | bytes 388
  256.2 23.1 %copy-start.25 = (pred[1,128]{1,0:T(4,128)(4,1)S(1)}, pred[1,128]{1,0:T(4,128)(4,1)}, u32[]{:S(2)}) copy-start(pred[1,128]{1,0:T(4,128)(4,1)} %constant.111.clone) | copy-start | bytes 388
  256.2 23.1 %copy-start.26 = (bf16[16]{0:T(256)(128)(2,1)S(1)}, bf16[16]{0:T(256)(128)(2,1)}, u32[]{:S(2)}) copy-start(bf16[16]{0:T(256)(128)(2,1)} %get-tuple-element.88) | copy-start | bytes 100
  256.2 23.1 %copy-start.27 = (bf16[16]{0:T(256)(128)(2,1)S(1)}, bf16[16]{0:T(256)(128)(2,1)}, u32[]{:S(2)}) copy-start(bf16[16]{0:T(256)(128)(2,1)} %get-tuple-element.89) | copy-start | bytes 100
  271.2 7.7 %all-to-all-start.15 = ((bf16[4,16,256]{2,1,0:T(8,128)(2,1)}), bf16[4,16,256]{2,1,0:T(8,128)(2,1)S(1)}, u32[]{:S(2)}, u32[]{:S(2)}) async-start(bf16[4,16,256]{2,1,0:T(8,128)(2,1)} %reshape.274), calls=%async_computation.15 | async-start | bytes 65536 | tf_op jit(solution)/shard_map/all_to_all | solution.py:45
  335.7 6.4 %collective-permute-start.4 = (bf16[256,1024]{1,0:T(8,128)(2,1)S(1)}, bf16[256,1024]{1,0:T(8,128)(2,1)S(1)}, u32[]{:S(2)}, u32[]{:S(2)}) collective-permute-start(bf16[256,1024]{1,0:T(8,128)(2,1)S(1)} %convolution_convert_fusion.5), channel_id=1, source_target_pairs={{0,1},{1,0},{2,3},{3,2},{4,5},{5,4},{6,7},{7,6},{8,9},{9,8},{10,11... | collective-permute-start | bytes 1572872 | tf_op jit(solution)/shard_map/ppermute | solution.py:78
  341.3 12.7 %copy-start.3 = (f32[64,1024]{1,0:T(8,128)S(1)}, f32[64,1024]{1,0:T(8,128)}, u32[]{:S(2)}) copy-start(f32[64,1024]{1,0:T(8,128)} %pad_maximum_fusion.11) | copy-start | bytes 786436
Sparse Core Ops, SparseCore 0:
  10.1 38.5 all-gather.3
  50.5 42.3 all-gather.5
  94.7 86.1 all-gather.7

commit v5 on v4

--- a/solution.py
+++ b/solution.py
@@ -111,6 +111,11 @@
         block = jnp.where(masks[2 * index], high, block)
         block = jnp.where(masks[2 * index + 1], values - high, block)
     return block.astype(B16)
+
+
+def lane_sums(values):
+    parts = [values[:, start : start + 128] for start in range(0, values.shape[1], 128)]
+    return sum(parts[1:], parts[0])
 
 
 def joined_column(block, first=0):
@@ -252,12 +257,6 @@
         blocks[:, :, width + hidden], ready["own_prompt"], 0, keepdims=False
     ).astype(F32)
     frequency = (rope_base ** (-np.arange(HD // 2) * 2.0 / HD)).astype(np.float32)
-    angles = own_positions[:, None] * frequency
-    tables = [
-        jnp.concatenate([table] * count, axis=0)
-        for count in (NZ, NY)
-        for table in (jnp.cos(angles), jnp.sin(angles))
-    ]
     encoded = first_sums[:, :width]
     back_hidden = first_sums[:, width:]
     features = [
@@ -269,7 +268,15 @@
         features + [back_hidden.reshape(-1, width)], axis=0
     ).astype(B16)
     feature_rows = POINTS * SEQ
-    own_rows = spread(sent_rows, "x", NX)
+    sent_blocks = jnp.broadcast_to(sent_rows[None], (NX,) + sent_rows.shape)
+    sent_blocks, own_positions = lax.optimization_barrier((sent_blocks, own_positions))
+    own_rows = swap(sent_blocks, "x")
+    angles = own_positions[:, None] * frequency
+    tables = [
+        jnp.concatenate([table] * count, axis=0)
+        for count in (NZ, NY)
+        for table in (jnp.cos(angles), jnp.sin(angles))
+    ]
     gate_up_turned = jnp.concatenate([turned(gate_weight), turned(up_weight)], axis=0)
     own_rows, changes, gate_up_turned, tables = lax.optimization_barrier(
         (own_rows, changes, gate_up_turned, tables)
@@ -289,17 +296,17 @@
     hidden_in = decoded + dec_bias + ready["error_rows"]
 
     gained = feat_part_rows((hidden_in * attn_gain).astype(B16))
-    squares = jnp.sum(
-        jnp.square(gained.astype(F32) * ready["attn_unscaled"]), axis=1, keepdims=True
-    )
+    squares = lane_sums(jnp.square(gained.astype(F32) * ready["attn_unscaled"]))
     projections = tok_sums(
         jnp.concatenate(
-            [dot_t(gained, turned_rows).astype(B16), split_column(masks, squares)], axis=1
+            [dot_t(gained, turned_rows).astype(B16), squares.astype(B16)], axis=1
         )
     )
     head_part = query_weight.shape[1]
     qkv_width = turned_rows.shape[0]
-    scale_rows = lax.rsqrt(joined_column(projections[:, qkv_width:]) / D + epsilon)
+    scale_rows = lax.rsqrt(
+        jnp.sum(projections[:, qkv_width:], axis=1, keepdims=True) / D + epsilon
+    )
     own_qkv = (projections[:, :qkv_width] * scale_rows).reshape(SEQ, NY, qkv_width // NY)
     kv_part = own_qkv.shape[2] - head_part
     own_keyval = own_qkv[:, :, head_part:].astype(B16).reshape(SEQ, NY * kv_part)
@@ -317,7 +324,10 @@
         tables,
         ready["visible"],
     )
-    attended, saved = lax.optimization_barrier((attended.astype(B16), saved))
+    scale_block = split_column(masks, jnp.zeros_like(scale_rows), scale_rows)
+    attended, saved, scale_block = lax.optimization_barrier(
+        (attended.astype(B16), saved, scale_block)
+    )
     projected = feat_part_sums(dot(tok_rows(attended), out_rows))
     middle = hidden_in + projected
 
@@ -326,15 +336,15 @@
     gained = jnp.where(first_core, gained, gained[:, ::-1])
 
     def gate_up_product(rows):
-        squares = jnp.sum(
-            jnp.square(rows.astype(F32) * ready["mlp_unscaled"]), axis=1, keepdims=True
-        )
+        squares = lane_sums(jnp.square(rows.astype(F32) * ready["mlp_unscaled"]))
         return jnp.concatenate(
-            [dot_t(rows, gate_up_turned).astype(B16), split_column(masks, squares)], axis=1
+            [dot_t(rows, gate_up_turned).astype(B16), squares.astype(B16)], axis=1
         ).astype(F32)
 
     gate_up = tok_sums_core_first(gained.reshape(-1, model_width), gate_up_product)
-    scale_mlp = lax.rsqrt(joined_column(gate_up[:, NY * 2 * hidden :]) / D + epsilon)
+    scale_mlp = lax.rsqrt(
+        jnp.sum(gate_up[:, NY * 2 * hidden :], axis=1, keepdims=True) / D + epsilon
+    )
     gate_up = gate_up[:, : NY * 2 * hidden].reshape(SEQ, NY, 2 * hidden)
     gate_raw = gate_up[:, :, :hidden]
     up_raw = gate_up[:, :, hidden:]
@@ -383,7 +393,7 @@
         attn_grads.astype(F32) * projections[:, :qkv_width], axis=1, keepdims=True
     )
     gathered = tok_rows(
-        jnp.concatenate([attn_grads, split_column(masks, meeting, scale_rows)], axis=1)
+        jnp.concatenate([attn_grads, split_column(masks, meeting) + scale_block], axis=1)
     )
     back_first = feat_part_sums(
         jnp.concatenate(

time: 363 us -> 363 us (level)
  no operation moved by 1% of the time
where the time goes in v5:
time: 363 us; the launch traced here: 361 us
  blocking collectives  238 us (66%)
  matrix products  31.5 us (9%)
  starting transfers between devices  31.1 us (9%)
  other arithmetic  17.7 us (5%)
  waiting for transfers between devices  17 us (5%)
  between operations  14.4 us (4%)
  local copies, waits for them, and re-layouts  11.4 us (3%)
    all_to_all x17, blocking collectives, swap(): return lax.all_to_all(blocks, axes, 0, 0, tiled=True)  238 us
    dot_general x10, matrix products, dot_t(): lax.dot_general(left_side, right_side, (((1,), (1,)), ((), ())), preferre...  19.3 us
    all_to_all x4, starting transfers between devices, swap(): return lax.all_to_all(blocks, axes, 0, 0, tiled=True)  17.2 us
    ppermute x4, starting transfers between devices, other_core(): return lax.ppermute(values, 'c', [(0, 1), (1, 0)])  12.3 us
    all_to_all x4, waiting for transfers between devices, swap(): return lax.all_to_all(blocks, axes, 0, 0, tiled=True)  11.4 us
    dot_general x5, matrix products, dot(): return jnp.dot(left_side, right_side, preferred_element_type=F32)  10.8 us
  transfers between devices with their start and end apart: 12, of which 8 were waited for; matrix products, arithmetic and copies ran while one was open for 10% of the time, Pallas kernels for 0%

profile of v5, /device:TPU:1, one launch (start us, length us, event | category | flops | bytes accessed | tf_op | source)
XLA Modules:
  0.0 361.1 jit_solution(4779591507347800386)
XLA Ops:
  6.5 1.9 convolution_convert_fusion.12
  8.4 1.6 collective-permute-start
  10.7 1.8 convolution_convert_fusion.13
  12.5 2.0 convolution_convert_fusion.10
  14.6 0.8 pad_maximum_fusion.6
  15.5 6.6 %all-to-all-start = ((bf16[8,16,1664]{2,1,0:T(8,128)(2,1)}), bf16[8,16,1664]{2,1,0:T(8,128)(2,1)S(1)}, u32[]{:S(2)}, u32[]{:S(2)}) async-start(bf16[8,16,1664]{2,1,0:T(8,128)(2,1)} %pad_maximum_fusion.6), calls=%async_computation | async-start | bytes 851968 | tf_op jit(solution)/shard_map/all_to_all | solution.py:45
  22.1 1.4 convolution_convert_fusion.6
  24.1 1.0 convert_element_type.216
  25.1 1.4 dynamic-slice_convert_fusion
  26.5 0.9 pad_maximum_fusion.5
  27.4 3.1 all-to-all-done
  31.1 0.9 broadcast_in_dim.194
  32.2 0.7 concatenate.108
  32.9 0.7 concatenate.109
  33.7 3.5 all-to-all-start.1
  37.2 0.7 pad_maximum_fusion.19
  37.9 0.7 pad_maximum_fusion.20
  38.7 0.7 pad_maximum_fusion.11
  39.4 2.0 convolution_convert_fusion.3
  41.4 0.7 convolution_convert_fusion.4
  42.1 1.5 pad_maximum_fusion
  43.6 2.9 all-to-all-done.1
  46.5 1.8 collective-permute-start.1
  48.3 1.6 collective-permute-done.1
  50.2 1.3 convolution_convert_fusion.2
  51.6 21.9 %all_to_all.105 = bf16[4,144,1024]{2,1,0:T(8,128)(2,1)S(1)} all-to-all(bf16[4,144,1024]{2,1,0:T(8,128)(2,1)S(1)} %pad_maximum_fusion.2), channel_id=1, replica_groups=mesh['y'=4,'half'=2,'quad'=4,'x'=4,'c'=2] {'y'}, dimensions={0} | all-to-all | bytes 2359296 | tf_op jit(solution)/shard_map/all_to_all | solution.py:45
  73.7 23.8 %all_to_all.106 = bf16[8,16,1024]{2,1,0:T(8,128)(2,1)S(1)} all-to-all(bf16[8,16,1024]{2,1,0:T(8,128)(2,1)S(1)} %bitcast.158), channel_id=1, replica_groups=mesh['y'=4,'half'=2,'quad'=4,'x'=4,'c'=2] {'half','quad'}, dimensions={0} | all-to-all | bytes 524288 | tf_op jit(solution)/shard_map/all_to_all | solution.py:45
  98.2 11.7 %all_to_all.107 = bf16[8,16,1024]{2,1,0:T(8,128)(2,1)S(1)} all-to-all(bf16[8,16,1024]{2,1,0:T(8,128)(2,1)S(1)} %broadcast_in_dim.195), channel_id=1, replica_groups=mesh['y'=4,'half'=2,'quad'=4,'x'=4,'c'=2] {'half','quad'}, dimensions={0} | all-to-all | bytes 524288 | tf_op jit(solution)/shard_map/all_to_all | solution.py:45
  110.7 3.0 convolution_convert_fusion.1
  113.7 16.6 %all_to_all.108 = bf16[8,16,1408]{2,1,0:T(8,128)(2,1)S(1)} all-to-all(bf16[8,16,1408]{2,1,0:T(8,128)(2,1)S(1)} %bitcast.149), channel_id=1, replica_groups=mesh['y'=4,'half'=2,'quad'=4,'x'=4,'c'=2] {'x','c'}, dimensions={0} | all-to-all | bytes 720896 | tf_op jit(solution)/shard_map/all_to_all | solution.py:45
  133.3 3.9 %all-to-all-start.6 = ((bf16[4,16,256]{2,1,0:T(8,128)(2,1)}), bf16[4,16,256]{2,1,0:T(8,128)(2,1)}, u32[]{:S(2)}, u32[]{:S(2)}) async-start(bf16[4,16,256]{2,1,0:T(8,128)(2,1)} %broadcast_in_dim.197), calls=%async_computation.6 | async-start | bytes 65536 | tf_op jit(solution)/shard_map/all_to_all | solution.py:45
  137.2 1.0 copy.229
  138.2 0.7 fusion.40
  138.9 1.0 concatenate.114
  140.8 1.0 all-to-all-done.6
  141.8 0.9 reshape.266
  144.7 10.8 %all_to_all.109 = bf16[8,16,1024]{2,1,0:T(8,128)(2,1)S(1)} all-to-all(bf16[8,16,1024]{2,1,0:T(8,128)(2,1)S(1)} %broadcast_in_dim.206), channel_id=1, replica_groups=mesh['y'=4,'half'=2,'quad'=4,'x'=4,'c'=2] {'x','c'}, dimensions={0} | all-to-all | bytes 524288 | tf_op jit(solution)/shard_map/all_to_all | solution.py:45
  155.9 12.6 %all_to_all.110 = bf16[8,16,1024]{2,1,0:T(8,128)(2,1)S(1)} all-to-all(bf16[8,16,1024]{2,1,0:T(8,128)(2,1)S(1)} %bitcast.157), channel_id=1, replica_groups=mesh['y'=4,'half'=2,'quad'=4,'x'=4,'c'=2] {'half','quad'}, dimensions={0} | all-to-all | bytes 524288 | tf_op jit(solution)/shard_map/all_to_all | solution.py:45
  168.6 12.2 %all_to_all.111 = bf16[8,16,1024]{2,1,0:T(8,128)(2,1)S(1)} all-to-all(bf16[8,16,1024]{2,1,0:T(8,128)(2,1)S(1)} %broadcast_in_dim.207), channel_id=1, replica_groups=mesh['y'=4,'half'=2,'quad'=4,'x'=4,'c'=2] {'half','quad'}, dimensions={0} | all-to-all | bytes 524288 | tf_op jit(solution)/shard_map/all_to_all | solution.py:45
  181.0 6.2 %convolution_convert_fusion = bf16[128,4096]{1,0:T(8,128)(2,1)S(1)} fusion(bf16[128,1024]{1,0:T(8,128)(2,1)S(1)} %bitcast.138, bf16[4096,1024]{1,0:T(8,128)(2,1)} %all-gather.8.cloned.1.call-done), kind=kOutput, calls=%fused_computation | convolution fusion | flops 1074266112 | bytes 9699328 | tf_op jit(solution)/shard_map/dot_general | solution.py:29
  187.4 3.5 collective-permute-start.2
  190.9 1.6 collective-permute-done.2
  192.6 11.9 %all_to_all.112 = bf16[4,16,4224]{2,1,0:T(8,128)(2,1)S(1)} all-to-all(bf16[4,16,4224]{2,1,0:T(8,128)(2,1)S(1)} %fusion.2), channel_id=1, replica_groups=mesh['y'=4,'half'=2,'quad'=4,'x'=4,'c'=2] {'x'}, dimensions={0} | all-to-all | bytes 1081344 | tf_op jit(solution)/shard_map/all_to_all | solution.py:45
  205.5 10.9 %all_to_all.113 = bf16[4,16,4224]{2,1,0:T(8,128)(2,1)S(1)} all-to-all(bf16[4,16,4224]{2,1,0:T(8,128)(2,1)S(1)} %broadcast_in_dim.216), channel_id=1, replica_groups=mesh['y'=4,'half'=2,'quad'=4,'x'=4,'c'=2] {'x'}, dimensions={0} | all-to-all | bytes 1081344 | tf_op jit(solution)/shard_map/all_to_all | solution.py:45
  216.4 2.1 collective-permute-start.3
  218.5 1.6 collective-permute-done.3
  220.3 4.8 %convolution_convert_fusion.8 = bf16[128,1024]{1,0:T(8,128)(2,1)S(1)} fusion(bf16[4096,1024]{1,0:T(8,128)(2,1)} %all-gather.8.cloned.1.call-done, bf16[128,4224]{1,0:T(8,128)(2,1)S(1)} %bitcast.131), kind=kOutput, calls=%fused_computation.11 | convolution fusion | flops 1073872896 | bytes 9699328 | tf_op jit(solution)/shard_map/dot_general | solution.py:25
  225.1 17.1 %all_to_all.114 = bf16[8,16,1152]{2,1,0:T(8,128)(2,1)S(1)} all-to-all(bf16[8,16,1152]{2,1,0:T(8,128)(2,1)S(1)} %bitcast.150), channel_id=1, replica_groups=mesh['y'=4,'half'=2,'quad'=4,'x'=4,'c'=2] {'half','quad'}, dimensions={0} | all-to-all | bytes 589824 | tf_op jit(solution)/shard_map/all_to_all | solution.py:45
  242.7 12.6 %all_to_all.115 = bf16[8,16,1024]{2,1,0:T(8,128)(2,1)S(1)} all-to-all(bf16[8,16,1024]{2,1,0:T(8,128)(2,1)S(1)} %broadcast_in_dim.217), channel_id=1, replica_groups=mesh['y'=4,'half'=2,'quad'=4,'x'=4,'c'=2] {'half','quad'}, dimensions={0} | all-to-all | bytes 524288 | tf_op jit(solution)/shard_map/all_to_all | solution.py:45
  255.3 0.8 convolution_convert_fusion.7
  256.1 11.6 %all_to_all.116 = bf16[8,16,1024]{2,1,0:T(8,128)(2,1)S(1)} all-to-all(bf16[8,16,1024]{2,1,0:T(8,128)(2,1)S(1)} %bitcast.155), channel_id=1, replica_groups=mesh['y'=4,'half'=2,'quad'=4,'x'=4,'c'=2] {'x','c'}, dimensions={0} | all-to-all | bytes 524288 | tf_op jit(solution)/shard_map/all_to_all | solution.py:45
  270.4 0.7 reshape.253
  271.1 3.3 all-to-all-start.15
  274.5 4.4 %all-to-all-done.15 = bf16[4,16,256]{2,1,0:T(8,128)(2,1)S(1)} async-done(((bf16[4,16,256]{2,1,0:T(8,128)(2,1)}), bf16[4,16,256]{2,1,0:T(8,128)(2,1)S(1)}, u32[]{:S(2)}, u32[]{:S(2)}) %all-to-all-start.15) | async-done | bytes 32800 | tf_op jit(solution)/shard_map/all_to_all | solution.py:45
  279.4 12.3 %all_to_all.117 = bf16[8,16,1408]{2,1,0:T(8,128)(2,1)S(1)} all-to-all(bf16[8,16,1408]{2,1,0:T(8,128)(2,1)S(1)} %broadcast_in_dim.220), channel_id=1, replica_groups=mesh['y'=4,'half'=2,'quad'=4,'x'=4,'c'=2] {'x','c'}, dimensions={0} | all-to-all | bytes 720896 | tf_op jit(solution)/shard_map/all_to_all | solution.py:45
  291.7 2.3 convolution_convert_fusion.11
  294.0 13.5 %all_to_all.118 = bf16[8,16,1152]{2,1,0:T(8,128)(2,1)S(1)} all-to-all(bf16[8,16,1152]{2,1,0:T(8,128)(2,1)S(1)} %bitcast.151), channel_id=1, replica_groups=mesh['y'=4,'half'=2,'quad'=4,'x'=4,'c'=2] {'half','quad'}, dimensions={0} | all-to-all | bytes 589824 | tf_op jit(solution)/shard_map/all_to_all | solution.py:45
  307.9 11.9 %all_to_all.119 = bf16[8,16,1024]{2,1,0:T(8,128)(2,1)S(1)} all-to-all(bf16[8,16,1024]{2,1,0:T(8,128)(2,1)S(1)} %broadcast_in_dim.221), channel_id=1, replica_groups=mesh['y'=4,'half'=2,'quad'=4,'x'=4,'c'=2] {'half','quad'}, dimensions={0} | all-to-all | bytes 524288 | tf_op jit(solution)/shard_map/all_to_all | solution.py:45
  320.0 14.7 %all_to_all.120 = bf16[4,128,1024]{2,1,0:T(8,128)(2,1)S(1)} all-to-all(bf16[4,128,1024]{2,1,0:T(8,128)(2,1)S(1)} %broadcast_in_dim.223), channel_id=1, replica_groups=mesh['y'=4,'half'=2,'quad'=4,'x'=4,'c'=2] {'y'}, dimensions={0} | all-to-all | bytes 2097152 | tf_op jit(solution)/shard_map/all_to_all | solution.py:45
  334.8 0.7 convolution_convert_fusion.5
  335.5 4.9 %collective-permute-start.4 = (bf16[256,1024]{1,0:T(8,128)(2,1)S(1)}, bf16[256,1024]{1,0:T(8,128)(2,1)S(1)}, u32[]{:S(2)}, u32[]{:S(2)}) collective-permute-start(bf16[256,1024]{1,0:T(8,128)(2,1)S(1)} %convolution_convert_fusion.5), channel_id=1, source_target_pairs={{0,1},{1,0},{2,3},{3,2},{4,5},{5,4},{6,7},{7,6},{8,9},{9,8},{10,11... | collective-permute-start | bytes 1572872 | tf_op jit(solution)/shard_map/ppermute | solution.py:78
  340.4 0.7 fusion
  341.2 0.8 collective-permute-done.4
  342.1 11.6 %all_to_all.121 = bf16[4,64,1024]{2,1,0:T(8,128)(2,1)S(1)} all-to-all(bf16[4,64,1024]{2,1,0:T(8,128)(2,1)S(1)} %fusion.4), channel_id=1, replica_groups=mesh['y'=4,'half'=2,'quad'=4,'x'=4,'c'=2] {'x'}, dimensions={0} | all-to-all | bytes 1048576 | tf_op jit(solution)/shard_map/all_to_all | solution.py:45
  (240 shorter events, 16.7 us)
Async XLA Ops:
  6.5 43.7 %copy-start = (bf16[1024,1024]{1,0:T(8,128)(2,1)S(1)}, bf16[1024,1024]{1,0:T(8,128)(2,1)}, u32[]{:S(2)}) copy-start(bf16[1024,1024]{1,0:T(8,128)(2,1)} %param.27) | copy-start | bytes 6291460
  6.5 5.9 %copy-start.9 = (bf16[128,1024]{1,0:T(8,128)(2,1)S(1)}, bf16[128,1024]{1,0:T(8,128)(2,1)}, u32[]{:S(2)}) copy-start(bf16[128,1024]{1,0:T(8,128)(2,1)} %param.23) | copy-start | bytes 786436
  6.5 67.0 %all-gather.4.cloned.1.call-start = ((), (), s32[]{:S(2)}) async-start(), calls=%async_computation.21 | async-start | bytes 2621440 | tf_op jit(solution)/shard_map/all_gather | solution.py:234
  8.4 18.1 %collective-permute-start = (bf16[64,1024]{1,0:T(8,128)(2,1)}, bf16[64,1024]{1,0:T(8,128)(2,1)S(1)}, u32[]{:S(2)}, u32[]{:S(2)}) collective-permute-start(bf16[64,1024]{1,0:T(8,128)(2,1)} %convolution_convert_fusion.12), channel_id=1, source_target_pairs={{0,0},{8,8},{16,32},{24,40},{32,16},{40,24},{48,48},{56,56},{64,64... | collective-permute-start | bytes 393224 | tf_op jit(solution)/shard_map/ppermute | solution.py:180
  14.5 9.0 %copy-start.16 = (f32[1024]{0:T(1024)S(1)}, f32[1024]{0:T(1024)}, u32[]{:S(2)}) copy-start(f32[1024]{0:T(1024)} %param.35) | copy-start | bytes 12292
  14.5 9.0 %copy-start.17 = (f32[1024]{0:T(1024)S(1)}, f32[1024]{0:T(1024)}, u32[]{:S(2)}) copy-start(f32[1024]{0:T(1024)} %param.31) | copy-start | bytes 12292
  15.5 15.1 %all-to-all-start = ((bf16[8,16,1664]{2,1,0:T(8,128)(2,1)}), bf16[8,16,1664]{2,1,0:T(8,128)(2,1)S(1)}, u32[]{:S(2)}, u32[]{:S(2)}) async-start(bf16[8,16,1664]{2,1,0:T(8,128)(2,1)} %pad_maximum_fusion.6), calls=%async_computation | async-start | bytes 851968 | tf_op jit(solution)/shard_map/all_to_all | solution.py:45
  22.1 8.9 %copy-start.15 = (f32[1024]{0:T(1024)S(1)}, f32[1024]{0:T(1024)}, u32[]{:S(2)}) copy-start(f32[1024]{0:T(1024)} %param.25) | copy-start | bytes 12292
  22.1 88.6 %all-gather.6.cloned.1.call-start = ((), (), s32[]{:S(2)}) async-start(), calls=%async_computation.22 | async-start | bytes 3276800 | tf_op jit(solution)/shard_map/all_gather | solution.py:253
  26.5 5.5 %copy-start.26 = (f32[64]{0:T(128)S(1)}, f32[64]{0:T(128)}, u32[]{:S(2)}) copy-start(f32[64]{0:T(128)} %constant.115.clone) | copy-start | bytes 772
  33.7 12.8 %all-to-all-start.1 = ((bf16[4,72,1024]{2,1,0:T(8,128)(2,1)}), bf16[4,72,1024]{2,1,0:T(8,128)(2,1)S(1)}, u32[]{:S(2)}, u32[]{:S(2)}) async-start(bf16[4,72,1024]{2,1,0:T(8,128)(2,1)} %broadcast_in_dim.194), calls=%async_computation.1 | async-start | bytes 1179648 | tf_op jit(solution)/shard_map/all_to_all | solution.py:45
  37.2 143.9 %all-gather.8.cloned.1.call-start = ((), (), s32[]{:S(2)}) async-start(), calls=%async_computation.23 | async-start | bytes 10485760 | tf_op jit(solution)/shard_map/all_gather | solution.py:292
  37.2 4.2 %copy-start.29 = (bf16[1024,512]{1,0:T(8,128)(2,1)S(1)}, bf16[1024,512]{1,0:T(8,128)(2,1)}, u32[]{:S(2)}) copy-start(bf16[1024,512]{1,0:T(8,128)(2,1)} %param.36) | copy-start | bytes 3145732
  46.5 3.4 collective-permute-start.1
  73.5 24.0 %copy-start.19 = (f32[1024]{0:T(1024)S(1)}, f32[1024]{0:T(1024)}, u32[]{:S(2)}) copy-start(f32[1024]{0:T(1024)} %param.28) | copy-start | bytes 12292
  110.6 3.0 copy-start.13
  131.8 8.2 %copy-start.22 = (pred[1,128]{1,0:T(4,128)(4,1)S(1)}, pred[1,128]{1,0:T(4,128)(4,1)}, u32[]{:S(2)}) copy-start(pred[1,128]{1,0:T(4,128)(4,1)} %constant.114.clone) | copy-start | bytes 388
  131.8 8.3 %copy-start.5 = (f32[128,64]{0,1:T(8,128)S(1)}, f32[128,64]{0,1:T(8,128)}, u32[]{:S(2)}) copy-start(f32[128,64]{0,1:T(8,128)} %concatenate.108) | copy-start | bytes 98308
  133.2 6.8 %copy-start.24 = (pred[1,128]{1,0:T(4,128)(4,1)S(1)}, pred[1,128]{1,0:T(4,128)(4,1)}, u32[]{:S(2)}) copy-start(pred[1,128]{1,0:T(4,128)(4,1)} %constant.113.clone) | copy-start | bytes 388
  133.2 6.8 %copy-start.27 = (bf16[16]{0:T(256)(128)(2,1)S(1)}, bf16[16]{0:T(256)(128)(2,1)}, u32[]{:S(2)}) copy-start(bf16[16]{0:T(256)(128)(2,1)} %get-tuple-element.106) | copy-start | bytes 100
  133.2 6.8 %copy-start.28 = (bf16[16]{0:T(256)(128)(2,1)S(1)}, bf16[16]{0:T(256)(128)(2,1)}, u32[]{:S(2)}) copy-start(bf16[16]{0:T(256)(128)(2,1)} %reduce_precision.46) | copy-start | bytes 100
  133.2 6.9 %copy-start.6 = (f32[128,64]{0,1:T(8,128)S(1)}, f32[128,64]{0,1:T(8,128)}, u32[]{:S(2)}) copy-start(f32[128,64]{0,1:T(8,128)} %concatenate.109) | copy-start | bytes 98308
  133.3 8.5 %all-to-all-start.6 = ((bf16[4,16,256]{2,1,0:T(8,128)(2,1)}), bf16[4,16,256]{2,1,0:T(8,128)(2,1)}, u32[]{:S(2)}, u32[]{:S(2)}) async-start(bf16[4,16,256]{2,1,0:T(8,128)(2,1)} %broadcast_in_dim.197), calls=%async_computation.6 | async-start | bytes 65536 | tf_op jit(solution)/shard_map/all_to_all | solution.py:45
  138.2 4.9 %copy-start.7 = (f32[64,64]{0,1:T(8,128)S(1)}, f32[64,64]{0,1:T(8,128)}, u32[]{:S(2)}) copy-start(f32[64,64]{0,1:T(8,128)} %pad_maximum_fusion.19) | copy-start | bytes 49156
  138.2 4.9 %copy-start.8 = (f32[64,64]{0,1:T(8,128)S(1)}, f32[64,64]{0,1:T(8,128)}, u32[]{:S(2)}) copy-start(f32[64,64]{0,1:T(8,128)} %pad_maximum_fusion.20) | copy-start | bytes 49156
  138.2 4.9 %copy-start.14 = (pred[128,64]{0,1:T(32,128)(4,1)S(1)}, pred[128,64]{0,1:T(32,128)(4,1)}, u32[]{:S(2)}) copy-start(pred[128,64]{0,1:T(32,128)(4,1)} %constant.110.clone) | copy-start | bytes 24580
  142.9 12.6 %copy-start.1 = (bf16[1024,1024]{1,0:T(8,128)(2,1)S(1)}, bf16[1024,1024]{1,0:T(8,128)(2,1)}, u32[]{:S(2)}) copy-start(bf16[1024,1024]{1,0:T(8,128)(2,1)} %all-gather.4.cloned.1.call-done) | copy-start | bytes 6291460
  144.6 23.9 %copy-start.4 = (f32[16,1024]{1,0:T(8,128)S(1)}, f32[16,1024]{1,0:T(8,128)}, u32[]{:S(2)}) copy-start(f32[16,1024]{1,0:T(8,128)} %get-tuple-element.109) | copy-start | bytes 196612
  155.5 25.4 %copy-start.18 = (f32[1024]{0:T(1024)S(1)}, f32[1024]{0:T(1024)}, u32[]{:S(2)}) copy-start(f32[1024]{0:T(1024)} %get-tuple-element.78) | copy-start | bytes 12292
  187.4 5.0 %collective-permute-start.2 = (bf16[4,16,4224]{2,1,0:T(8,128)(2,1)S(1)}, bf16[4,16,4224]{2,1,0:T(8,128)(2,1)S(1)}, u32[]{:S(2)}, u32[]{:S(2)}) collective-permute-start(bf16[4,16,4224]{2,1,0:T(8,128)(2,1)S(1)} %slice_bitcast_fusion), channel_id=1, source_target_pairs={{0,1},{1,0},{2,3},{3,2},{4,5},{5,4},{6,7},{7,6},{8,9},{9,8},{10,11... | collective-permute-start | bytes 1622024 | tf_op jit(solution)/shard_map/ppermute | solution.py:78
  192.6 12.7 %copy-start.20 = (pred[1,128]{1,0:T(4,128)(4,1)S(1)}, pred[1,128]{1,0:T(4,128)(4,1)}, u32[]{:S(2)}) copy-start(pred[1,128]{1,0:T(4,128)(4,1)} %constant.112.clone) | copy-start | bytes 388
  192.6 12.7 %copy-start.21 = (pred[1,128]{1,0:T(4,128)(4,1)S(1)}, pred[1,128]{1,0:T(4,128)(4,1)}, u32[]{:S(2)}) copy-start(pred[1,128]{1,0:T(4,128)(4,1)} %constant.111.clone) | copy-start | bytes 388
  192.6 12.7 %copy-start.23 = (pred[1,128]{1,0:T(4,128)(4,1)S(1)}, pred[1,128]{1,0:T(4,128)(4,1)}, u32[]{:S(2)}) copy-start(pred[1,128]{1,0:T(4,128)(4,1)} %constant.114.clone) | copy-start | bytes 388
  192.6 12.7 %copy-start.25 = (pred[1,128]{1,0:T(4,128)(4,1)S(1)}, pred[1,128]{1,0:T(4,128)(4,1)}, u32[]{:S(2)}) copy-start(pred[1,128]{1,0:T(4,128)(4,1)} %constant.113.clone) | copy-start | bytes 388
  216.4 3.7 %collective-permute-start.3 = (bf16[4,16,4224]{2,1,0:T(8,128)(2,1)S(1)}, bf16[4,16,4224]{2,1,0:T(8,128)(2,1)S(1)}, u32[]{:S(2)}, u32[]{:S(2)}) collective-permute-start(bf16[4,16,4224]{2,1,0:T(8,128)(2,1)S(1)} %all_to_all.113), channel_id=1, source_target_pairs={{0,1},{1,0},{2,3},{3,2},{4,5},{5,4},{6,7},{7,6},{8,9},{9,8},{10,11... | collective-permute-start | bytes 1622024 | tf_op jit(solution)/shard_map/ppermute | solution.py:78
  220.3 22.3 %copy-start.12 = (f32[16,1024]{1,0:T(8,128)S(1)}, f32[16,1024]{1,0:T(8,128)}, u32[]{:S(2)}) copy-start(f32[16,1024]{1,0:T(8,128)} %get-tuple-element.49) | copy-start | bytes 196612
  225.1 30.2 %copy-start.2 = (bf16[1024,1024]{1,0:T(8,128)(2,1)S(1)}, bf16[1024,1024]{1,0:T(8,128)(2,1)}, u32[]{:S(2)}) copy-start(bf16[1024,1024]{1,0:T(8,128)(2,1)} %all-gather.4.cloned.1.call-done) | copy-start | bytes 6291460
  242.7 25.7 %copy-start.11 = (f32[64,128]{0,1:T(8,128)S(1)}, f32[64,128]{0,1:T(8,128)}, u32[]{:S(2)}) copy-start(f32[64,128]{0,1:T(8,128)} %pad_maximum_fusion.15) | copy-start | bytes 98308
  255.3 14.2 %copy-start.10 = (f32[128,128]{0,1:T(8,128)S(1)}, f32[128,128]{0,1:T(8,128)}, u32[]{:S(2)}) copy-start(f32[128,128]{0,1:T(8,128)} %pad_maximum_fusion.13) | copy-start | bytes 196612
  271.1 7.7 %all-to-all-start.15 = ((bf16[4,16,256]{2,1,0:T(8,128)(2,1)}), bf16[4,16,256]{2,1,0:T(8,128)(2,1)S(1)}, u32[]{:S(2)}, u32[]{:S(2)}) async-start(bf16[4,16,256]{2,1,0:T(8,128)(2,1)} %reshape.253), calls=%async_computation.15 | async-start | bytes 65536 | tf_op jit(solution)/shard_map/all_to_all | solution.py:45
  335.5 6.4 %collective-permute-start.4 = (bf16[256,1024]{1,0:T(8,128)(2,1)S(1)}, bf16[256,1024]{1,0:T(8,128)(2,1)S(1)}, u32[]{:S(2)}, u32[]{:S(2)}) collective-permute-start(bf16[256,1024]{1,0:T(8,128)(2,1)S(1)} %convolution_convert_fusion.5), channel_id=1, source_target_pairs={{0,1},{1,0},{2,3},{3,2},{4,5},{5,4},{6,7},{7,6},{8,9},{9,8},{10,11... | collective-permute-start | bytes 1572872 | tf_op jit(solution)/shard_map/ppermute | solution.py:78
  341.2 12.7 %copy-start.3 = (f32[64,1024]{1,0:T(8,128)S(1)}, f32[64,1024]{1,0:T(8,128)}, u32[]{:S(2)}) copy-start(f32[64,1024]{1,0:T(8,128)} %pad_maximum_fusion.11) | copy-start | bytes 786436
Sparse Core Ops, SparseCore 0:
  10.1 38.5 all-gather.3
  50.5 42.3 all-gather.5
  94.7 86.1 all-gather.7
